TPU v7x, 32 devices: a whole 2x2x4 slice. The times are simulated.
32 devices in a mesh: band: 8 (over z, y), grid: 4 (over x, core).
Axes of the slice: x: 2, y: 2, z: 4, core: 2. Of those that a mesh axis runs over, the one named last changes fastest.
Arguments:
- orbitals: bfloat16 [512, 64, 4096], P('band', 'grid'), may hold values from -6 to 6
- picks: int32 [1], replicated, may hold values from 0 to 511
Outputs:
- exchange_vectors: bfloat16 [512, 64, 4096], P('band', 'grid')
- gram: float32 [512, 512], P('band')
All inputs are finite; a program needn't handle non-finite values.
Results may differ from a plain program's by a relative error of at most 0.00085.
Values may be sent and summed in bfloat16 or wider, within the bound.
A program may use at most 192 MiB of HBM per device.

v0:
```python
import math

import jax
import jax.numpy as jnp
from jax import lax
from jax.experimental import pallas as pl
from jax.experimental.pallas import tpu as pltpu
from jax.sharding import PartitionSpec as P

NG = 64
NPTS = 262144
KERNEL_SCALE = 128.0
BF = jnp.bfloat16
F32 = jnp.float32


def spread(value, axis, source):
    kept = jnp.where(lax.axis_index(axis) == source, value, 0).astype(value.dtype)
    return lax.psum(kept, axis)


def cas_matrix(length):
    products = (
        jnp.arange(length, dtype=jnp.int32)[:, None]
        * jnp.arange(length, dtype=jnp.int32)[None, :]
        % length
    )
    angles = products.astype(F32) * (2.0 * math.pi / length)
    return jnp.cos(angles) + jnp.sin(angles)


def halves(value):
    high = value.astype(BF)
    return high, (value - high.astype(F32)).astype(BF)


def matrix_halves(value):
    high = lax.reduce_precision(value, 8, 7)
    return high.astype(BF), (value - high).astype(BF)


def kernel_table():
    frequency = jnp.arange(NG, dtype=jnp.int32)
    folded = jnp.minimum(frequency, NG - frequency).astype(F32)
    square = folded * folded
    summed = square[:, None, None] + square[None, :, None] + square[None, None, :]
    table = jnp.where(summed > 0, KERNEL_SCALE / NPTS / jnp.maximum(summed, 1.0), 0.0)
    return jnp.concatenate([table, table], axis=2)


def dot(a, b):
    return jnp.dot(a, b, preferred_element_type=F32)


def solve_body(slabs, rows, orb, partner, table, left_hi, left_lo, right_hi, right_lo, out, work):
    def along_rows(value):
        high, low = halves(value)
        both = dot(left_hi[...], jnp.concatenate([high, low], axis=1))
        return both[:, :128] + both[:, 128:] + dot(left_lo[...], high)

    def along_lanes(value):
        high, low = halves(value)
        return dot(jnp.concatenate([high, low], axis=1), right_hi[...]) + dot(high, right_lo[...])

    for slab in range(slabs):
        @pl.loop(0, rows // 4, unroll=2)
        def _(i):
            at = pl.ds(i * 4, 4)
            x = slab * rows + i * 4
            field = orb[slab, 0, at].astype(F32) * partner[pl.ds(x, 4)].astype(F32)
            field = along_rows(along_lanes(field.reshape(256, 128)))
            work[pl.ds(x, 4)] = field.reshape(4, NG, 128)

    @pl.loop(0, NG // 8)
    def _(i):
        at = pl.ds(pl.multiple_of(i * 8, 8), 8)
        planes = jnp.swapaxes(work[:, at, :], 0, 1)
        done = []
        for part in range(2):
            field = planes[part * 4:part * 4 + 4].reshape(256, 128)
            field = along_rows(field) * table[pl.ds(i * 8 + part * 4, 4)].reshape(256, 128)
            done.append(along_rows(field).reshape(4, NG, 128))
        work[:, at, :] = jnp.swapaxes(jnp.concatenate(done, axis=0), 0, 1)

    for slab in range(slabs):
        @pl.loop(0, rows // 4, unroll=2)
        def _(i):
            x = slab * rows + i * 4
            field = along_lanes(along_rows(work[pl.ds(x, 4)].reshape(256, 128)))
            field = field.reshape(4, NG, 128) * partner[pl.ds(x, 4)].astype(F32)
            out[slab, 0, pl.ds(i * 4, 4)] = (-field).astype(BF)


def solve(pairs, partner):
    slabs, count, rows = pairs.shape[:3]
    matrix = cas_matrix(NG)
    left = matrix_halves(jnp.kron(jnp.eye(4, dtype=F32), matrix))
    right = matrix_halves(jnp.kron(jnp.eye(2, dtype=F32), matrix))
    right_hi = jnp.concatenate([right[0], right[0]], axis=0)
    block = pl.BlockSpec((slabs, 1, rows, NG, 128), lambda i: (0, i, 0, 0, 0))
    whole = lambda array: pl.BlockSpec(array.shape, lambda i: (0,) * array.ndim)
    fixed = (partner, kernel_table(), left[0], left[1], right_hi, right[1])
    return pl.pallas_call(
        lambda *refs: solve_body(slabs, rows, *refs),
        grid=(count,),
        in_specs=[block] + [whole(a) for a in fixed],
        out_specs=block,
        out_shape=jax.ShapeDtypeStruct(pairs.shape, BF),
        scratch_shapes=[pltpu.VMEM((NG, NG, 128), F32)],
        compiler_params=pltpu.CompilerParams(vmem_limit_bytes=48 * 1024 * 1024),
        cost_estimate=pl.CostEstimate(
            flops=count * 60 * NG * NG * 128 * 256, bytes_accessed=4 * pairs.size, transcendentals=0
        ),
    )(pairs, *fixed)


def gram_body(left, right, out):
    @pl.when(pl.program_id(0) == 0)
    def _():
        out[...] = jnp.zeros_like(out)

    size = out.shape[0]
    a = left[:, 0].reshape(size, left.shape[3])
    b = right[:, 0].reshape(size, right.shape[3])
    out[...] += lax.dot_general(a, b, (((1,), (1,)), ((), ())), preferred_element_type=F32)


def gram_product(left, right):
    shares, planes, bands, points = left.shape
    size = shares * bands
    if bands % 16 or points % 128:
        return jnp.einsum("gxbk,hxck->gbhc", left, right, preferred_element_type=F32).reshape(size, size)
    block = pl.BlockSpec((shares, 1, bands, points), lambda i: (0, i, 0, 0))
    return pl.pallas_call(
        gram_body,
        grid=(planes,),
        in_specs=[block, block],
        out_specs=pl.BlockSpec((size, size), lambda i: (0, 0)),
        out_shape=jax.ShapeDtypeStruct((size, size), F32),
        compiler_params=pltpu.CompilerParams(vmem_limit_bytes=32 * 1024 * 1024),
        cost_estimate=pl.CostEstimate(
            flops=2 * size * size * planes * points, bytes_accessed=4 * left.size, transcendentals=0
        ),
    )(left, right)


def to_shares(array):
    shares = lax.axis_size("band")
    bands, planes, square = array.shape
    cut = array.reshape(bands, planes, shares, square // shares).transpose(2, 1, 0, 3)
    return lax.all_to_all(cut, "band", split_axis=0, concat_axis=0)


def per_device(orbitals, picks):
    bands, planes, square = orbitals.shape
    groups = lax.axis_size("grid")
    pairs = bands // groups // 2
    target = picks[0]
    mine = lax.dynamic_index_in_dim(orbitals, target % bands, 0, keepdims=False)
    slab = spread(mine, "band", target // bands).reshape(planes, NG, NG)
    partner = lax.all_gather(jnp.concatenate([slab, slab], axis=2), "grid", axis=0, tiled=True)

    paired = orbitals.reshape(groups, pairs, 2, planes, NG, NG).transpose(0, 1, 3, 4, 2, 5)
    paired = paired.reshape(groups, pairs, planes, NG, 128)
    cubes = lax.all_to_all(paired, "grid", split_axis=0, concat_axis=0)
    spread_orbitals = to_shares(orbitals)
    solved = solve(cubes, partner)
    back = lax.all_to_all(solved, "grid", split_axis=0, concat_axis=0)
    vectors = back.reshape(groups, pairs, planes, NG, 2, NG).transpose(0, 1, 4, 2, 3, 5)
    vectors = vectors.reshape(bands, planes, square)
    spread_vectors = to_shares(vectors)
    product = gram_product(spread_orbitals, spread_vectors)
    partial_rows = lax.psum_scatter(product * (1.0 / NPTS), "band", scatter_dimension=0, tiled=True)
    gram = lax.psum(partial_rows, "grid")
    return (vectors, gram)


def solution(mesh):
    return jax.shard_map(
        per_device,
        mesh=mesh,
        in_specs=(P("band", "grid", None), P()),
        out_specs=(P("band", "grid", None), P("band", None)),
        check_vma=False,
    )
```

profile of v0, /device:TPU:0, one launch (start us, length us, event | category | flops | bytes accessed | tf_op | source)
XLA Modules:
  0.0 929.2 jit_solution(14104385010902799118)
XLA Ops:
  7.2 23.6 %reshape.135 = bf16[4,8,2,16,64,64]{5,4,3,2,1,0:T(8,128)(2,1)} reshape(bf16[64,16,4096]{2,1,0:T(8,128)(2,1)} %param.2) | data formatting | bytes 16777216 | tf_op jit(solution)/shard_map/reshape | solution.py:163
  30.7 30.8 %copy.20 = bf16[4,8,2,16,64,64]{5,2,4,3,1,0:T(2,128)(2,1)} copy(bf16[4,8,2,16,64,64]{5,4,3,2,1,0:T(8,128)(2,1)} %reshape.135) | data formatting | bytes 16777216 | tf_op jit(solution)/shard_map/reshape | solution.py:163
  61.6 26.9 %reshape.136 = bf16[4,8,16,64,128]{4,3,2,1,0:T(8,128)(2,1)} reshape(bf16[4,8,16,64,2,64]{5,4,3,2,1,0:T(2,128)(2,1)} %bitcast.29) | data formatting | bytes 16777216 | tf_op jit(solution)/shard_map/reshape | solution.py:164
  88.5 5.6 all-to-all-start
  94.1 0.0 all-reduce.3.cloned.1.call-start
  94.9 0.9 dynamic-slice_select_fusion
  95.8 1.0 reshape.137
  96.8 0.0 all-reduce.3.cloned.1.call-update
  96.8 0.0 all-gather.2.cloned.1.call-start
  96.9 0.1 sine_add_fusion
  97.0 0.1 broadcast_multiply_fusion.1
  97.2 0.3 mul.163
  97.5 74.6 %all-reduce.3.cloned.1.call-done = bf16[16,64,64]{2,1,0:T(8,128)(2,1)} async-done(((bf16[16,64,64]{2,1,0:T(8,128)(2,1)}), bf16[16,64,64]{2,1,0:T(8,128)(2,1)}) %all-reduce.3.cloned.1.call-update) | async-done | bytes 131088 | tf_op jit(solution)/shard_map/psum | solution.py:19
  172.1 1.9 pad_maximum_fusion.1
  174.0 0.0 all-gather.2.cloned.1.call-update
  174.0 0.1 broadcast_multiply_fusion.2
  174.1 0.1 mul.167
  174.3 0.1 broadcast_add_fusion
  174.4 0.6 fusion.1
  175.0 0.6 pad_maximum_fusion.refs_2_
  175.7 19.2 %all-gather.2.cloned.1.call-done.refs_1_ = bf16[64,64,128]{2,1,0:T(8,128)(2,1)} async-done(((bf16[16,64,128]{2,1,0:T(8,128)(2,1)}), bf16[64,64,128]{2,1,0:T(8,128)(2,1)}) %all-gather.2.cloned.1.call-update) | async-done | bytes 1048592 | tf_op jit(solution)/shard_map/all_gather | solution.py:161
  194.9 0.0 all-to-all-done.refs_0_
  194.9 0.0 copy-start
  194.9 1.2 copy-done
  196.1 141.5 %shard_map.41 = bf16[4,8,16,64,128]{4,3,2,1,0:T(8,128)(2,1)} custom-call(bf16[4,8,16,64,128]{4,3,2,1,0:T(8,128)(2,1)} %all-to-all-done.refs_0_, bf16[64,64,128]{2,1,0:T(8,128)(2,1)S(1)} %copy-done, f32[64,64,128]{2,1,0:T(8,128)S(1)} %pad_maximum_fusion.refs_2_, bf16[256,256]{1,0:T(8,128)(2,1)S(1)} %get-tuple-element.3.refs_3_, ...), custom_call_target="tpu_custom_call" | custom-call | flops 64424509440 | bytes 16777216 | tf_op jit(solution)/shard_map/pallas_call | solution.py:103
  337.7 5.8 all-to-all-start.1
  343.5 12.2 %copy.14 = bf16[128,8,8,512]{3,2,1,0:T(8,128)(2,1)} copy(bf16[128,8,8,512]{3,1,2,0:T(8,128)(2,1)} %bitcast.30) | data formatting | bytes 16777216
  355.7 11.3 %copy.22 = bf16[64,16,8,512]{3,0,1,2:T(8,128)(2,1)} copy(bf16[64,16,8,512]{3,2,1,0:T(8,128)(2,1)} %bitcast.33) | data formatting | bytes 16777216 | tf_op jit(solution)/shard_map/reshape | solution.py:150
  367.0 69.4 %all-to-all-done.1 = bf16[4,8,16,64,128]{4,3,2,1,0:T(8,128)(2,1)} async-done(((bf16[4,8,16,64,128]{4,3,2,1,0:T(8,128)(2,1)}), bf16[4,8,16,64,128]{4,3,2,1,0:T(8,128)(2,1)}, u32[]{:S(2)}, u32[]{:S(2)}) %all-to-all-start.1) | async-done | bytes 8388640 | tf_op jit(solution)/shard_map/all_to_all | solution.py:168
  436.5 6.4 all-to-all-start.2
  442.9 0.3 reduce-scatter.2.cloned.1.call-start
  443.1 27.8 %reshape.138 = bf16[4,8,16,64,2,64]{5,4,3,2,1,0:T(2,128)(2,1)} reshape(bf16[4,8,16,64,128]{4,3,2,1,0:T(8,128)(2,1)} %all-to-all-done.1) | data formatting | bytes 16777216 | tf_op jit(solution)/shard_map/reshape | solution.py:169
  471.0 15.1 %copy.19 = bf16[4,8,16,64,2,64]{5,3,2,4,1,0:T(8,128)(2,1)} copy(bf16[4,8,16,64,2,64]{5,4,3,2,1,0:T(2,128)(2,1)} %reshape.138) | data formatting | bytes 16777216 | tf_op jit(solution)/shard_map/reshape | solution.py:169
  486.1 22.4 %reshape_reshape.3 = bf16[64,16,8,512]{3,2,1,0:T(8,128)(2,1)} reshape(bf16[4,8,2,16,64,64]{5,4,3,2,1,0:T(8,128)(2,1)} %bitcast.27) | data formatting | bytes 16777216 | tf_op jit(solution)/shard_map/reshape;reshape | solution.py:150
  508.6 11.3 %copy.21 = bf16[64,16,8,512]{3,0,1,2:T(8,128)(2,1)} copy(bf16[64,16,8,512]{3,2,1,0:T(8,128)(2,1)} %reshape_reshape.3) | data formatting | bytes 16777216 | tf_op jit(solution)/shard_map/reshape;reshape | solution.py:150
  519.9 105.9 %all-to-all-done.2.left = bf16[8,16,64,512]{3,2,1,0:T(8,128)(2,1)} async-done(((bf16[8,16,64,512]{3,2,1,0:T(8,128)(2,1)}), bf16[8,16,64,512]{3,2,1,0:T(8,128)(2,1)}, u32[]{:S(2)}, u32[]{:S(2)}) %all-to-all-start.2) | async-done | bytes 8388640 | tf_op jit(solution)/shard_map/all_to_all | solution.py:151
  625.9 186.9 %all_to_all.20.right = bf16[8,16,64,512]{3,2,1,0:T(8,128)(2,1)S(1)} all-to-all(bf16[8,16,64,512]{3,2,1,0:T(8,128)(2,1)} %bitcast.32), channel_id=1, replica_groups=mesh['band'=8,'grid'=4] {'band'}, dimensions={0} | all-to-all | bytes 16777216 | tf_op jit(solution)/shard_map/all_to_all | solution.py:151
  812.7 13.1 %shard_map.42 = f32[512,512]{1,0:T(8,128)S(1)} custom-call(bf16[8,16,64,512]{3,2,1,0:T(8,128)(2,1)} %all-to-all-done.2.left, bf16[8,16,64,512]{3,2,1,0:T(8,128)(2,1)S(1)} %all_to_all.20.right), custom_call_target="tpu_custom_call" | custom-call | flops 4294967296 | bytes 16777216 | tf_op jit(solution)/shard_map/pallas_call | solution.py:134
  825.8 1.1 broadcast_multiply_fusion
  826.9 0.0 reduce-scatter.2.cloned.1.call-update
  826.9 0.0 all-reduce.5.cloned.1.call-start
  826.9 61.6 %reduce-scatter.2.cloned.1.call-done = f32[64,512]{1,0:T(8,128)} async-done(((f32[512,512]{1,0:T(8,128)}), f32[64,512]{1,0:T(8,128)}) %reduce-scatter.2.cloned.1.call-update) | async-done | bytes 131088 | tf_op jit(solution)/shard_map/reduce_scatter | solution.py:173
  888.5 0.0 all-reduce.5.cloned.1.call-update
  888.5 22.6 %reshape.139 = bf16[64,16,4096]{2,1,0:T(8,128)(2,1)} reshape(bf16[4,8,2,16,64,64]{5,4,3,2,1,0:T(8,128)(2,1)} %bitcast.28) | data formatting | bytes 16777216 | tf_op jit(solution)/shard_map/reshape | solution.py:170
  911.1 10.0 %all-reduce.5.cloned.1.call-done = f32[64,512]{1,0:T(8,128)} async-done(((f32[64,512]{1,0:T(8,128)}), f32[64,512]{1,0:T(8,128)}) %all-reduce.5.cloned.1.call-update) | async-done | bytes 131088 | tf_op jit(solution)/shard_map/psum | solution.py:174
  921.1 1.6 copy.26
  (6 shorter events, 0.1 us)
Async XLA Ops:
  88.5 106.4 %all-to-all-start = ((bf16[4,8,16,64,128]{4,3,2,1,0:T(8,128)(2,1)}), bf16[4,8,16,64,128]{4,3,2,1,0:T(8,128)(2,1)}, u32[]{:S(2)}, u32[]{:S(2)}) async-start(bf16[4,8,16,64,128]{4,3,2,1,0:T(8,128)(2,1)} %reshape.136), calls=%async_computation | async-start | bytes 16777216 | tf_op jit(solution)/shard_map/all_to_all | solution.py:165
  94.1 78.0 %all-reduce.3.cloned.1.call-start = ((), (), s32[]{:S(2)}) async-start(), calls=%async_computation.5 | async-start | bytes 524288 | tf_op jit(solution)/shard_map/psum | solution.py:19
  96.8 98.1 %all-gather.2.cloned.1.call-start = ((), (), s32[]{:S(2)}) async-start(), calls=%async_computation.6 | async-start | bytes 1310720 | tf_op jit(solution)/shard_map/all_gather | solution.py:161
  194.9 1.2 copy-start
  337.7 98.8 %all-to-all-start.1 = ((bf16[4,8,16,64,128]{4,3,2,1,0:T(8,128)(2,1)}), bf16[4,8,16,64,128]{4,3,2,1,0:T(8,128)(2,1)}, u32[]{:S(2)}, u32[]{:S(2)}) async-start(bf16[4,8,16,64,128]{4,3,2,1,0:T(8,128)(2,1)} %shard_map.41), calls=%async_computation.1 | async-start | bytes 16777216 | tf_op jit(solution)/shard_map/all_to_all | solution.py:168
  436.5 189.4 %all-to-all-start.2 = ((bf16[8,16,64,512]{3,2,1,0:T(8,128)(2,1)}), bf16[8,16,64,512]{3,2,1,0:T(8,128)(2,1)}, u32[]{:S(2)}, u32[]{:S(2)}) async-start(bf16[8,16,64,512]{3,2,1,0:T(8,128)(2,1)} %bitcast.31), calls=%async_computation.2 | async-start | bytes 16777216 | tf_op jit(solution)/shard_map/all_to_all | solution.py:151
  442.9 445.6 %reduce-scatter.2.cloned.1.call-start = ((), (), s32[]{:S(2)}) async-start(), calls=%async_computation.7 | async-start | bytes 1179648 | tf_op jit(solution)/shard_map/reduce_scatter | solution.py:173
  826.9 94.2 %all-reduce.5.cloned.1.call-start = ((), (), s32[]{:S(2)}) async-start(), calls=%async_computation.8 | async-start | bytes 262144 | tf_op jit(solution)/shard_map/psum | solution.py:174
Sparse Core Ops, SparseCore 0:
  98.3 73.7 all-reduce.2
  174.2 20.7 all-gather.1
  827.0 61.4 reduce-scatter.1
  890.7 30.4 all-reduce.4
where the time goes:
time: 933 us; the launch traced here: 929 us
  waiting for transfers between devices  341 us (37%)
  local copies, waits for them, and re-layouts  208 us (22%)
  blocking collectives  187 us (20%)
  Pallas kernels  155 us (17%)
  starting transfers between devices  18.2 us (2%)
  between operations  14.5 us (2%)
    all_to_all x1, blocking collectives, to_shares(): return lax.all_to_all(cut, 'band', split_axis=0, concat_axis=0)  187 us
    pallas_call x1, Pallas kernels, solve(): pl.pallas_call(lambda *refs: solve_body(slabs, rows, *refs), grid=(count,...  142 us
    all_to_all x1, waiting for transfers between devices, to_shares(): return lax.all_to_all(cut, 'band', split_axis=0, concat_axis=0)  106 us
    psum x1, waiting for transfers between devices, spread(): return lax.psum(kept, axis)  74.6 us
    all_to_all x1, waiting for transfers between devices, per_device(): back = lax.all_to_all(solved, 'grid', split_axis=0, concat_axis=0)  69.4 us
    reduce_scatter x1, waiting for transfers between devices, per_device(): lax.psum_scatter(product * (1.0 / NPTS), 'band', scatter_dimension=0, til...  61.6 us
    reshape x2, local copies, waits for them, and re-layouts, per_device(): orbitals.reshape(groups, pairs, 2, planes, NG, NG)  54.4 us
    reshape x2, local copies, waits for them, and re-layouts, per_device(): back.reshape(groups, pairs, planes, NG, 2, NG).transpose(0, 1, 4, 2, 3, 5)  43 us
  transfers between devices with their start and end apart: 7, of which 6 were waited for; matrix products, arithmetic and copies ran while one was open for 14% of the time, Pallas kernels for 0%

commit v1 on v0

v1 whole, which is shorter than its diff:
```python
import math
import jax, jax.numpy as jnp
from jax import lax
from jax.experimental import pallas as pl
from jax.experimental.pallas import tpu as pltpu
from jax.sharding import PartitionSpec as P

NG = 64
NPTS = NG ** 3
KERNEL_SCALE = 128.0
LANES = 128
BF = jnp.bfloat16
F32 = jnp.float32
HALF = NG // 2
XW = 512
PLANES = 32
TILE = 16
SWAP = 256


def cas_matrix(length):
    products = (
        jnp.arange(length, dtype=jnp.int32)[:, None]
        * jnp.arange(length, dtype=jnp.int32)[None, :]
        % length
    )
    angles = products.astype(F32) * (2.0 * math.pi / length)
    return jnp.cos(angles) + jnp.sin(angles)


def halves(value):
    high = value.astype(BF)
    return high, (value - high.astype(F32)).astype(BF)


def matrix_halves(value):
    high = lax.reduce_precision(value, 8, 7)
    return high.astype(BF), (value - high).astype(BF)


def kernel_table():
    frequency = jnp.arange(NG, dtype=jnp.int32)
    folded = jnp.minimum(frequency, NG - frequency).astype(F32)
    square = folded * folded
    summed = square[:, None, None] + square[None, :, None] + square[None, None, :]
    table = jnp.where(summed > 0, KERNEL_SCALE / NPTS / jnp.maximum(summed, 1.0), 0.0)
    return table.reshape(NG // 4, 4, NG, NG).transpose(0, 2, 1, 3).reshape(NG // 4, NG, 4 * NG)


def row_factor(matrix):
    high, low = matrix_halves(matrix)
    return jnp.concatenate([high, high, low], axis=1)


def lane_factor(matrix):
    high, low = matrix_halves(jnp.kron(jnp.eye(2, dtype=F32), matrix))
    upper = jnp.concatenate([high, low], axis=1)
    lower = jnp.concatenate([high, jnp.zeros_like(low)], axis=1)
    return jnp.concatenate([upper, lower], axis=0)


def dot(a, b):
    return jnp.dot(a, b, preferred_element_type=F32)


def solve_body(groups, *refs):
    ins, refs = refs[:groups], refs[groups:]
    partner, table, x_there, x_back, y_there, y_back, z_both = refs[:7]
    outs, work = refs[7:7 + groups], refs[7 + groups]
    rows = NG // groups

    def along_rows(factor, value):
        high, low = halves(value)
        return dot(factor[...], jnp.concatenate([high, low, high], axis=0))

    def along_lanes(value):
        high, low = halves(value)
        both = dot(jnp.concatenate([high, low], axis=1), z_both[...])
        return both[:, :LANES] + both[:, LANES:]

    @pl.loop(0, NG * NG // XW, unroll=4)
    def _(i):
        at = pl.ds(pl.multiple_of(i * XW, XW), XW)
        field = jnp.concatenate([ref[0, :, at].astype(F32) for ref in ins], axis=0)
        field = along_rows(x_there, field * partner[:, at].astype(F32))
        for tile in range(XW // LANES):
            work[pl.ds(i * (XW // LANES) + tile, NG, stride=HALF), :] = field[:, tile * LANES:(tile + 1) * LANES]

    @pl.loop(0, NG // PLANES, unroll=2)
    def _(i):
        left = lax.broadcasted_iota(jnp.int32, (HALF, LANES), 1) < NG
        base = i * PLANES * HALF
        parts = []
        for pair in range(PLANES // 2):
            a = work[pl.ds(base + pair * NG, HALF), :]
            b = work[pl.ds(base + pair * NG + HALF, HALF), :]
            parts.append(jnp.where(left, a, pltpu.roll(b, NG, 1)))
            parts.append(jnp.where(left, pltpu.roll(a, NG, 1), b))
        field = along_lanes(jnp.concatenate(parts, axis=0))
        done = []
        for quad in range(PLANES // 4):
            wide = jnp.concatenate(
                [field[quad * 128:quad * 128 + 64], field[quad * 128 + 64:quad * 128 + 128]], axis=1
            )
            wide = along_rows(y_there, wide) * table[i * (PLANES // 4) + quad]
            wide = along_rows(y_back, wide)
            done.append(wide[:, :LANES])
            done.append(wide[:, LANES:])
        field = along_lanes(jnp.concatenate(done, axis=0))
        for pair in range(PLANES // 2):
            u = field[pair * NG:pair * NG + HALF]
            v = field[pair * NG + HALF:pair * NG + NG]
            work[pl.ds(base + pair * NG, HALF), :] = jnp.where(left, u, pltpu.roll(v, NG, 1))
            work[pl.ds(base + pair * NG + HALF, HALF), :] = jnp.where(left, pltpu.roll(u, NG, 1), v)

    @pl.loop(0, NG * NG // XW, unroll=4)
    def _(i):
        at = pl.ds(pl.multiple_of(i * XW, XW), XW)
        field = jnp.concatenate(
            [work[pl.ds(i * (XW // LANES) + tile, NG, stride=HALF), :] for tile in range(XW // LANES)], axis=1
        )
        field = (-along_rows(x_back, field) * partner[:, at].astype(F32)).astype(BF)
        for index, ref in enumerate(outs):
            ref[0, :, at] = field[index * rows:(index + 1) * rows]


def factors(planes_at):
    matrix = cas_matrix(NG)
    by_plane = jnp.take(matrix, planes_at, axis=1)
    by_line = matrix.reshape(NG, HALF, 2).transpose(0, 2, 1).reshape(NG, NG)
    return (
        kernel_table(), row_factor(by_plane), row_factor(by_plane.T),
        row_factor(by_line), row_factor(by_line.T), lane_factor(matrix),
    )


def solve(pieces, partner, fixed):
    groups = len(pieces)
    count, rows, square = pieces[0].shape
    block = pl.BlockSpec((1, rows, square), lambda i: (i, 0, 0))
    whole = lambda array: pl.BlockSpec(array.shape, lambda i: (0,) * array.ndim)
    fixed = (partner,) + fixed
    return pl.pallas_call(
        lambda *refs: solve_body(groups, *refs),
        grid=(count,),
        in_specs=[block] * groups + [whole(a) for a in fixed],
        out_specs=[block] * groups,
        out_shape=[jax.ShapeDtypeStruct(p.shape, BF) for p in pieces],
        scratch_shapes=[pltpu.VMEM((NG * HALF, LANES), F32)],
        compiler_params=pltpu.CompilerParams(vmem_limit_bytes=32 * 1024 * 1024),
        cost_estimate=pl.CostEstimate(
            flops=count * 12 * NG * NG * NG * 256, bytes_accessed=4 * count * NPTS, transcendentals=0
        ),
    )(*pieces, *fixed)


def order_body(pieces, rows, *refs):
    sources, refs = refs[:pieces], refs[pieces:]
    keep_a, keep_b, send_a, send_b, natural, held, sem, out_sem = refs
    me = lax.axis_index("grid")
    share = held.shape[0] // pieces
    copies = []
    for index, source in enumerate(sources):
        place = pl.multiple_of((me ^ index) * share, share)
        copies.append(pltpu.make_async_copy(source, held.at[pl.ds(place, share)], sem.at[index]))
    for copy in copies:
        copy.start()
    for copy in copies:
        copy.wait()
    out = pltpu.make_async_copy(held, natural, out_sem)
    out.start()
    swap_into(held, (keep_a, keep_b), (send_a, send_b))
    out.wait()


def swap_into(held, keep, send):
    width = held.shape[2] // 2
    mine = lax.axis_index("band") % 2

    @pl.loop(0, width // SWAP)
    def _(i):
        for at, outs in ((mine, keep), (1 - mine, send)):
            lanes = pl.ds(pl.multiple_of(at * width + i * SWAP, SWAP), SWAP)
            turned = jnp.swapaxes(held[:, :, lanes], 0, 1)
            half = turned.shape[0] // 2
            put = pl.ds(pl.multiple_of(i * SWAP, SWAP), SWAP)
            outs[0][:, :, put] = turned[:half]
            outs[1][:, :, put] = turned[half:]


def order_vectors(pieces):
    count, rows, square = pieces[0].shape
    bands = count * len(pieces)
    part = jax.ShapeDtypeStruct((rows // 2, bands, square // 2), BF)
    return pl.pallas_call(
        lambda *refs: order_body(len(pieces), rows, *refs),
        in_specs=[pl.BlockSpec(memory_space=pl.ANY)] * len(pieces),
        out_specs=[pl.BlockSpec(memory_space=pltpu.VMEM)] * 4 + [pl.BlockSpec(memory_space=pl.ANY)],
        out_shape=[part] * 4 + [jax.ShapeDtypeStruct((bands, rows, square), BF)],
        scratch_shapes=[
            pltpu.VMEM((bands, rows, square), BF),
            pltpu.SemaphoreType.DMA((len(pieces),)),
            pltpu.SemaphoreType.DMA,
        ],
        compiler_params=pltpu.CompilerParams(vmem_limit_bytes=24 * 1024 * 1024),
        cost_estimate=pl.CostEstimate(flops=0, bytes_accessed=6 * bands * rows * square, transcendentals=0),
    )(*pieces)


def order_orbitals(orbitals):
    bands, rows, square = orbitals.shape
    part = jax.ShapeDtypeStruct((rows // 2, bands, square // 2), BF)
    spec = pl.BlockSpec((rows // 2, TILE, square // 2), lambda i: (0, i, 0))
    return pl.pallas_call(
        lambda held, a, b, c, d: swap_into(held, (a, b), (c, d)),
        grid=(bands // TILE,),
        in_specs=[pl.BlockSpec((TILE, rows, square), lambda i: (i, 0, 0))],
        out_specs=[spec] * 4,
        out_shape=[part] * 4,
        compiler_params=pltpu.CompilerParams(vmem_limit_bytes=24 * 1024 * 1024),
        cost_estimate=pl.CostEstimate(flops=0, bytes_accessed=4 * orbitals.size, transcendentals=0),
    )(orbitals)


def blocks_body(sizes, *refs):
    out = refs[-1]
    values, at = [], 0
    for size in sizes:
        values.append(jnp.concatenate([ref[0] for ref in refs[at:at + size]], axis=0))
        at += size
    o1, o2, x1, x2, x3, x4, e1, e2, y1, y2, y3, y4 = values

    def across(a, b):
        return lax.dot_general(a, b, (((1,), (1,)), ((), ())), preferred_element_type=F32)

    @pl.when(pl.program_id(0) == 0)
    def _():
        out[...] = jnp.zeros_like(out)

    size = out.shape[1]
    first = across(jnp.concatenate([o1, x1, x2, x3], axis=0), e1)
    second = across(jnp.concatenate([o2, x4], axis=0), e2)
    third = across(o2, jnp.concatenate([y1, y2, y3], axis=0))
    out[0] += first[:size] + second[:size]
    out[1] += first[size:2 * size] + second[size:]
    out[2] += first[2 * size:3 * size]
    out[3] += first[3 * size:]
    out[4] += third[:, :size] + across(o1, y4)
    out[5] += third[:, size:2 * size]
    out[6] += third[:, 2 * size:]


def blocks(families):
    sizes = [len(family) for family in families]
    arrays = [array for family in families for array in family]
    planes = arrays[0].shape[0]
    size = sum(array.shape[1] for array in families[0])
    points = arrays[0].shape[2]
    return pl.pallas_call(
        lambda *refs: blocks_body(sizes, *refs),
        grid=(planes,),
        in_specs=[pl.BlockSpec((1,) + a.shape[1:], lambda i: (i, 0, 0)) for a in arrays],
        out_specs=pl.BlockSpec((7, size, size), lambda i: (0, 0, 0)),
        out_shape=jax.ShapeDtypeStruct((7, size, size), F32),
        compiler_params=pltpu.CompilerParams(vmem_limit_bytes=40 * 1024 * 1024),
        cost_estimate=pl.CostEstimate(
            flops=20 * size * size * planes * points,
            bytes_accessed=2 * sum(a.size for a in arrays), transcendentals=0,
        ),
    )(*arrays)


def shift(values, step, layers):
    pairs = [(2 * z + y, 2 * (z + step) + y) for z in layers for y in range(2)]
    return [lax.ppermute(v, "band", pairs) for v in values]


def flip(value, axis, bits):
    return lax.ppermute(value, axis, [(i, i ^ bits) for i in range(lax.axis_size(axis))])


def summed_rows(parts):
    rank = lax.axis_index("band")
    layer, line = rank // 2, rank % 2
    half = parts.shape[1] // 2

    def plain(block):
        own_rows = jnp.where(line == 0, block, jnp.roll(block, half, 0))
        return jnp.where(line == 0, own_rows, jnp.roll(own_rows, half, 1))

    rows = []
    for other in range(lax.axis_size("band") // 2):
        total = jnp.where(layer == other, parts[0], 0.0)
        for step in range(1, 4):
            if other - step >= 0:
                total = jnp.where(layer == other - step, parts[3 + step], total)
            if other + step < 4:
                total = jnp.where(layer == other + step, parts[step].T, total)
        rows.append(plain(total))
    rows = jnp.stack(rows) * (1.0 / NPTS)
    size = rows.shape[1]
    keep = lax.dynamic_slice_in_dim(rows, line * half, half, 1)
    give = lax.dynamic_slice_in_dim(rows, (1 - line) * half, half, 1)
    total = keep + flip(give, "band", 1)
    bit = 1
    while bit < lax.axis_size("grid"):
        total = total + flip(total, "grid", bit)
        bit *= 2
    return total


def reduce_blocks(parts):
    rank = lax.axis_index("band")
    layer = rank // 2
    layers = lax.axis_size("band") // 2
    rows = summed_rows(parts)
    half, size = rows.shape[1:]
    result = rows
    for bits in range(1, layers):
        there = layer ^ bits
        block = lax.dynamic_index_in_dim(rows, there, 0, keepdims=False)
        both = [flip(block, "band", 2 * bits), flip(block, "band", 2 * bits + 1)]
        line = rank % 2
        low = jnp.where(line == 0, both[0], both[1])
        high = jnp.where(line == 0, both[1], both[0])
        whole = jnp.concatenate([low, high], axis=0)
        mine = lax.dynamic_slice_in_dim(whole, line * half, half, 1).T
        result = lax.dynamic_update_index_in_dim(result, block + mine, there, 0)
    return result.transpose(1, 0, 2).reshape(half, layers * size)


def gram_body(left, right, out):
    @pl.when(pl.program_id(0) == 0)
    def _():
        out[...] = jnp.zeros_like(out)

    size = out.shape[0]
    a = left[:, 0].reshape(size, left.shape[3])
    b = right[:, 0].reshape(size, right.shape[3])
    out[...] += lax.dot_general(a, b, (((1,), (1,)), ((), ())), preferred_element_type=F32)


def gram_product(left, right):
    shares, planes, bands, points = left.shape
    size = shares * bands
    if bands % 16 or points % 128:
        return jnp.einsum("gxbk,hxck->gbhc", left, right, preferred_element_type=F32).reshape(size, size)
    block = pl.BlockSpec((shares, 1, bands, points), lambda i: (0, i, 0, 0))
    return pl.pallas_call(
        gram_body,
        grid=(planes,),
        in_specs=[block, block],
        out_specs=pl.BlockSpec((size, size), lambda i: (0, 0)),
        out_shape=jax.ShapeDtypeStruct((size, size), F32),
        compiler_params=pltpu.CompilerParams(vmem_limit_bytes=32 * 1024 * 1024),
        cost_estimate=pl.CostEstimate(
            flops=2 * size * size * planes * points, bytes_accessed=4 * left.size, transcendentals=0
        ),
    )(left, right)


def to_shares(array):
    shares = lax.axis_size("band")
    bands, planes, square = array.shape
    cut = array.reshape(bands, planes, shares, square // shares).transpose(2, 1, 0, 3)
    return lax.all_to_all(cut, "band", split_axis=0, concat_axis=0)


def spread(orbitals, target):
    bands = orbitals.shape[0]
    mine = lax.dynamic_index_in_dim(orbitals, target % bands, 0, keepdims=False)
    slab = jnp.where(lax.axis_index("band") == target // bands, mine, 0).astype(BF)
    bit = 1
    while bit < lax.axis_size("band"):
        slab = slab + flip(slab, "band", bit)
        bit *= 2
    groups = lax.axis_size("grid")
    return jnp.concatenate([slab] + [flip(slab, "grid", d) for d in range(1, groups)], axis=0)


def per_device(orbitals, picks):
    bands, planes, square = orbitals.shape
    groups, shares = lax.axis_size("grid"), lax.axis_size("band")
    me = lax.axis_index("grid")
    tiled = shares == 8 and bands % TILE == 0 and planes % 16 == 0
    chunk = TILE if bands % TILE == 0 else bands
    count = chunk // groups
    order = (me ^ jnp.arange(groups, dtype=jnp.int32))[:, None] * planes
    fixed = factors((order + jnp.arange(planes, dtype=jnp.int32)[None]).reshape(-1))
    partner = spread(orbitals, picks[0])

    if tiled:
        keep1, keep2, send1, send2 = order_orbitals(orbitals)
        o1 = [keep1, flip(send1, "band", 1)]
        o2 = [keep2, flip(send2, "band", 1)]
        x1 = shift(o1, 1, (0, 1))
        x2 = shift(x1, 1, (1, 2))
        x3 = shift(x2, 1, (2,))
        x4 = shift(o2, 1, (0,))

    vectors, e1, e2 = [], [[], []], [[], []]
    y1, y2, y3, y4 = [[], []], [[], []], [[], []], [[], []]
    for start in range(0, bands, chunk):
        pieces = []
        for d in range(groups):
            part = lax.dynamic_slice_in_dim(orbitals, start + (me ^ d) * count, count, 0)
            pieces.append(flip(part, "grid", d) if d else part)
        solved = solve(pieces, partner, fixed)
        back = [flip(p, "grid", d) if d else p for d, p in enumerate(solved)]
        if tiled:
            keep1, keep2, send1, send2, natural = order_vectors(back)
            vectors.append(natural)
            now1 = [keep1, flip(send1, "band", 1)]
            now2 = [keep2, flip(send2, "band", 1)]
            step1 = shift(now2, -1, (3, 2))
            step2 = shift(step1, -1, (2, 1))
            step3 = shift(step2, -1, (1,))
            step4 = shift(now1, -1, (3,))
            for into, values in ((e1, now1), (e2, now2), (y1, step1), (y2, step2), (y3, step3), (y4, step4)):
                into[0].append(values[0])
                into[1].append(values[1])
        else:
            stacked = jnp.take(jnp.stack(back), me ^ jnp.arange(groups), axis=0)
            vectors.append(stacked.reshape(chunk, planes, square))
    vectors = vectors[0] if len(vectors) == 1 else jnp.concatenate(vectors, axis=0)
    if tiled:
        families = [o1, o2, x1, x2, x3, x4] + [f[0] + f[1] for f in (e1, e2, y1, y2, y3, y4)]
        gram = reduce_blocks(blocks(families))
    else:
        product = gram_product(to_shares(orbitals), to_shares(vectors))
        rows = lax.psum_scatter(product * (1.0 / NPTS), "band", scatter_dimension=0, tiled=True)
        gram = lax.psum(rows, "grid")
    return (vectors, gram)


def solution(mesh):
    return jax.shard_map(
        per_device,
        mesh=mesh,
        in_specs=(P("band", "grid", None), P()),
        out_specs=(P("band", "grid", None), P("band", None)),
        check_vma=False,
    )
```

time: 933 us -> 722 us (0.77)
  blocking collectives: 187 us -> 0 us
  local copies, waits for them, and re-layouts: 208 us -> 64.1 us
  starting transfers between devices: 18.2 us -> 132 us
  waiting for transfers between devices: 341 us -> 406 us
  Pallas kernels: 155 us -> 97.4 us
  other arithmetic: 5.65 us -> 17.3 us
  between operations: 14.5 us -> 2.88 us
    ppermute x0 -> x89, waiting for transfers between devices: none -> 406 us  [the longest x49 216 us: flip(): lax.ppermute(value, axis, [(i, i ^ bits) for i in range(lax.axis_size(axi...]
    all_to_all x1 -> x0, blocking collectives: 187 us -> none  [to_shares(): return lax.all_to_all(cut, 'band', split_axis=0, concat_axis=0)]
    all_to_all x3 -> x0, waiting for transfers between devices: 175 us -> none  [the longest x1 106 us: to_shares(): return lax.all_to_all(cut, 'band', split_axis=0, concat_axis=0)]
    reshape x8 -> x1, local copies, waits for them, and re-layouts: 159 us -> 0.66 us  [reduce_blocks(): return result.transpose(1, 0, 2).reshape(half, layers * size)]
    ppermute x0 -> x89, starting transfers between devices: none -> 132 us  [the longest x40 68.5 us: shift(): return [lax.ppermute(v, 'band', pairs) for v in values]]
    psum x2 -> x0, waiting for transfers between devices: 84.6 us -> none  [the longest x1 74.6 us: spread(): return lax.psum(kept, axis)]
    reduce_scatter x1 -> x0, waiting for transfers between devices: 61.6 us -> none  [per_device(): lax.psum_scatter(product * (1.0 / NPTS), 'band', scatter_dimension=0, til...]
    pallas_call x2 -> x10, Pallas kernels: 155 us -> 97.4 us  [the longest x4 72 us: solve(): pl.pallas_call(lambda *refs: solve_body(groups, *refs), grid=(count,), in...]
  transfers between devices with their start and end apart: 7 -> 89, of which waited for: 6 -> 40; matrix products, arithmetic and copies ran while one was open for 14% -> 3% of each run, Pallas kernels for 0% -> 11%
where the time goes in v1:
time: 722 us; the launch traced here: 719 us
  waiting for transfers between devices  406 us (56%)
  starting transfers between devices  132 us (18%)
  Pallas kernels  97.4 us (13%)
  local copies, waits for them, and re-layouts  64.1 us (9%)
  other arithmetic  17.3 us (2%)
    ppermute x49, waiting for transfers between devices, flip(): lax.ppermute(value, axis, [(i, i ^ bits) for i in range(lax.axis_size(axi...  216 us
    ppermute x40, waiting for transfers between devices, shift(): return [lax.ppermute(v, 'band', pairs) for v in values]  190 us
    pallas_call x4, Pallas kernels, solve(): pl.pallas_call(lambda *refs: solve_body(groups, *refs), grid=(count,), in...  72 us
    ppermute x40, starting transfers between devices, shift(): return [lax.ppermute(v, 'band', pairs) for v in values]  68.5 us
    ppermute x49, starting transfers between devices, flip(): lax.ppermute(value, axis, [(i, i ^ bits) for i in range(lax.axis_size(axi...  63 us
    unnamed x180, local copies, waits for them, and re-layouts  49.5 us
    pallas_call x1, Pallas kernels, blocks(): pl.pallas_call(lambda *refs: blocks_body(sizes, *refs), grid=(planes,), i...  18.6 us
  transfers between devices with their start and end apart: 89, of which 40 were waited for; matrix products, arithmetic and copies ran while one was open for 3% of the time, Pallas kernels for 11%

profile of v1, /device:TPU:0, one launch (start us, length us, event | category | flops | bytes accessed | tf_op | source)
XLA Modules:
  0.0 719.3 jit_solution(2571754237684769755)
XLA Ops:
  0.7 6.3 constant_dynamic-slice_fusion.13
  9.1 2.6 collective-permute-start.3
  14.1 2.2 add.399
  16.4 3.2 add.400
  24.6 1.6 collective-permute-start.4
  26.3 4.2 collective-permute-done.4
  30.6 2.7 collective-permute-start.5
  33.9 5.7 collective-permute-done.5
  43.0 2.4 collective-permute-done.8
  46.2 2.2 collective-permute-done.7
  54.2 18.9 %shard_map.45 = (bf16[4,16,4096]{2,1,0:T(8,128)(2,1)S(1)}, bf16[4,16,4096]{2,1,0:T(8,128)(2,1)S(1)}, bf16[4,16,4096]{2,1,0:T(8,128)(2,1)S(1)}, bf16[4,16,4096]{2,1,0:T(8,128)(2,1)S(1)}) custom-call(bf16[4,16,4096]{2,1,0:T(8,128)(2,1)S(1)} %get-tuple-element.89.refs_0_, bf16[4,16,4096]{2,1,0:T(8,128)(2,1)} %collective-permute-done.18.refs_1_, ...), custom_call_target="tpu_custom_call" | custom-call | flops 3221225472 | bytes 4194304 | tf_op jit(solution)/shard_map/pallas_call | solution.py:143
  75.5 11.3 %collective-permute-done.1.refs_2_ = bf16[4,16,4096]{2,1,0:T(8,128)(2,1)S(1)} collective-permute-done((bf16[4,16,4096]{2,1,0:T(8,128)(2,1)}, bf16[4,16,4096]{2,1,0:T(8,128)(2,1)S(1)}, u32[]{:S(2)}, u32[]{:S(2)}) %collective-permute-start.1) | collective-permute-done | bytes 524320 | tf_op jit(solution)/shard_map/ppermute | solution.py:279
  87.2 17.7 %shard_map.43 = (bf16[4,16,4096]{2,1,0:T(8,128)(2,1)S(1)}, bf16[4,16,4096]{2,1,0:T(8,128)(2,1)S(1)}, bf16[4,16,4096]{2,1,0:T(8,128)(2,1)S(1)}, bf16[4,16,4096]{2,1,0:T(8,128)(2,1)S(1)}) custom-call(bf16[4,16,4096]{2,1,0:T(8,128)(2,1)S(1)} %copy-done.59, bf16[4,16,4096]{2,1,0:T(8,128)(2,1)S(1)} %collective-permute-done.12.refs_1_, ...), custom_call_target="tpu_custom_call" | custom-call | flops 3221225472 | bytes 4194304 | tf_op jit(solution)/shard_map/pallas_call | solution.py:143
  105.0 17.9 %shard_map.41 = (bf16[4,16,4096]{2,1,0:T(8,128)(2,1)S(1)}, bf16[4,16,4096]{2,1,0:T(8,128)(2,1)S(1)}, bf16[4,16,4096]{2,1,0:T(8,128)(2,1)S(1)}, bf16[4,16,4096]{2,1,0:T(8,128)(2,1)S(1)}) custom-call(bf16[4,16,4096]{2,1,0:T(8,128)(2,1)S(1)} %get-tuple-element.96.refs_0_, bf16[4,16,4096]{2,1,0:T(8,128)(2,1)S(1)} %collective-permute-done.refs_1_, ...), custom_call_target="tpu_custom_call" | custom-call | flops 3221225472 | bytes 4194304 | tf_op jit(solution)/shard_map/pallas_call | solution.py:143
  122.9 1.7 collective-permute-start.16
  125.1 6.7 collective-permute-done.22.refs_2_
  131.8 1.7 collective-permute-start.17
  133.5 17.7 %shard_map.47 = (bf16[4,16,4096]{2,1,0:T(8,128)(2,1)S(1)}, bf16[4,16,4096]{2,1,0:T(8,128)(2,1)S(1)}, bf16[4,16,4096]{2,1,0:T(8,128)(2,1)S(1)}, bf16[4,16,4096]{2,1,0:T(8,128)(2,1)S(1)}) custom-call(bf16[4,16,4096]{2,1,0:T(8,128)(2,1)S(1)} %get-tuple-element.85.refs_0_, bf16[4,16,4096]{2,1,0:T(8,128)(2,1)S(1)} %copy-done.61, ...), custom_call_target="tpu_custom_call" | custom-call | flops 3221225472 | bytes 4194304 | tf_op jit(solution)/shard_map/pallas_call | solution.py:143
  151.8 2.4 collective-permute-done.10.refs_2_
  154.7 9.9 %collective-permute-done.11.refs_3_ = bf16[4,16,4096]{2,1,0:T(8,128)(2,1)S(1)} collective-permute-done((bf16[4,16,4096]{2,1,0:T(8,128)(2,1)S(1)}, bf16[4,16,4096]{2,1,0:T(8,128)(2,1)S(1)}, u32[]{:S(2)}, u32[]{:S(2)}) %collective-permute-start.11) | collective-permute-done | bytes 524320 | tf_op jit(solution)/shard_map/ppermute | solution.py:279
  167.9 7.9 %collective-permute-done.17.refs_3_ = bf16[4,16,4096]{2,1,0:T(8,128)(2,1)S(1)} collective-permute-done((bf16[4,16,4096]{2,1,0:T(8,128)(2,1)S(1)}, bf16[4,16,4096]{2,1,0:T(8,128)(2,1)S(1)}, u32[]{:S(2)}, u32[]{:S(2)}) %collective-permute-start.17) | collective-permute-done | bytes 524320 | tf_op jit(solution)/shard_map/ppermute | solution.py:279
  178.6 8.4 %collective-permute-done.23.refs_3_ = bf16[4,16,4096]{2,1,0:T(8,128)(2,1)S(1)} collective-permute-done((bf16[4,16,4096]{2,1,0:T(8,128)(2,1)S(1)}, bf16[4,16,4096]{2,1,0:T(8,128)(2,1)S(1)}, u32[]{:S(2)}, u32[]{:S(2)}) %collective-permute-start.23) | collective-permute-done | bytes 524320 | tf_op jit(solution)/shard_map/ppermute | solution.py:279
  191.4 7.8 %collective-permute-done.28.refs_2_ = bf16[4,16,4096]{2,1,0:T(8,128)(2,1)S(1)} collective-permute-done((bf16[4,16,4096]{2,1,0:T(8,128)(2,1)S(1)}, bf16[4,16,4096]{2,1,0:T(8,128)(2,1)S(1)}, u32[]{:S(2)}, u32[]{:S(2)}) %collective-permute-start.28) | collective-permute-done | bytes 524320 | tf_op jit(solution)/shard_map/ppermute | solution.py:279
  199.2 10.3 %collective-permute-done.29.refs_3_ = bf16[4,16,4096]{2,1,0:T(8,128)(2,1)S(1)} collective-permute-done((bf16[4,16,4096]{2,1,0:T(8,128)(2,1)S(1)}, bf16[4,16,4096]{2,1,0:T(8,128)(2,1)S(1)}, u32[]{:S(2)}, u32[]{:S(2)}) %collective-permute-start.29) | collective-permute-done | bytes 524320 | tf_op jit(solution)/shard_map/ppermute | solution.py:279
  212.4 3.0 shard_map.49
  219.5 7.0 collective-permute-done.43.refs_19_
  227.1 55.7 %collective-permute-done.44.refs_24_ = bf16[8,16,2048]{2,1,0:T(8,128)(2,1)S(1)} collective-permute-done((bf16[8,16,2048]{2,1,0:T(8,128)(2,1)S(1)}, bf16[8,16,2048]{2,1,0:T(8,128)(2,1)S(1)}, u32[]{:S(2)}, u32[]{:S(2)}) %collective-permute-start.44) | collective-permute-done | bytes 524320 | tf_op jit(solution)/shard_map/ppermute | solution.py:279
  283.4 10.5 %collective-permute-done.45.refs_25_ = bf16[8,16,2048]{2,1,0:T(8,128)(2,1)S(1)} collective-permute-done((bf16[8,16,2048]{2,1,0:T(8,128)(2,1)S(1)}, bf16[8,16,2048]{2,1,0:T(8,128)(2,1)S(1)}, u32[]{:S(2)}, u32[]{:S(2)}) %collective-permute-start.45) | collective-permute-done | bytes 524320 | tf_op jit(solution)/shard_map/ppermute | solution.py:279
  294.7 10.5 %collective-permute-done.46.refs_26_ = bf16[8,16,2048]{2,1,0:T(8,128)(2,1)S(1)} collective-permute-done((bf16[8,16,2048]{2,1,0:T(8,128)(2,1)S(1)}, bf16[8,16,2048]{2,1,0:T(8,128)(2,1)S(1)}, u32[]{:S(2)}, u32[]{:S(2)}) %collective-permute-start.46) | collective-permute-done | bytes 524320 | tf_op jit(solution)/shard_map/ppermute | solution.py:279
  305.9 10.2 %collective-permute-done.47.refs_27_ = bf16[8,16,2048]{2,1,0:T(8,128)(2,1)S(1)} collective-permute-done((bf16[8,16,2048]{2,1,0:T(8,128)(2,1)S(1)}, bf16[8,16,2048]{2,1,0:T(8,128)(2,1)S(1)}, u32[]{:S(2)}, u32[]{:S(2)}) %collective-permute-start.47) | collective-permute-done | bytes 524320 | tf_op jit(solution)/shard_map/ppermute | solution.py:279
  318.1 5.0 collective-permute-start.32
  323.0 11.2 %collective-permute-start.38 = (bf16[8,64,2048]{2,1,0:T(8,128)(2,1)S(1)}, bf16[8,64,2048]{2,1,0:T(8,128)(2,1)S(1)}, u32[]{:S(2)}, u32[]{:S(2)}) collective-permute-start(bf16[8,64,2048]{2,1,0:T(8,128)(2,1)S(1)} %get-tuple-element.64.refs_2_), channel_id=1, source_target_pairs={{0,8},{4,12},{1,9},{5,13},{2,10},{6,14},{3,11},{7,15}} | collective-permute-start | bytes 6291464 | tf_op jit(solution)/shard_map/ppermute | solution.py:275
  339.5 25.5 %collective-permute-done.31.refs_3_ = bf16[8,64,2048]{2,1,0:T(8,128)(2,1)} collective-permute-done((bf16[8,64,2048]{2,1,0:T(8,128)(2,1)S(1)}, bf16[8,64,2048]{2,1,0:T(8,128)(2,1)}, u32[]{:S(2)}, u32[]{:S(2)}) %collective-permute-start.31) | collective-permute-done | bytes 2097184 | tf_op jit(solution)/shard_map/ppermute | solution.py:279
  366.5 2.4 collective-permute-done.32.refs_4_
  370.5 43.4 %collective-permute-done.38.refs_10_ = bf16[8,64,2048]{2,1,0:T(8,128)(2,1)S(1)} collective-permute-done((bf16[8,64,2048]{2,1,0:T(8,128)(2,1)S(1)}, bf16[8,64,2048]{2,1,0:T(8,128)(2,1)S(1)}, u32[]{:S(2)}, u32[]{:S(2)}) %collective-permute-start.38) | collective-permute-done | bytes 2097184 | tf_op jit(solution)/shard_map/ppermute | solution.py:275
  421.8 2.1 collective-permute-start.34
  423.8 32.4 %collective-permute-done.33.refs_5_ = bf16[8,64,2048]{2,1,0:T(8,128)(2,1)S(1)} collective-permute-done((bf16[8,64,2048]{2,1,0:T(8,128)(2,1)S(1)}, bf16[8,64,2048]{2,1,0:T(8,128)(2,1)S(1)}, u32[]{:S(2)}, u32[]{:S(2)}) %collective-permute-start.33) | collective-permute-done | bytes 2097184 | tf_op jit(solution)/shard_map/ppermute | solution.py:275
  456.2 2.0 collective-permute-start.35
  463.4 9.4 %collective-permute-done.59.refs_39_ = bf16[8,16,2048]{2,1,0:T(8,128)(2,1)S(1)} collective-permute-done((bf16[8,16,2048]{2,1,0:T(8,128)(2,1)S(1)}, bf16[8,16,2048]{2,1,0:T(8,128)(2,1)S(1)}, u32[]{:S(2)}, u32[]{:S(2)}) %collective-permute-start.59) | collective-permute-done | bytes 524320 | tf_op jit(solution)/shard_map/ppermute | solution.py:275
  482.4 12.3 %collective-permute-done.60.refs_40_ = bf16[8,16,2048]{2,1,0:T(8,128)(2,1)S(1)} collective-permute-done((bf16[8,16,2048]{2,1,0:T(8,128)(2,1)S(1)}, bf16[8,16,2048]{2,1,0:T(8,128)(2,1)S(1)}, u32[]{:S(2)}, u32[]{:S(2)}) %collective-permute-start.60) | collective-permute-done | bytes 524320 | tf_op jit(solution)/shard_map/ppermute | solution.py:275
  496.8 9.1 %collective-permute-done.61.refs_41_ = bf16[8,16,2048]{2,1,0:T(8,128)(2,1)S(1)} collective-permute-done((bf16[8,16,2048]{2,1,0:T(8,128)(2,1)S(1)}, bf16[8,16,2048]{2,1,0:T(8,128)(2,1)S(1)}, u32[]{:S(2)}, u32[]{:S(2)}) %collective-permute-start.61) | collective-permute-done | bytes 524320 | tf_op jit(solution)/shard_map/ppermute | solution.py:275
  508.0 9.3 %collective-permute-done.62.refs_42_ = bf16[8,16,2048]{2,1,0:T(8,128)(2,1)} collective-permute-done((bf16[8,16,2048]{2,1,0:T(8,128)(2,1)S(1)}, bf16[8,16,2048]{2,1,0:T(8,128)(2,1)}, u32[]{:S(2)}, u32[]{:S(2)}) %collective-permute-start.62) | collective-permute-done | bytes 524320 | tf_op jit(solution)/shard_map/ppermute | solution.py:275
  519.3 9.2 %collective-permute-done.63.refs_43_ = bf16[8,16,2048]{2,1,0:T(8,128)(2,1)} collective-permute-done((bf16[8,16,2048]{2,1,0:T(8,128)(2,1)S(1)}, bf16[8,16,2048]{2,1,0:T(8,128)(2,1)}, u32[]{:S(2)}, u32[]{:S(2)}) %collective-permute-start.63) | collective-permute-done | bytes 524320 | tf_op jit(solution)/shard_map/ppermute | solution.py:275
  528.5 11.0 %collective-permute-start.39 = (bf16[8,64,2048]{2,1,0:T(8,128)(2,1)}, bf16[8,64,2048]{2,1,0:T(8,128)(2,1)}, u32[]{:S(2)}, u32[]{:S(2)}) collective-permute-start(bf16[8,64,2048]{2,1,0:T(8,128)(2,1)} %collective-permute-done.31.refs_3_), channel_id=1, source_target_pairs={{0,8},{4,12},{1,9},{5,13},{2,10},{6,14},{3,11},{7,15}} | collective-permute-start | bytes 6291464 | tf_op jit(solution)/shard_map/ppermute | solution.py:275
  539.5 2.1 collective-permute-start.36
  541.6 2.0 collective-permute-start.37
  545.7 5.0 collective-permute-done.65.refs_45_
  552.0 9.9 %collective-permute-done.66.refs_46_ = bf16[8,16,2048]{2,1,0:T(8,128)(2,1)S(1)} collective-permute-done((bf16[8,16,2048]{2,1,0:T(8,128)(2,1)S(1)}, bf16[8,16,2048]{2,1,0:T(8,128)(2,1)S(1)}, u32[]{:S(2)}, u32[]{:S(2)}) %collective-permute-start.66) | collective-permute-done | bytes 524320 | tf_op jit(solution)/shard_map/ppermute | solution.py:275
  563.3 9.9 %collective-permute-done.67.refs_47_ = bf16[8,16,2048]{2,1,0:T(8,128)(2,1)S(1)} collective-permute-done((bf16[8,16,2048]{2,1,0:T(8,128)(2,1)S(1)}, bf16[8,16,2048]{2,1,0:T(8,128)(2,1)S(1)}, u32[]{:S(2)}, u32[]{:S(2)}) %collective-permute-start.67) | collective-permute-done | bytes 524320 | tf_op jit(solution)/shard_map/ppermute | solution.py:275
  574.5 9.9 %collective-permute-done.68.refs_48_ = bf16[8,16,2048]{2,1,0:T(8,128)(2,1)S(1)} collective-permute-done((bf16[8,16,2048]{2,1,0:T(8,128)(2,1)S(1)}, bf16[8,16,2048]{2,1,0:T(8,128)(2,1)S(1)}, u32[]{:S(2)}, u32[]{:S(2)}) %collective-permute-start.68) | collective-permute-done | bytes 524320 | tf_op jit(solution)/shard_map/ppermute | solution.py:275
  585.7 9.9 %collective-permute-done.69.refs_49_ = bf16[8,16,2048]{2,1,0:T(8,128)(2,1)S(1)} collective-permute-done((bf16[8,16,2048]{2,1,0:T(8,128)(2,1)S(1)}, bf16[8,16,2048]{2,1,0:T(8,128)(2,1)S(1)}, u32[]{:S(2)}, u32[]{:S(2)}) %collective-permute-start.69) | collective-permute-done | bytes 524320 | tf_op jit(solution)/shard_map/ppermute | solution.py:275
  597.9 9.1 %collective-permute-done.70.refs_50_ = bf16[8,16,2048]{2,1,0:T(8,128)(2,1)} collective-permute-done((bf16[8,16,2048]{2,1,0:T(8,128)(2,1)}, bf16[8,16,2048]{2,1,0:T(8,128)(2,1)}, u32[]{:S(2)}, u32[]{:S(2)}) %collective-permute-start.70) | collective-permute-done | bytes 524320 | tf_op jit(solution)/shard_map/ppermute | solution.py:275
  607.0 8.6 %collective-permute-done.71.refs_51_ = bf16[8,16,2048]{2,1,0:T(8,128)(2,1)} collective-permute-done((bf16[8,16,2048]{2,1,0:T(8,128)(2,1)}, bf16[8,16,2048]{2,1,0:T(8,128)(2,1)}, u32[]{:S(2)}, u32[]{:S(2)}) %collective-permute-start.71) | collective-permute-done | bytes 524320 | tf_op jit(solution)/shard_map/ppermute | solution.py:275
  642.8 18.6 %shard_map.50 = f32[7,128,128]{2,1,0:T(8,128)S(1)} custom-call(bf16[8,64,2048]{2,1,0:T(8,128)(2,1)} %copy-done, bf16[8,64,2048]{2,1,0:T(8,128)(2,1)} %copy-done.62, bf16[8,64,2048]{2,1,0:T(8,128)(2,1)} %copy-done.1, bf16[8,64,2048]{2,1,0:T(8,128)(2,1)} %collective-permute-done.31.refs_3_, bf16[8,64,2048]{2,1,0:T(8,128)(2,1)} %copy-done.63, ...), custom_call_target="tpu_custom_call" | custom-call | flops 5368709120 | bytes 50331648 | tf_op jit(solution)/shard_map/pallas_call | solution.py:259
  663.4 4.3 collective-permute-done.80
  670.7 4.1 collective-permute-done.82
  674.9 2.2 collective-permute-start.83
  677.1 2.6 collective-permute-done.84
  680.1 14.6 %collective-permute-start.86 = (f32[64,128]{1,0:T(8,128)S(1)}, f32[64,128]{1,0:T(8,128)S(1)}, u32[]{:S(2)}, u32[]{:S(2)}) collective-permute-start(f32[64,128]{1,0:T(8,128)S(1)} %get-tuple-element.109), channel_id=1, source_target_pairs={{0,20},{4,16},{8,28},{12,24},{16,4},{20,0},{24,12},{28,8},{1,21},{... | collective-permute-start | bytes 98312 | tf_op jit(solution)/shard_map/ppermute | solution.py:279
  694.7 2.8 collective-permute-start.85
  697.5 3.0 collective-permute-done.86
  701.9 4.3 collective-permute-start.88
  706.1 5.7 collective-permute-start.87
  711.9 6.6 pad_maximum_fusion
  (384 shorter events, 126.3 us)
Async XLA Ops:
  7.0 33.6 %collective-permute-start.24 = (bf16[4,16,4096]{2,1,0:T(8,128)(2,1)}, bf16[4,16,4096]{2,1,0:T(8,128)(2,1)S(1)}, u32[]{:S(2)}, u32[]{:S(2)}) collective-permute-start(bf16[4,16,4096]{2,1,0:T(8,128)(2,1)} %get-tuple-element.84), channel_id=1, source_target_pairs={{0,1},{1,0},{2,3},{3,2},{4,5},{5,4},{6,7},{7,6},{8,9},{9,8},{10,11... | collective-permute-start | bytes 1572872 | tf_op jit(solution)/shard_map/ppermute | solution.py:279
  11.7 38.1 %collective-permute-start.18 = (bf16[4,16,4096]{2,1,0:T(8,128)(2,1)}, bf16[4,16,4096]{2,1,0:T(8,128)(2,1)}, u32[]{:S(2)}, u32[]{:S(2)}) collective-permute-start(bf16[4,16,4096]{2,1,0:T(8,128)(2,1)} %get-tuple-element.88), channel_id=1, source_target_pairs={{0,1},{1,0},{2,3},{3,2},{4,5},{5,4},{6,7},{7,6},{8,9},{9,8},{10,11... | collective-permute-start | bytes 1572872 | tf_op jit(solution)/shard_map/ppermute | solution.py:279
  11.9 39.3 %collective-permute-start.19 = (bf16[4,16,4096]{2,1,0:T(8,128)(2,1)}, bf16[4,16,4096]{2,1,0:T(8,128)(2,1)}, u32[]{:S(2)}, u32[]{:S(2)}) collective-permute-start(bf16[4,16,4096]{2,1,0:T(8,128)(2,1)} %get-tuple-element.87), channel_id=1, source_target_pairs={{0,2},{1,3},{2,0},{3,1},{4,6},{5,7},{6,4},{7,5},{8,10},{9,11},{10,... | collective-permute-start | bytes 1572872 | tf_op jit(solution)/shard_map/ppermute | solution.py:279
  13.4 38.1 %collective-permute-start.20 = (bf16[4,16,4096]{2,1,0:T(8,128)(2,1)}, bf16[4,16,4096]{2,1,0:T(8,128)(2,1)}, u32[]{:S(2)}, u32[]{:S(2)}) collective-permute-start(bf16[4,16,4096]{2,1,0:T(8,128)(2,1)} %get-tuple-element.86), channel_id=1, source_target_pairs={{0,3},{1,2},{2,1},{3,0},{4,7},{5,6},{6,5},{7,4},{8,11},{9,10},{10,... | collective-permute-start | bytes 1572872 | tf_op jit(solution)/shard_map/ppermute | solution.py:279
  49.3 23.8 %collective-permute-start.13 = (bf16[4,16,4096]{2,1,0:T(8,128)(2,1)}, bf16[4,16,4096]{2,1,0:T(8,128)(2,1)S(1)}, u32[]{:S(2)}, u32[]{:S(2)}) collective-permute-start(bf16[4,16,4096]{2,1,0:T(8,128)(2,1)} %get-tuple-element.91), channel_id=1, source_target_pairs={{0,2},{1,3},{2,0},{3,1},{4,6},{5,7},{6,4},{7,5},{8,10},{9,11},{10,... | collective-permute-start | bytes 1572872 | tf_op jit(solution)/shard_map/ppermute | solution.py:279
  49.8 24.8 %collective-permute-start.14 = (bf16[4,16,4096]{2,1,0:T(8,128)(2,1)}, bf16[4,16,4096]{2,1,0:T(8,128)(2,1)S(1)}, u32[]{:S(2)}, u32[]{:S(2)}) collective-permute-start(bf16[4,16,4096]{2,1,0:T(8,128)(2,1)} %get-tuple-element.90), channel_id=1, source_target_pairs={{0,3},{1,2},{2,1},{3,0},{4,7},{5,6},{6,5},{7,4},{8,11},{9,10},{10,... | collective-permute-start | bytes 1572872 | tf_op jit(solution)/shard_map/ppermute | solution.py:279
  51.2 24.2 %collective-permute-start = (bf16[4,16,4096]{2,1,0:T(8,128)(2,1)}, bf16[4,16,4096]{2,1,0:T(8,128)(2,1)S(1)}, u32[]{:S(2)}, u32[]{:S(2)}) collective-permute-start(bf16[4,16,4096]{2,1,0:T(8,128)(2,1)} %get-tuple-element.95), channel_id=1, source_target_pairs={{0,1},{1,0},{2,3},{3,2},{4,5},{5,4},{6,7},{7,6},{8,9},{9,8},{10,11... | collective-permute-start | bytes 1572872 | tf_op jit(solution)/shard_map/ppermute | solution.py:279
  51.6 35.3 %collective-permute-start.1 = (bf16[4,16,4096]{2,1,0:T(8,128)(2,1)}, bf16[4,16,4096]{2,1,0:T(8,128)(2,1)S(1)}, u32[]{:S(2)}, u32[]{:S(2)}) collective-permute-start(bf16[4,16,4096]{2,1,0:T(8,128)(2,1)} %get-tuple-element.94), channel_id=1, source_target_pairs={{0,2},{1,3},{2,0},{3,1},{4,6},{5,7},{6,4},{7,5},{8,10},{9,11},{10,... | collective-permute-start | bytes 1572872 | tf_op jit(solution)/shard_map/ppermute | solution.py:279
  53.0 51.9 %collective-permute-start.2 = (bf16[4,16,4096]{2,1,0:T(8,128)(2,1)}, bf16[4,16,4096]{2,1,0:T(8,128)(2,1)S(1)}, u32[]{:S(2)}, u32[]{:S(2)}) collective-permute-start(bf16[4,16,4096]{2,1,0:T(8,128)(2,1)} %get-tuple-element.82), channel_id=1, source_target_pairs={{0,3},{1,2},{2,1},{3,0},{4,7},{5,6},{6,5},{7,4},{8,11},{9,10},{10,... | collective-permute-start | bytes 1572872 | tf_op jit(solution)/shard_map/ppermute | solution.py:279
  73.1 49.8 %collective-permute-start.25 = (bf16[4,16,4096]{2,1,0:T(8,128)(2,1)S(1)}, bf16[4,16,4096]{2,1,0:T(8,128)(2,1)S(1)}, u32[]{:S(2)}, u32[]{:S(2)}) collective-permute-start(bf16[4,16,4096]{2,1,0:T(8,128)(2,1)S(1)} %copy-done.84), channel_id=1, source_target_pairs={{0,2},{1,3},{2,0},{3,1},{4,6},{5,7},{6,4},{7,5},{8,10},{9,11},{10,... | collective-permute-start | bytes 1572872 | tf_op jit(solution)/shard_map/ppermute | solution.py:279
  74.7 49.9 %collective-permute-start.26 = (bf16[4,16,4096]{2,1,0:T(8,128)(2,1)S(1)}, bf16[4,16,4096]{2,1,0:T(8,128)(2,1)S(1)}, u32[]{:S(2)}, u32[]{:S(2)}) collective-permute-start(bf16[4,16,4096]{2,1,0:T(8,128)(2,1)S(1)} %copy-done.83), channel_id=1, source_target_pairs={{0,3},{1,2},{2,1},{3,0},{4,7},{5,6},{6,5},{7,4},{8,11},{9,10},{10,... | collective-permute-start | bytes 1572872 | tf_op jit(solution)/shard_map/ppermute | solution.py:279
  75.4 49.1 %collective-permute-start.21 = (bf16[4,16,4096]{2,1,0:T(8,128)(2,1)S(1)}, bf16[4,16,4096]{2,1,0:T(8,128)(2,1)S(1)}, u32[]{:S(2)}, u32[]{:S(2)}) collective-permute-start(bf16[4,16,4096]{2,1,0:T(8,128)(2,1)S(1)} %get-tuple-element.53), channel_id=1, source_target_pairs={{0,1},{1,0},{2,3},{3,2},{4,5},{5,4},{6,7},{7,6},{8,9},{9,8},{10,11... | collective-permute-start | bytes 1572872 | tf_op jit(solution)/shard_map/ppermute | solution.py:279
  86.8 44.9 %collective-permute-start.22 = (bf16[4,16,4096]{2,1,0:T(8,128)(2,1)S(1)}, bf16[4,16,4096]{2,1,0:T(8,128)(2,1)S(1)}, u32[]{:S(2)}, u32[]{:S(2)}) collective-permute-start(bf16[4,16,4096]{2,1,0:T(8,128)(2,1)S(1)} %get-tuple-element.54), channel_id=1, source_target_pairs={{0,2},{1,3},{2,0},{3,1},{4,6},{5,7},{6,4},{7,5},{8,10},{9,11},{10,... | collective-permute-start | bytes 1572872 | tf_op jit(solution)/shard_map/ppermute | solution.py:279
  104.9 26.8 %collective-permute-start.15 = (bf16[4,16,4096]{2,1,0:T(8,128)(2,1)S(1)}, bf16[4,16,4096]{2,1,0:T(8,128)(2,1)S(1)}, u32[]{:S(2)}, u32[]{:S(2)}) collective-permute-start(bf16[4,16,4096]{2,1,0:T(8,128)(2,1)S(1)} %get-tuple-element.48), channel_id=1, source_target_pairs={{0,1},{1,0},{2,3},{3,2},{4,5},{5,4},{6,7},{7,6},{8,9},{9,8},{10,11... | collective-permute-start | bytes 1572872 | tf_op jit(solution)/shard_map/ppermute | solution.py:279
  122.9 28.3 %collective-permute-start.16 = (bf16[4,16,4096]{2,1,0:T(8,128)(2,1)S(1)}, bf16[4,16,4096]{2,1,0:T(8,128)(2,1)S(1)}, u32[]{:S(2)}, u32[]{:S(2)}) collective-permute-start(bf16[4,16,4096]{2,1,0:T(8,128)(2,1)S(1)} %get-tuple-element.49), channel_id=1, source_target_pairs={{0,2},{1,3},{2,0},{3,1},{4,6},{5,7},{6,4},{7,5},{8,10},{9,11},{10,... | collective-permute-start | bytes 1572872 | tf_op jit(solution)/shard_map/ppermute | solution.py:279
  124.6 26.7 %collective-permute-start.9 = (bf16[4,16,4096]{2,1,0:T(8,128)(2,1)S(1)}, bf16[4,16,4096]{2,1,0:T(8,128)(2,1)S(1)}, u32[]{:S(2)}, u32[]{:S(2)}) collective-permute-start(bf16[4,16,4096]{2,1,0:T(8,128)(2,1)S(1)} %get-tuple-element.43), channel_id=1, source_target_pairs={{0,1},{1,0},{2,3},{3,2},{4,5},{5,4},{6,7},{7,6},{8,9},{9,8},{10,11... | collective-permute-start | bytes 1572872 | tf_op jit(solution)/shard_map/ppermute | solution.py:279
  124.6 29.6 %collective-permute-start.10 = (bf16[4,16,4096]{2,1,0:T(8,128)(2,1)S(1)}, bf16[4,16,4096]{2,1,0:T(8,128)(2,1)S(1)}, u32[]{:S(2)}, u32[]{:S(2)}) collective-permute-start(bf16[4,16,4096]{2,1,0:T(8,128)(2,1)S(1)} %get-tuple-element.44), channel_id=1, source_target_pairs={{0,2},{1,3},{2,0},{3,1},{4,6},{5,7},{6,4},{7,5},{8,10},{9,11},{10,... | collective-permute-start | bytes 1572872 | tf_op jit(solution)/shard_map/ppermute | solution.py:279
  131.7 32.8 %collective-permute-start.11 = (bf16[4,16,4096]{2,1,0:T(8,128)(2,1)S(1)}, bf16[4,16,4096]{2,1,0:T(8,128)(2,1)S(1)}, u32[]{:S(2)}, u32[]{:S(2)}) collective-permute-start(bf16[4,16,4096]{2,1,0:T(8,128)(2,1)S(1)} %get-tuple-element.45), channel_id=1, source_target_pairs={{0,3},{1,2},{2,1},{3,0},{4,7},{5,6},{6,5},{7,4},{8,11},{9,10},{10,... | collective-permute-start | bytes 1572872 | tf_op jit(solution)/shard_map/ppermute | solution.py:279
  131.8 44.0 %collective-permute-start.17 = (bf16[4,16,4096]{2,1,0:T(8,128)(2,1)S(1)}, bf16[4,16,4096]{2,1,0:T(8,128)(2,1)S(1)}, u32[]{:S(2)}, u32[]{:S(2)}) collective-permute-start(bf16[4,16,4096]{2,1,0:T(8,128)(2,1)S(1)} %get-tuple-element.50), channel_id=1, source_target_pairs={{0,3},{1,2},{2,1},{3,0},{4,7},{5,6},{6,5},{7,4},{8,11},{9,10},{10,... | collective-permute-start | bytes 1572872 | tf_op jit(solution)/shard_map/ppermute | solution.py:279
  151.2 35.8 %collective-permute-start.23 = (bf16[4,16,4096]{2,1,0:T(8,128)(2,1)S(1)}, bf16[4,16,4096]{2,1,0:T(8,128)(2,1)S(1)}, u32[]{:S(2)}, u32[]{:S(2)}) collective-permute-start(bf16[4,16,4096]{2,1,0:T(8,128)(2,1)S(1)} %get-tuple-element.55), channel_id=1, source_target_pairs={{0,3},{1,2},{2,1},{3,0},{4,7},{5,6},{6,5},{7,4},{8,11},{9,10},{10,... | collective-permute-start | bytes 1572872 | tf_op jit(solution)/shard_map/ppermute | solution.py:279
  151.3 38.6 %collective-permute-start.27 = (bf16[4,16,4096]{2,1,0:T(8,128)(2,1)S(1)}, bf16[4,16,4096]{2,1,0:T(8,128)(2,1)S(1)}, u32[]{:S(2)}, u32[]{:S(2)}) collective-permute-start(bf16[4,16,4096]{2,1,0:T(8,128)(2,1)S(1)} %get-tuple-element.58), channel_id=1, source_target_pairs={{0,1},{1,0},{2,3},{3,2},{4,5},{5,4},{6,7},{7,6},{8,9},{9,8},{10,11... | collective-permute-start | bytes 1572872 | tf_op jit(solution)/shard_map/ppermute | solution.py:279
  154.2 44.9 %collective-permute-start.28 = (bf16[4,16,4096]{2,1,0:T(8,128)(2,1)S(1)}, bf16[4,16,4096]{2,1,0:T(8,128)(2,1)S(1)}, u32[]{:S(2)}, u32[]{:S(2)}) collective-permute-start(bf16[4,16,4096]{2,1,0:T(8,128)(2,1)S(1)} %get-tuple-element.59), channel_id=1, source_target_pairs={{0,2},{1,3},{2,0},{3,1},{4,6},{5,7},{6,4},{7,5},{8,10},{9,11},{10,... | collective-permute-start | bytes 1572872 | tf_op jit(solution)/shard_map/ppermute | solution.py:279
  164.5 44.9 %collective-permute-start.29 = (bf16[4,16,4096]{2,1,0:T(8,128)(2,1)S(1)}, bf16[4,16,4096]{2,1,0:T(8,128)(2,1)S(1)}, u32[]{:S(2)}, u32[]{:S(2)}) collective-permute-start(bf16[4,16,4096]{2,1,0:T(8,128)(2,1)S(1)} %get-tuple-element.60), channel_id=1, source_target_pairs={{0,3},{1,2},{2,1},{3,0},{4,7},{5,6},{6,5},{7,4},{8,11},{9,10},{10,... | collective-permute-start | bytes 1572872 | tf_op jit(solution)/shard_map/ppermute | solution.py:279
  175.8 41.2 %collective-permute-start.40 = (bf16[8,16,2048]{2,1,0:T(8,128)(2,1)S(1)}, bf16[8,16,2048]{2,1,0:T(8,128)(2,1)S(1)}, u32[]{:S(2)}, u32[]{:S(2)}) collective-permute-start(bf16[8,16,2048]{2,1,0:T(8,128)(2,1)S(1)} %get-tuple-element.70), channel_id=1, source_target_pairs={{0,4},{4,0},{8,12},{12,8},{16,20},{20,16},{24,28},{28,24},{1,5},{5... | collective-permute-start | bytes 1572872 | tf_op jit(solution)/shard_map/ppermute | solution.py:279
  187.0 30.5 %collective-permute-start.41 = (bf16[8,16,2048]{2,1,0:T(8,128)(2,1)S(1)}, bf16[8,16,2048]{2,1,0:T(8,128)(2,1)S(1)}, u32[]{:S(2)}, u32[]{:S(2)}) collective-permute-start(bf16[8,16,2048]{2,1,0:T(8,128)(2,1)S(1)} %get-tuple-element.71), channel_id=1, source_target_pairs={{0,4},{4,0},{8,12},{12,8},{16,20},{20,16},{24,28},{28,24},{1,5},{5... | collective-permute-start | bytes 1572872 | tf_op jit(solution)/shard_map/ppermute | solution.py:279
  189.9 29.2 %collective-permute-start.42 = (bf16[8,16,2048]{2,1,0:T(8,128)(2,1)S(1)}, bf16[8,16,2048]{2,1,0:T(8,128)(2,1)S(1)}, u32[]{:S(2)}, u32[]{:S(2)}) collective-permute-start(bf16[8,16,2048]{2,1,0:T(8,128)(2,1)S(1)} %get-tuple-element.72), channel_id=1, source_target_pairs={{0,4},{4,0},{8,12},{12,8},{16,20},{20,16},{24,28},{28,24},{1,5},{5... | collective-permute-start | bytes 1572872 | tf_op jit(solution)/shard_map/ppermute | solution.py:279
  211.8 14.7 %collective-permute-start.43 = (bf16[8,16,2048]{2,1,0:T(8,128)(2,1)S(1)}, bf16[8,16,2048]{2,1,0:T(8,128)(2,1)S(1)}, u32[]{:S(2)}, u32[]{:S(2)}) collective-permute-start(bf16[8,16,2048]{2,1,0:T(8,128)(2,1)S(1)} %get-tuple-element.73), channel_id=1, source_target_pairs={{0,4},{4,0},{8,12},{12,8},{16,20},{20,16},{24,28},{28,24},{1,5},{5... | collective-permute-start | bytes 1572872 | tf_op jit(solution)/shard_map/ppermute | solution.py:279
  215.4 119.6 %collective-permute-start.30 = (bf16[8,64,2048]{2,1,0:T(8,128)(2,1)S(1)}, bf16[8,64,2048]{2,1,0:T(8,128)(2,1)S(1)}, u32[]{:S(2)}, u32[]{:S(2)}) collective-permute-start(bf16[8,64,2048]{2,1,0:T(8,128)(2,1)S(1)} %get-tuple-element.63), channel_id=1, source_target_pairs={{0,4},{4,0},{8,12},{12,8},{16,20},{20,16},{24,28},{28,24},{1,5},{5... | collective-permute-start | bytes 6291464 | tf_op jit(solution)/shard_map/ppermute | solution.py:279
  217.0 65.7 %collective-permute-start.44 = (bf16[8,16,2048]{2,1,0:T(8,128)(2,1)S(1)}, bf16[8,16,2048]{2,1,0:T(8,128)(2,1)S(1)}, u32[]{:S(2)}, u32[]{:S(2)}) collective-permute-start(bf16[8,16,2048]{2,1,0:T(8,128)(2,1)S(1)} %get-tuple-element.78), channel_id=1, source_target_pairs={{0,4},{4,0},{8,12},{12,8},{16,20},{20,16},{24,28},{28,24},{1,5},{5... | collective-permute-start | bytes 1572872 | tf_op jit(solution)/shard_map/ppermute | solution.py:279
  217.5 76.5 %collective-permute-start.45 = (bf16[8,16,2048]{2,1,0:T(8,128)(2,1)S(1)}, bf16[8,16,2048]{2,1,0:T(8,128)(2,1)S(1)}, u32[]{:S(2)}, u32[]{:S(2)}) collective-permute-start(bf16[8,16,2048]{2,1,0:T(8,128)(2,1)S(1)} %get-tuple-element.79), channel_id=1, source_target_pairs={{0,4},{4,0},{8,12},{12,8},{16,20},{20,16},{24,28},{28,24},{1,5},{5... | collective-permute-start | bytes 1572872 | tf_op jit(solution)/shard_map/ppermute | solution.py:279
  219.0 86.2 %collective-permute-start.46 = (bf16[8,16,2048]{2,1,0:T(8,128)(2,1)S(1)}, bf16[8,16,2048]{2,1,0:T(8,128)(2,1)S(1)}, u32[]{:S(2)}, u32[]{:S(2)}) collective-permute-start(bf16[8,16,2048]{2,1,0:T(8,128)(2,1)S(1)} %get-tuple-element.80), channel_id=1, source_target_pairs={{0,4},{4,0},{8,12},{12,8},{16,20},{20,16},{24,28},{28,24},{1,5},{5... | collective-permute-start | bytes 1572872 | tf_op jit(solution)/shard_map/ppermute | solution.py:279
  226.6 89.6 %collective-permute-start.47 = (bf16[8,16,2048]{2,1,0:T(8,128)(2,1)S(1)}, bf16[8,16,2048]{2,1,0:T(8,128)(2,1)S(1)}, u32[]{:S(2)}, u32[]{:S(2)}) collective-permute-start(bf16[8,16,2048]{2,1,0:T(8,128)(2,1)S(1)} %get-tuple-element.81), channel_id=1, source_target_pairs={{0,4},{4,0},{8,12},{12,8},{16,20},{20,16},{24,28},{28,24},{1,5},{5... | collective-permute-start | bytes 1572872 | tf_op jit(solution)/shard_map/ppermute | solution.py:279
  282.7 34.1 %collective-permute-start.48 = (bf16[8,16,2048]{2,1,0:T(8,128)(2,1)S(1)}, bf16[8,16,2048]{2,1,0:T(8,128)(2,1)S(1)}, u32[]{:S(2)}, u32[]{:S(2)}) collective-permute-start(bf16[8,16,2048]{2,1,0:T(8,128)(2,1)S(1)} %get-tuple-element.74.refs_20_), channel_id=1, source_target_pairs={{24,16},{28,20},{16,8},{20,12},{25,17},{29,21},{17,9},{21,13},{26,... | collective-permute-start | bytes 1572872 | tf_op jit(solution)/shard_map/ppermute | solution.py:275
  294.0 23.6 %collective-permute-start.49 = (bf16[8,16,2048]{2,1,0:T(8,128)(2,1)S(1)}, bf16[8,16,2048]{2,1,0:T(8,128)(2,1)S(1)}, u32[]{:S(2)}, u32[]{:S(2)}) collective-permute-start(bf16[8,16,2048]{2,1,0:T(8,128)(2,1)S(1)} %get-tuple-element.75.refs_21_), channel_id=1, source_target_pairs={{24,16},{28,20},{16,8},{20,12},{25,17},{29,21},{17,9},{21,13},{26,... | collective-permute-start | bytes 1572872 | tf_op jit(solution)/shard_map/ppermute | solution.py:275
  316.8 17.4 %collective-permute-start.72 = (bf16[8,16,2048]{2,1,0:T(8,128)(2,1)S(1)}, bf16[8,16,2048]{2,1,0:T(8,128)(2,1)S(1)}, u32[]{:S(2)}, u32[]{:S(2)}) collective-permute-start(bf16[8,16,2048]{2,1,0:T(8,128)(2,1)S(1)} %get-tuple-element.66.refs_12_), channel_id=1, source_target_pairs={{24,16},{28,20},{25,17},{29,21},{26,18},{30,22},{27,19},{31,23}} | collective-permute-start | bytes 1572872 | tf_op jit(solution)/shard_map/ppermute | solution.py:275
  317.5 47.5 %collective-permute-start.31 = (bf16[8,64,2048]{2,1,0:T(8,128)(2,1)S(1)}, bf16[8,64,2048]{2,1,0:T(8,128)(2,1)}, u32[]{:S(2)}, u32[]{:S(2)}) collective-permute-start(bf16[8,64,2048]{2,1,0:T(8,128)(2,1)S(1)} %get-tuple-element.65), channel_id=1, source_target_pairs={{0,4},{4,0},{8,12},{12,8},{16,20},{20,16},{24,28},{28,24},{1,5},{5... | collective-permute-start | bytes 6291464 | tf_op jit(solution)/shard_map/ppermute | solution.py:279
  318.1 50.9 %collective-permute-start.32 = (bf16[8,64,2048]{2,1,0:T(8,128)(2,1)S(1)}, bf16[8,64,2048]{2,1,0:T(8,128)(2,1)S(1)}, u32[]{:S(2)}, u32[]{:S(2)}) collective-permute-start(bf16[8,64,2048]{2,1,0:T(8,128)(2,1)S(1)} %get-tuple-element.62.refs_0_), channel_id=1, source_target_pairs={{0,8},{4,12},{8,16},{12,20},{1,9},{5,13},{9,17},{13,21},{2,10},{6,... | collective-permute-start | bytes 6291464 | tf_op jit(solution)/shard_map/ppermute | solution.py:275
  323.0 90.9 %collective-permute-start.38 = (bf16[8,64,2048]{2,1,0:T(8,128)(2,1)S(1)}, bf16[8,64,2048]{2,1,0:T(8,128)(2,1)S(1)}, u32[]{:S(2)}, u32[]{:S(2)}) collective-permute-start(bf16[8,64,2048]{2,1,0:T(8,128)(2,1)S(1)} %get-tuple-element.64.refs_2_), channel_id=1, source_target_pairs={{0,8},{4,12},{1,9},{5,13},{2,10},{6,14},{3,11},{7,15}} | collective-permute-start | bytes 6291464 | tf_op jit(solution)/shard_map/ppermute | solution.py:275
  335.0 121.2 %collective-permute-start.33 = (bf16[8,64,2048]{2,1,0:T(8,128)(2,1)S(1)}, bf16[8,64,2048]{2,1,0:T(8,128)(2,1)S(1)}, u32[]{:S(2)}, u32[]{:S(2)}) collective-permute-start(bf16[8,64,2048]{2,1,0:T(8,128)(2,1)S(1)} %collective-permute-done.30.refs_1_), channel_id=1, source_target_pairs={{0,8},{4,12},{8,16},{12,20},{1,9},{5,13},{9,17},{13,21},{2,10},{6,... | collective-permute-start | bytes 6291464 | tf_op jit(solution)/shard_map/ppermute | solution.py:275
  338.0 77.5 %collective-permute-start.52 = (bf16[8,16,2048]{2,1,0:T(8,128)(2,1)S(1)}, bf16[8,16,2048]{2,1,0:T(8,128)(2,1)S(1)}, u32[]{:S(2)}, u32[]{:S(2)}) collective-permute-start(bf16[8,16,2048]{2,1,0:T(8,128)(2,1)S(1)} %collective-permute-done.44.refs_24_), channel_id=1, source_target_pairs={{24,16},{28,20},{16,8},{20,12},{25,17},{29,21},{17,9},{21,13},{26,... | collective-permute-start | bytes 1572872 | tf_op jit(solution)/shard_map/ppermute | solution.py:275
  365.1 52.5 %collective-permute-start.53 = (bf16[8,16,2048]{2,1,0:T(8,128)(2,1)S(1)}, bf16[8,16,2048]{2,1,0:T(8,128)(2,1)S(1)}, u32[]{:S(2)}, u32[]{:S(2)}) collective-permute-start(bf16[8,16,2048]{2,1,0:T(8,128)(2,1)S(1)} %collective-permute-done.45.refs_25_), channel_id=1, source_target_pairs={{24,16},{28,20},{16,8},{20,12},{25,17},{29,21},{17,9},{21,13},{26,... | collective-permute-start | bytes 1572872 | tf_op jit(solution)/shard_map/ppermute | solution.py:275
  369.0 50.7 %collective-permute-start.54 = (bf16[8,16,2048]{2,1,0:T(8,128)(2,1)S(1)}, bf16[8,16,2048]{2,1,0:T(8,128)(2,1)S(1)}, u32[]{:S(2)}, u32[]{:S(2)}) collective-permute-start(bf16[8,16,2048]{2,1,0:T(8,128)(2,1)S(1)} %collective-permute-done.46.refs_26_), channel_id=1, source_target_pairs={{24,16},{28,20},{16,8},{20,12},{25,17},{29,21},{17,9},{21,13},{26,... | collective-permute-start | bytes 1572872 | tf_op jit(solution)/shard_map/ppermute | solution.py:275
  415.4 42.8 %collective-permute-start.56 = (bf16[8,16,2048]{2,1,0:T(8,128)(2,1)S(1)}, bf16[8,16,2048]{2,1,0:T(8,128)(2,1)S(1)}, u32[]{:S(2)}, u32[]{:S(2)}) collective-permute-start(bf16[8,16,2048]{2,1,0:T(8,128)(2,1)S(1)} %collective-permute-done.48.refs_28_), channel_id=1, source_target_pairs={{16,8},{20,12},{8,0},{12,4},{17,9},{21,13},{9,1},{13,5},{18,10},{2... | collective-permute-start | bytes 1572872 | tf_op jit(solution)/shard_map/ppermute | solution.py:275
  417.6 42.8 %collective-permute-start.57 = (bf16[8,16,2048]{2,1,0:T(8,128)(2,1)S(1)}, bf16[8,16,2048]{2,1,0:T(8,128)(2,1)S(1)}, u32[]{:S(2)}, u32[]{:S(2)}) collective-permute-start(bf16[8,16,2048]{2,1,0:T(8,128)(2,1)S(1)} %collective-permute-done.49.refs_29_), channel_id=1, source_target_pairs={{16,8},{20,12},{8,0},{12,4},{17,9},{21,13},{9,1},{13,5},{18,10},{2... | collective-permute-start | bytes 1572872 | tf_op jit(solution)/shard_map/ppermute | solution.py:275
  419.7 42.2 %collective-permute-start.58 = (bf16[8,16,2048]{2,1,0:T(8,128)(2,1)S(1)}, bf16[8,16,2048]{2,1,0:T(8,128)(2,1)S(1)}, u32[]{:S(2)}, u32[]{:S(2)}) collective-permute-start(bf16[8,16,2048]{2,1,0:T(8,128)(2,1)S(1)} %collective-permute-done.50.refs_30_), channel_id=1, source_target_pairs={{16,8},{20,12},{8,0},{12,4},{17,9},{21,13},{9,1},{13,5},{18,10},{2... | collective-permute-start | bytes 1572872 | tf_op jit(solution)/shard_map/ppermute | solution.py:275
  421.8 117.7 %collective-permute-start.34 = (bf16[8,64,2048]{2,1,0:T(8,128)(2,1)S(1)}, bf16[8,64,2048]{2,1,0:T(8,128)(2,1)}, u32[]{:S(2)}, u32[]{:S(2)}) collective-permute-start(bf16[8,64,2048]{2,1,0:T(8,128)(2,1)S(1)} %collective-permute-done.32.refs_4_), channel_id=1, source_target_pairs={{8,16},{12,20},{16,24},{20,28},{9,17},{13,21},{17,25},{21,29},{10,... | collective-permute-start | bytes 6291464 | tf_op jit(solution)/shard_map/ppermute | solution.py:275
  456.2 85.4 %collective-permute-start.35 = (bf16[8,64,2048]{2,1,0:T(8,128)(2,1)S(1)}, bf16[8,64,2048]{2,1,0:T(8,128)(2,1)}, u32[]{:S(2)}, u32[]{:S(2)}) collective-permute-start(bf16[8,64,2048]{2,1,0:T(8,128)(2,1)S(1)} %collective-permute-done.33.refs_5_), channel_id=1, source_target_pairs={{8,16},{12,20},{16,24},{20,28},{9,17},{13,21},{17,25},{21,29},{10,... | collective-permute-start | bytes 6291464 | tf_op jit(solution)/shard_map/ppermute | solution.py:275
  476.1 18.6 %collective-permute-start.60 = (bf16[8,16,2048]{2,1,0:T(8,128)(2,1)S(1)}, bf16[8,16,2048]{2,1,0:T(8,128)(2,1)S(1)}, u32[]{:S(2)}, u32[]{:S(2)}) collective-permute-start(bf16[8,16,2048]{2,1,0:T(8,128)(2,1)S(1)} %collective-permute-done.52.refs_32_), channel_id=1, source_target_pairs={{16,8},{20,12},{8,0},{12,4},{17,9},{21,13},{9,1},{13,5},{18,10},{2... | collective-permute-start | bytes 1572872 | tf_op jit(solution)/shard_map/ppermute | solution.py:275
  478.2 27.7 %collective-permute-start.61 = (bf16[8,16,2048]{2,1,0:T(8,128)(2,1)S(1)}, bf16[8,16,2048]{2,1,0:T(8,128)(2,1)S(1)}, u32[]{:S(2)}, u32[]{:S(2)}) collective-permute-start(bf16[8,16,2048]{2,1,0:T(8,128)(2,1)S(1)} %collective-permute-done.53.refs_33_), channel_id=1, source_target_pairs={{16,8},{20,12},{8,0},{12,4},{17,9},{21,13},{9,1},{13,5},{18,10},{2... | collective-permute-start | bytes 1572872 | tf_op jit(solution)/shard_map/ppermute | solution.py:275
  480.3 36.9 %collective-permute-start.62 = (bf16[8,16,2048]{2,1,0:T(8,128)(2,1)S(1)}, bf16[8,16,2048]{2,1,0:T(8,128)(2,1)}, u32[]{:S(2)}, u32[]{:S(2)}) collective-permute-start(bf16[8,16,2048]{2,1,0:T(8,128)(2,1)S(1)} %collective-permute-done.54.refs_34_), channel_id=1, source_target_pairs={{16,8},{20,12},{8,0},{12,4},{17,9},{21,13},{9,1},{13,5},{18,10},{2... | collective-permute-start | bytes 1572872 | tf_op jit(solution)/shard_map/ppermute | solution.py:275
  494.7 33.8 %collective-permute-start.63 = (bf16[8,16,2048]{2,1,0:T(8,128)(2,1)S(1)}, bf16[8,16,2048]{2,1,0:T(8,128)(2,1)}, u32[]{:S(2)}, u32[]{:S(2)}) collective-permute-start(bf16[8,16,2048]{2,1,0:T(8,128)(2,1)S(1)} %collective-permute-done.55.refs_35_), channel_id=1, source_target_pairs={{16,8},{20,12},{8,0},{12,4},{17,9},{21,13},{9,1},{13,5},{18,10},{2... | collective-permute-start | bytes 1572872 | tf_op jit(solution)/shard_map/ppermute | solution.py:275
  505.9 37.7 %collective-permute-start.64 = (bf16[8,16,2048]{2,1,0:T(8,128)(2,1)S(1)}, bf16[8,16,2048]{2,1,0:T(8,128)(2,1)S(1)}, u32[]{:S(2)}, u32[]{:S(2)}) collective-permute-start(bf16[8,16,2048]{2,1,0:T(8,128)(2,1)S(1)} %collective-permute-done.56.refs_36_), channel_id=1, source_target_pairs={{8,0},{12,4},{9,1},{13,5},{10,2},{14,6},{11,3},{15,7}} | collective-permute-start | bytes 1572872 | tf_op jit(solution)/shard_map/ppermute | solution.py:275
  517.2 33.5 %collective-permute-start.65 = (bf16[8,16,2048]{2,1,0:T(8,128)(2,1)S(1)}, bf16[8,16,2048]{2,1,0:T(8,128)(2,1)S(1)}, u32[]{:S(2)}, u32[]{:S(2)}) collective-permute-start(bf16[8,16,2048]{2,1,0:T(8,128)(2,1)S(1)} %collective-permute-done.57.refs_37_), channel_id=1, source_target_pairs={{8,0},{12,4},{9,1},{13,5},{10,2},{14,6},{11,3},{15,7}} | collective-permute-start | bytes 1572872 | tf_op jit(solution)/shard_map/ppermute | solution.py:275
  528.5 87.2 %collective-permute-start.39 = (bf16[8,64,2048]{2,1,0:T(8,128)(2,1)}, bf16[8,64,2048]{2,1,0:T(8,128)(2,1)}, u32[]{:S(2)}, u32[]{:S(2)}) collective-permute-start(bf16[8,64,2048]{2,1,0:T(8,128)(2,1)} %collective-permute-done.31.refs_3_), channel_id=1, source_target_pairs={{0,8},{4,12},{1,9},{5,13},{2,10},{6,14},{3,11},{7,15}} | collective-permute-start | bytes 6291464 | tf_op jit(solution)/shard_map/ppermute | solution.py:275
  539.5 76.2 %collective-permute-start.36 = (bf16[8,64,2048]{2,1,0:T(8,128)(2,1)}, bf16[8,64,2048]{2,1,0:T(8,128)(2,1)}, u32[]{:S(2)}, u32[]{:S(2)}) collective-permute-start(bf16[8,64,2048]{2,1,0:T(8,128)(2,1)} %collective-permute-done.34.refs_6_), channel_id=1, source_target_pairs={{16,24},{20,28},{17,25},{21,29},{18,26},{22,30},{19,27},{23,31}} | collective-permute-start | bytes 6291464 | tf_op jit(solution)/shard_map/ppermute | solution.py:275
  541.6 74.0 %collective-permute-start.37 = (bf16[8,64,2048]{2,1,0:T(8,128)(2,1)}, bf16[8,64,2048]{2,1,0:T(8,128)(2,1)}, u32[]{:S(2)}, u32[]{:S(2)}) collective-permute-start(bf16[8,64,2048]{2,1,0:T(8,128)(2,1)} %collective-permute-done.35.refs_7_), channel_id=1, source_target_pairs={{16,24},{20,28},{17,25},{21,29},{18,26},{22,30},{19,27},{23,31}} | collective-permute-start | bytes 6291464 | tf_op jit(solution)/shard_map/ppermute | solution.py:275
  543.6 18.4 %collective-permute-start.66 = (bf16[8,16,2048]{2,1,0:T(8,128)(2,1)S(1)}, bf16[8,16,2048]{2,1,0:T(8,128)(2,1)S(1)}, u32[]{:S(2)}, u32[]{:S(2)}) collective-permute-start(bf16[8,16,2048]{2,1,0:T(8,128)(2,1)S(1)} %collective-permute-done.58.refs_38_), channel_id=1, source_target_pairs={{8,0},{12,4},{9,1},{13,5},{10,2},{14,6},{11,3},{15,7}} | collective-permute-start | bytes 1572872 | tf_op jit(solution)/shard_map/ppermute | solution.py:275
  550.7 22.5 %collective-permute-start.67 = (bf16[8,16,2048]{2,1,0:T(8,128)(2,1)S(1)}, bf16[8,16,2048]{2,1,0:T(8,128)(2,1)S(1)}, u32[]{:S(2)}, u32[]{:S(2)}) collective-permute-start(bf16[8,16,2048]{2,1,0:T(8,128)(2,1)S(1)} %collective-permute-done.59.refs_39_), channel_id=1, source_target_pairs={{8,0},{12,4},{9,1},{13,5},{10,2},{14,6},{11,3},{15,7}} | collective-permute-start | bytes 1572872 | tf_op jit(solution)/shard_map/ppermute | solution.py:275
  562.0 22.5 %collective-permute-start.68 = (bf16[8,16,2048]{2,1,0:T(8,128)(2,1)S(1)}, bf16[8,16,2048]{2,1,0:T(8,128)(2,1)S(1)}, u32[]{:S(2)}, u32[]{:S(2)}) collective-permute-start(bf16[8,16,2048]{2,1,0:T(8,128)(2,1)S(1)} %collective-permute-done.60.refs_40_), channel_id=1, source_target_pairs={{8,0},{12,4},{9,1},{13,5},{10,2},{14,6},{11,3},{15,7}} | collective-permute-start | bytes 1572872 | tf_op jit(solution)/shard_map/ppermute | solution.py:275
  573.2 22.5 %collective-permute-start.69 = (bf16[8,16,2048]{2,1,0:T(8,128)(2,1)S(1)}, bf16[8,16,2048]{2,1,0:T(8,128)(2,1)S(1)}, u32[]{:S(2)}, u32[]{:S(2)}) collective-permute-start(bf16[8,16,2048]{2,1,0:T(8,128)(2,1)S(1)} %collective-permute-done.61.refs_41_), channel_id=1, source_target_pairs={{8,0},{12,4},{9,1},{13,5},{10,2},{14,6},{11,3},{15,7}} | collective-permute-start | bytes 1572872 | tf_op jit(solution)/shard_map/ppermute | solution.py:275
  584.4 22.6 %collective-permute-start.70 = (bf16[8,16,2048]{2,1,0:T(8,128)(2,1)}, bf16[8,16,2048]{2,1,0:T(8,128)(2,1)}, u32[]{:S(2)}, u32[]{:S(2)}) collective-permute-start(bf16[8,16,2048]{2,1,0:T(8,128)(2,1)} %collective-permute-done.62.refs_42_), channel_id=1, source_target_pairs={{8,0},{12,4},{9,1},{13,5},{10,2},{14,6},{11,3},{15,7}} | collective-permute-start | bytes 1572872 | tf_op jit(solution)/shard_map/ppermute | solution.py:275
  596.6 19.1 %collective-permute-start.71 = (bf16[8,16,2048]{2,1,0:T(8,128)(2,1)}, bf16[8,16,2048]{2,1,0:T(8,128)(2,1)}, u32[]{:S(2)}, u32[]{:S(2)}) collective-permute-start(bf16[8,16,2048]{2,1,0:T(8,128)(2,1)} %collective-permute-done.63.refs_43_), channel_id=1, source_target_pairs={{8,0},{12,4},{9,1},{13,5},{10,2},{14,6},{11,3},{15,7}} | collective-permute-start | bytes 1572872 | tf_op jit(solution)/shard_map/ppermute | solution.py:275
  680.1 20.4 %collective-permute-start.86 = (f32[64,128]{1,0:T(8,128)S(1)}, f32[64,128]{1,0:T(8,128)S(1)}, u32[]{:S(2)}, u32[]{:S(2)}) collective-permute-start(f32[64,128]{1,0:T(8,128)S(1)} %get-tuple-element.109), channel_id=1, source_target_pairs={{0,20},{4,16},{8,28},{12,24},{16,4},{20,0},{24,12},{28,8},{1,21},{... | collective-permute-start | bytes 98312 | tf_op jit(solution)/shard_map/ppermute | solution.py:279
  701.9 16.7 %collective-permute-start.88 = (f32[64,128]{0,1:T(8,128)S(1)}, f32[64,128]{0,1:T(8,128)S(1)}, u32[]{:S(2)}, u32[]{:S(2)}) collective-permute-start(f32[64,128]{0,1:T(8,128)S(1)} %copy.37), channel_id=1, source_target_pairs={{0,28},{4,24},{8,20},{12,16},{16,12},{20,8},{24,4},{28,0},{1,29},{... | collective-permute-start | bytes 98312 | tf_op jit(solution)/shard_map/ppermute | solution.py:279
  (113 other events, 3899.2 us)

commit v2 on v1

v2 whole, which is shorter than its diff:
```python
import math
import jax, jax.numpy as jnp
from jax import lax
from jax.experimental import pallas as pl
from jax.experimental.pallas import tpu as pltpu
from jax.sharding import PartitionSpec as P

NG = 64
NPTS = NG ** 3
KERNEL_SCALE = 128.0
LANES = 128
BF = jnp.bfloat16
F32 = jnp.float32
HALF = NG // 2
XW = 512
PLANES = 32
TILE = 16
SWAP = 256
HELD = ({2: (3,), 3: (4,)}, {0: (1, 2), 2: (3,), 3: (4,)}, {1: (1,), 0: (2,), 3: (3, 4)}, {1: (1,), 0: (2,)})


def cas_matrix(length):
    products = (
        jnp.arange(length, dtype=jnp.int32)[:, None]
        * jnp.arange(length, dtype=jnp.int32)[None, :]
        % length
    )
    angles = products.astype(F32) * (2.0 * math.pi / length)
    return jnp.cos(angles) + jnp.sin(angles)


def halves(value):
    high = value.astype(BF)
    return high, (value - high.astype(F32)).astype(BF)


def matrix_halves(value):
    high = lax.reduce_precision(value, 8, 7)
    return high.astype(BF), (value - high).astype(BF)


def kernel_table():
    frequency = jnp.arange(NG, dtype=jnp.int32)
    folded = jnp.minimum(frequency, NG - frequency).astype(F32)
    square = folded * folded
    summed = square[:, None, None] + square[None, :, None] + square[None, None, :]
    table = jnp.where(summed > 0, KERNEL_SCALE / NPTS / jnp.maximum(summed, 1.0), 0.0)
    return table.reshape(NG // 4, 4, NG, NG).transpose(0, 2, 1, 3).reshape(NG // 4, NG, 4 * NG)


def row_factor(matrix):
    high, low = matrix_halves(matrix)
    return jnp.concatenate([high, high, low], axis=1)


def lane_factor(matrix):
    high, low = matrix_halves(jnp.kron(jnp.eye(2, dtype=F32), matrix))
    upper = jnp.concatenate([high, low], axis=1)
    lower = jnp.concatenate([high, jnp.zeros_like(low)], axis=1)
    return jnp.concatenate([upper, lower], axis=0)


def dot(a, b):
    return jnp.dot(a, b, preferred_element_type=F32)


def solve_one(ins, partner, table, x_there, x_back, y_there, y_back, z_both, outs, work):
    rows = NG // len(ins)

    def along_rows(factor, value):
        high, low = halves(value)
        return dot(factor[...], jnp.concatenate([high, low, high], axis=0))

    def along_lanes(value):
        high, low = halves(value)
        both = dot(jnp.concatenate([high, low], axis=1), z_both[...])
        return both[:, :LANES] + both[:, LANES:]

    @pl.loop(0, NG * NG // XW, unroll=4)
    def _(i):
        at = pl.ds(pl.multiple_of(i * XW, XW), XW)
        field = jnp.concatenate([ref[:, at].astype(F32) for ref in ins], axis=0)
        field = along_rows(x_there, field * partner[:, at].astype(F32))
        for tile in range(XW // LANES):
            work[pl.ds(i * (XW // LANES) + tile, NG, stride=HALF), :] = field[:, tile * LANES:(tile + 1) * LANES]

    @pl.loop(0, NG // PLANES, unroll=2)
    def _(i):
        left = lax.broadcasted_iota(jnp.int32, (HALF, LANES), 1) < NG
        base = i * PLANES * HALF
        parts = []
        for pair in range(PLANES // 2):
            a = work[pl.ds(base + pair * NG, HALF), :]
            b = work[pl.ds(base + pair * NG + HALF, HALF), :]
            parts.append(jnp.where(left, a, pltpu.roll(b, NG, 1)))
            parts.append(jnp.where(left, pltpu.roll(a, NG, 1), b))
        field = along_lanes(jnp.concatenate(parts, axis=0))
        done = []
        for quad in range(PLANES // 4):
            wide = jnp.concatenate(
                [field[quad * 128:quad * 128 + 64], field[quad * 128 + 64:quad * 128 + 128]], axis=1
            )
            wide = along_rows(y_there, wide) * table[i * (PLANES // 4) + quad]
            wide = along_rows(y_back, wide)
            done.append(wide[:, :LANES])
            done.append(wide[:, LANES:])
        field = along_lanes(jnp.concatenate(done, axis=0))
        for pair in range(PLANES // 2):
            u = field[pair * NG:pair * NG + HALF]
            v = field[pair * NG + HALF:pair * NG + NG]
            work[pl.ds(base + pair * NG, HALF), :] = jnp.where(left, u, pltpu.roll(v, NG, 1))
            work[pl.ds(base + pair * NG + HALF, HALF), :] = jnp.where(left, pltpu.roll(u, NG, 1), v)

    @pl.loop(0, NG * NG // XW, unroll=4)
    def _(i):
        at = pl.ds(pl.multiple_of(i * XW, XW), XW)
        field = jnp.concatenate(
            [work[pl.ds(i * (XW // LANES) + tile, NG, stride=HALF), :] for tile in range(XW // LANES)], axis=1
        )
        field = (-along_rows(x_back, field) * partner[:, at].astype(F32)).astype(BF)
        for index, ref in enumerate(outs):
            ref[:, at] = field[index * rows:(index + 1) * rows]


def solve_body(groups, *refs):
    ins, outs = refs[:groups], refs[groups + 7:2 * groups + 7]
    solve_one([ref.at[0] for ref in ins], *refs[groups:groups + 7], [ref.at[0] for ref in outs], refs[-1])


def factors(planes_at):
    matrix = cas_matrix(NG)
    by_plane = jnp.take(matrix, planes_at, axis=1)
    by_line = matrix.reshape(NG, HALF, 2).transpose(0, 2, 1).reshape(NG, NG)
    return (
        kernel_table(), row_factor(by_plane), row_factor(by_plane.T),
        row_factor(by_line), row_factor(by_line.T), lane_factor(matrix),
    )


def solve(pieces, partner, fixed):
    groups = len(pieces)
    count, rows, square = pieces[0].shape
    block = pl.BlockSpec((1, rows, square), lambda i: (i, 0, 0))
    whole = lambda array: pl.BlockSpec(array.shape, lambda i: (0,) * array.ndim)
    fixed = (partner,) + fixed
    return pl.pallas_call(
        lambda *refs: solve_body(groups, *refs),
        grid=(count,),
        in_specs=[block] * groups + [whole(a) for a in fixed],
        out_specs=[block] * groups,
        out_shape=[jax.ShapeDtypeStruct(p.shape, BF) for p in pieces],
        scratch_shapes=[pltpu.VMEM((NG * HALF, LANES), F32)],
        compiler_params=pltpu.CompilerParams(vmem_limit_bytes=32 * 1024 * 1024),
        cost_estimate=pl.CostEstimate(
            flops=count * 12 * NG * NG * NG * 256, bytes_accessed=4 * count * NPTS, transcendentals=0
        ),
    )(*pieces, *fixed)
def swap_into(held, keep, send):
    width = held.shape[2] // 2
    mine = lax.axis_index("band") % 2

    @pl.loop(0, width // SWAP)
    def _(i):
        put = pl.ds(pl.multiple_of(i * SWAP, SWAP), SWAP)
        for at, out in ((mine, keep), (1 - mine, send)):
            lanes = pl.ds(pl.multiple_of(at * width + i * SWAP, SWAP), SWAP)
            out[:, :, put] = jnp.swapaxes(held[:, :, lanes], 0, 1)


def order_orbitals(orbitals):
    bands, rows, square = orbitals.shape
    part = jax.ShapeDtypeStruct((rows, bands, square // 2), BF)
    spec = pl.BlockSpec((rows, TILE, square // 2), lambda i: (0, i, 0))
    return pl.pallas_call(
        swap_into,
        grid=(bands // TILE,),
        in_specs=[pl.BlockSpec((TILE, rows, square), lambda i: (i, 0, 0))],
        out_specs=[spec] * 2,
        out_shape=[part] * 2,
        compiler_params=pltpu.CompilerParams(vmem_limit_bytes=24 * 1024 * 1024),
        cost_estimate=pl.CostEstimate(flops=0, bytes_accessed=4 * orbitals.size, transcendentals=0),
    )(orbitals)


def whole_body(chunks, groups, *refs):
    (orb, slab, okeep, osend, table, x_there, x_back, y_there, y_back, z_both,
     vectors, opeer, slots, parts,
     cubes, solved, fresh, partner, hyper, ekeep, epeer, esend, lslots, work, obuf, abuf,
     hyper_sem, pick_sem, fwd_sem, own_sem, back_sem, stay_sem, out_sem,
     oy_sem, r_sem, ey_sem, l_sem, load_sem) = refs
    count, rows = cubes.shape[2:4]
    mid = rows // 2
    band, me = lax.axis_index("band"), lax.axis_index("grid")
    layer = band // 2
    peer = band ^ 1
    up, down = lax.rem(band + 2, 8), lax.rem(band + 6, 8)

    def remote(source, target, sems, axis, index):
        return pltpu.make_async_remote_copy(
            src_ref=source, dst_ref=target, send_sem=sems[0], recv_sem=sems[1],
            device_id={axis: index}, device_id_type=pl.DeviceIdType.MESH,
        )

    def sems(array, *at):
        return array.at[(0,) + at], array.at[(1,) + at]

    barrier = pltpu.get_barrier_semaphore()
    for bits in (1, 2, 4, 6):
        pl.semaphore_signal(barrier, inc=1, device_id={"band": band ^ bits}, device_id_type=pl.DeviceIdType.MESH)
    for d in range(1, groups):
        pl.semaphore_signal(barrier, inc=1, device_id={"grid": me ^ d}, device_id_type=pl.DeviceIdType.MESH)
    pl.semaphore_wait(barrier, 3 + groups)

    def forward(c):
        def at(d):
            return orb.at[pl.ds(c * TILE + (me ^ d) * count, count)]
        moves = [remote(at(d), cubes.at[c, d], sems(fwd_sem, c, d - 1), "grid", me ^ d) for d in range(1, groups)]
        return moves, pltpu.make_async_copy(at(0), cubes.at[c, 0], own_sem.at[c])

    def start_forward(c):
        moves, stay = forward(c)
        for move in moves:
            move.start()
        stay.start()

    def back(c, mine):
        def at(d):
            return fresh.at[c, pl.ds((me if mine else me ^ d) * count, count)]
        moves = [remote(solved.at[c % 2, d], at(d), sems(back_sem, c, d - 1), "grid", me ^ d) for d in range(1, groups)]
        return moves, pltpu.make_async_copy(solved.at[c % 2, 0], fresh.at[c, pl.ds(me * count, count)], stay_sem.at[c])

    def r_move(slot, side, source):
        return remote(source, slots.at[slot, side], sems(r_sem, slot, side), "band", up)

    def l_move(slot, side, c, source):
        return remote(source, lslots.at[slot, side, c], sems(l_sem, slot, side, c), "band", down)

    def oy(half):
        at = pl.ds(half * mid, mid)
        return remote(osend.at[at], opeer.at[at], sems(oy_sem, half), "band", peer)

    def ey(c, half):
        at = pl.ds(half * mid, mid)
        return remote(esend.at[c, at], epeer.at[c, at], sems(ey_sem, c, half), "band", peer)

    steps = [remote(slab, hyper.at[0], sems(hyper_sem, 0), "band", band ^ 1)]
    steps.append(remote(hyper.at[3], hyper.at[1], sems(hyper_sem, 1), "band", band ^ 2))
    steps.append(remote(hyper.at[4], hyper.at[2], sems(hyper_sem, 2), "band", band ^ 4))
    mine = pl.ds(0, rows)
    picks = [
        remote(partner.at[mine], partner.at[pl.ds(d * rows, rows)], sems(pick_sem, d - 1), "grid", me ^ d)
        for d in range(1, groups)
    ]
    steps[0].start()
    start_forward(0)
    steps[0].wait_recv()
    hyper[3] = slab[...] + hyper[0]
    steps[1].start()
    steps[1].wait_recv()
    hyper[4] = hyper[3] + hyper[1]
    steps[2].start()
    steps[2].wait_recv()
    partner[mine] = hyper[4] + hyper[2]
    for move in picks:
        move.start()

    def only(layers, moves):
        for at in layers:
            @pl.when(layer == at)
            def _():
                for move in moves:
                    move.start()

    def first_orbitals():
        oy(0).start()
        only((0, 1), [r_move(0, 0, okeep.at[pl.ds(0, mid)])])
        start_forward(1)
        oy(1).start()

    def second_orbitals():
        oy(0).wait_recv()

        @pl.when((layer == 1) | (layer == 2))
        def _():
            r_move(0, 0, slots.at[0, 0]).wait_recv()

        only((1,), [r_move(1, 0, slots.at[0, 0])])
        only((2,), [r_move(0, 0, slots.at[0, 0])])
        only((0, 1), [r_move(0, 1, opeer.at[pl.ds(0, mid)])])

    def third_orbitals():
        @pl.when((layer == 1) | (layer == 2))
        def _():
            r_move(0, 1, slots.at[0, 1]).wait_recv()

        only((1,), [r_move(1, 1, slots.at[0, 1])])

        @pl.when(layer == 2)
        def _():
            r_move(1, 0, slots.at[1, 0]).wait_recv()
            r_move(1, 0, slots.at[1, 0]).start()
            r_move(0, 1, slots.at[0, 1]).start()

        only((0,), [r_move(1, 0, okeep.at[pl.ds(mid, mid)])])

    def fourth_orbitals():
        oy(1).wait_recv()

        @pl.when(layer == 2)
        def _():
            r_move(1, 1, slots.at[1, 1]).wait_recv()
            r_move(1, 1, slots.at[1, 1]).start()

        only((0,), [r_move(1, 1, opeer.at[pl.ds(mid, mid)])])

    def out_move(c):
        return pltpu.make_async_copy(fresh.at[c], vectors.at[pl.ds(c * TILE, TILE)], out_sem.at[c])

    def collect(c):
        moves, stay = back(c, False)
        for move in moves:
            move.wait_recv()
        stay.wait()
        out_move(c).start()
        swap_into(fresh.at[c], ekeep.at[c], esend.at[c])
        ey(c, 1).start()
        ey(c, 0).start()

    def send_vectors(c, side):
        source = epeer if side else ekeep
        low, high = source.at[c, pl.ds(0, mid)], source.at[c, pl.ds(mid, mid)]
        if side:
            ey(c, 1).wait_recv()
        only((2, 3), [l_move(0, side, c, high)])
        if side:
            ey(c, 0).wait_recv()
        only((3,), [l_move(1, side, c, low)])

    def pass_first(c, side):
        @pl.when((layer == 1) | (layer == 2))
        def _():
            l_move(0, side, c, lslots.at[0, side, c]).wait_recv()

        only((2,), [l_move(1, side, c, lslots.at[0, side, c])])
        only((1,), [l_move(0, side, c, lslots.at[0, side, c])])

    def pass_second(c, side):
        @pl.when(layer == 1)
        def _():
            l_move(1, side, c, lslots.at[1, side, c]).wait_recv()
            l_move(1, side, c, lslots.at[1, side, c]).start()

    orbital_steps = (first_orbitals, second_orbitals, third_orbitals, fourth_orbitals)
    orbital_steps[0]()
    for move in picks:
        move.wait_recv()
    for step in range(chunks + 4):
        if step < chunks:
            moves, stay = forward(step)
            for move in moves:
                move.wait_recv()
            stay.wait()
            if step + 2 < chunks:
                start_forward(step + 2)
            if step >= 2:
                moves, _ = back(step - 2, True)
                for move in moves:
                    move.wait_send()

            @pl.loop(0, count)
            def _(j):
                solve_one(
                    [cubes.at[step, d, j] for d in range(groups)], partner, table, x_there, x_back,
                    y_there, y_back, z_both, [solved.at[step % 2, d, j] for d in range(groups)], work,
                )

            moves, stay = back(step, True)
            for move in moves:
                move.start()
            stay.start()
        if 0 <= step - 1 < chunks:
            collect(step - 1)
            send_vectors(step - 1, 0)
        if 0 <= step - 2 < chunks:
            send_vectors(step - 2, 1)
            pass_first(step - 2, 0)
        if 0 < step < 4:
            orbital_steps[step]()
        if 0 <= step - 3 < chunks:
            pass_first(step - 3, 1)
            pass_second(step - 3, 0)
        if 0 <= step - 4 < chunks:
            pass_second(step - 4, 1)

    sides = [(side, c) for side in range(2) for c in range(chunks)]

    @pl.when(layer == 0)
    def _():
        for side, c in sides:
            for slot in range(2):
                l_move(slot, side, c, lslots.at[slot, side, c]).wait_recv()

    @pl.when(layer == 2)
    def _():
        for side, c in sides:
            l_move(1, side, c, lslots.at[1, side, c]).wait_recv()

    @pl.when(layer == 1)
    def _():
        for side in range(2):
            r_move(1, side, slots.at[1, side]).wait_recv()

    @pl.when(layer == 3)
    def _():
        for side in range(2):
            for slot in range(2):
                r_move(slot, side, slots.at[slot, side]).wait_recv()

    def loads(p, at):
        moves = []
        for half in range(2):
            for side, source in enumerate((okeep, opeer)):
                moves.append(pltpu.make_async_copy(
                    source.at[half * mid + p], obuf.at[at, half, side], load_sem.at[at, len(moves)]))
        return moves

    def slot_loads(p, at):
        return [
            pltpu.make_async_copy(slots.at[slot, side, p], abuf.at[at, slot, side], load_sem.at[at, 4 + slot * 2 + side])
            for slot in range(2) for side in range(2)
        ]

    def start_loads(p, at):
        for move in loads(p, at):
            move.start()

        @pl.when(layer > 0)
        def _():
            for move in slot_loads(p, at):
                move.start()

    def across(a, b):
        return lax.dot_general(a, b, (((1,), (1,)), ((), ())), preferred_element_type=F32)

    parts[...] = jnp.zeros_like(parts)
    start_loads(0, 0)

    @pl.loop(0, mid)
    def _(p):
        at = lax.rem(p, 2)

        @pl.when(p + 1 < mid)
        def _():
            start_loads(p + 1, 1 - at)

        for move in loads(p, at):
            move.wait()
        low = jnp.concatenate([obuf[at, 0, side] for side in range(2)], axis=0)
        high = jnp.concatenate([obuf[at, 1, side] for side in range(2)], axis=0)

        def vector_rows(plane):
            return jnp.concatenate([ref[c, plane] for ref in (ekeep, epeer) for c in range(chunks)], axis=0)

        e_low, e_high = vector_rows(p), vector_rows(mid + p)
        parts[0] += across(low, e_low) + across(high, e_high)

        @pl.when(layer > 0)
        def _():
            for move in slot_loads(p, at):
                move.wait()
            first = jnp.concatenate([abuf[at, 0, side] for side in range(2)], axis=0)
            second = jnp.concatenate([abuf[at, 1, side] for side in range(2)], axis=0)
            parts[1] += across(first, e_low)
            parts[2] += across(second, jnp.where(layer == 1, e_high, e_low))

        @pl.when(layer < 3)
        def _():
            first = jnp.concatenate([lslots[0, side, c, p] for side, c in sides], axis=0)
            second = jnp.concatenate([lslots[1, side, c, p] for side, c in sides], axis=0)
            parts[3] += across(high, first)
            parts[4] += across(jnp.where(layer == 2, low, high), second)

    for move in steps + picks:
        move.wait_send()
    for half in range(2):
        oy(half).wait_send()
    for c in range(chunks):
        out_move(c).wait()
        for move in forward(c)[0]:
            move.wait_send()
        for half in range(2):
            ey(c, half).wait_send()
        if c >= chunks - 2:
            for move in back(c, True)[0]:
                move.wait_send()

    @pl.when(layer < 3)
    def _():
        for side in range(2):
            for slot in range(2):
                r_move(slot, side, slots.at[slot, side]).wait_send()

    @pl.when(layer > 0)
    def _():
        for side, c in sides:
            for slot in range(2):
                l_move(slot, side, c, lslots.at[slot, side, c]).wait_send()


def whole(orbitals, slab, okeep, osend, fixed):
    bands, rows, square = orbitals.shape
    groups = lax.axis_size("grid")
    chunks, count = bands // TILE, TILE // groups
    mid, width = rows // 2, square // 2
    anywhere = pl.BlockSpec(memory_space=pl.ANY)
    inside = pl.BlockSpec(memory_space=pltpu.VMEM)
    dma = pltpu.SemaphoreType.DMA
    sides = 2 * bands
    return pl.pallas_call(
        lambda *refs: whole_body(chunks, groups, *refs),
        in_specs=[anywhere, inside, anywhere, anywhere] + [inside] * len(fixed),
        out_specs=[anywhere, anywhere, anywhere, inside],
        out_shape=[
            jax.ShapeDtypeStruct(orbitals.shape, BF),
            jax.ShapeDtypeStruct((rows, bands, width), BF),
            jax.ShapeDtypeStruct((2, 2, mid, bands, width), BF),
            jax.ShapeDtypeStruct((5, sides, sides), F32),
        ],
        scratch_shapes=[
            pltpu.VMEM((chunks, groups, count, rows, square), BF),
            pltpu.VMEM((2, groups, count, rows, square), BF),
            pltpu.VMEM((chunks, TILE, rows, square), BF),
            pltpu.VMEM((NG, square), BF),
            pltpu.VMEM((5, rows, square), BF),
            pltpu.VMEM((chunks, rows, TILE, width), BF),
            pltpu.VMEM((chunks, rows, TILE, width), BF),
            pltpu.VMEM((chunks, rows, TILE, width), BF),
            pltpu.VMEM((2, 2, chunks, mid, TILE, width), BF),
            pltpu.VMEM((NG * HALF, LANES), F32),
            pltpu.VMEM((2, 2, 2, bands, width), BF),
            pltpu.VMEM((2, 2, 2, bands, width), BF),
            dma((2, 3)), dma((2, groups - 1)), dma((2, chunks, groups - 1)), dma((chunks,)),
            dma((2, chunks, groups - 1)), dma((chunks,)), dma((chunks,)),
            dma((2, 2)), dma((2, 2, 2)), dma((2, chunks, 2)), dma((2, 2, 2, chunks)), dma((2, 8)),
        ],
        compiler_params=pltpu.CompilerParams(
            collective_id=0, has_side_effects=True, vmem_limit_bytes=58 * 1024 * 1024
        ),
        cost_estimate=pl.CostEstimate(
            flops=count * chunks * 12 * NG * NG * NG * 256, bytes_accessed=16 * orbitals.size, transcendentals=0
        ),
    )(orbitals, slab, okeep, osend, *fixed)


def flip(value, axis, bits):
    return lax.ppermute(value, axis, [(i, i ^ bits) for i in range(lax.axis_size(axis))])


def summed_rows(parts):
    rank = lax.axis_index("band")
    layer, line = rank // 2, rank % 2
    half = parts.shape[1] // 2

    def plain(block):
        own_rows = jnp.where(line == 0, block, jnp.roll(block, half, 0))
        return jnp.where(line == 0, own_rows, jnp.roll(own_rows, half, 1))

    rows = []
    for other in range(lax.axis_size("band") // 2):
        total = jnp.where(layer == other, parts[0], 0.0)
        for at in range(4):
            blocks = [parts[i] if i > 2 else parts[i].T for i in HELD[at].get(other, ())]
            if blocks:
                total = jnp.where(layer == at, sum(blocks[1:], blocks[0]), total)
        rows.append(plain(total))
    rows = jnp.stack(rows) * (1.0 / NPTS)
    size = rows.shape[1]
    keep = lax.dynamic_slice_in_dim(rows, line * half, half, 1)
    give = lax.dynamic_slice_in_dim(rows, (1 - line) * half, half, 1)
    total = keep + flip(give, "band", 1)
    bit = 1
    while bit < lax.axis_size("grid"):
        total = total + flip(total, "grid", bit)
        bit *= 2
    return total


def reduce_blocks(parts):
    rank = lax.axis_index("band")
    layer = rank // 2
    layers = lax.axis_size("band") // 2
    rows = summed_rows(parts)
    half, size = rows.shape[1:]
    result = rows
    for bits in range(1, layers):
        there = layer ^ bits
        block = lax.dynamic_index_in_dim(rows, there, 0, keepdims=False)
        both = [flip(block, "band", 2 * bits), flip(block, "band", 2 * bits + 1)]
        line = rank % 2
        low = jnp.where(line == 0, both[0], both[1])
        high = jnp.where(line == 0, both[1], both[0])
        whole = jnp.concatenate([low, high], axis=0)
        mine = lax.dynamic_slice_in_dim(whole, line * half, half, 1).T
        result = lax.dynamic_update_index_in_dim(result, block + mine, there, 0)
    return result.transpose(1, 0, 2).reshape(half, layers * size)


def gram_body(left, right, out):
    @pl.when(pl.program_id(0) == 0)
    def _():
        out[...] = jnp.zeros_like(out)

    size = out.shape[0]
    a = left[:, 0].reshape(size, left.shape[3])
    b = right[:, 0].reshape(size, right.shape[3])
    out[...] += lax.dot_general(a, b, (((1,), (1,)), ((), ())), preferred_element_type=F32)


def gram_product(left, right):
    shares, planes, bands, points = left.shape
    size = shares * bands
    if bands % 16 or points % 128:
        return jnp.einsum("gxbk,hxck->gbhc", left, right, preferred_element_type=F32).reshape(size, size)
    block = pl.BlockSpec((shares, 1, bands, points), lambda i: (0, i, 0, 0))
    return pl.pallas_call(
        gram_body,
        grid=(planes,),
        in_specs=[block, block],
        out_specs=pl.BlockSpec((size, size), lambda i: (0, 0)),
        out_shape=jax.ShapeDtypeStruct((size, size), F32),
        compiler_params=pltpu.CompilerParams(vmem_limit_bytes=32 * 1024 * 1024),
        cost_estimate=pl.CostEstimate(
            flops=2 * size * size * planes * points, bytes_accessed=4 * left.size, transcendentals=0
        ),
    )(left, right)


def to_shares(array):
    shares = lax.axis_size("band")
    bands, planes, square = array.shape
    cut = array.reshape(bands, planes, shares, square // shares).transpose(2, 1, 0, 3)
    return lax.all_to_all(cut, "band", split_axis=0, concat_axis=0)


def spread(slab):
    bit = 1
    while bit < lax.axis_size("band"):
        slab = slab + flip(slab, "band", bit)
        bit *= 2
    groups = lax.axis_size("grid")
    return jnp.concatenate([slab] + [flip(slab, "grid", d) for d in range(1, groups)], axis=0)


def per_device(orbitals, picks):
    bands, planes, square = orbitals.shape
    groups, shares = lax.axis_size("grid"), lax.axis_size("band")
    me = lax.axis_index("grid")
    order = (me ^ jnp.arange(groups, dtype=jnp.int32))[:, None] * planes
    fixed = factors((order + jnp.arange(planes, dtype=jnp.int32)[None]).reshape(-1))
    target = picks[0]
    mine = lax.dynamic_index_in_dim(orbitals, target % bands, 0, keepdims=False)
    slab = jnp.where(lax.axis_index("band") == target // bands, mine, 0).astype(BF)

    if shares == 8 and bands == 4 * TILE and planes % 16 == 0:
        vectors, _, _, parts = whole(orbitals, slab, *order_orbitals(orbitals), fixed)
        return (vectors, reduce_blocks(parts))

    partner = spread(slab)
    count = bands // groups
    pieces = []
    for d in range(groups):
        part = lax.dynamic_slice_in_dim(orbitals, (me ^ d) * count, count, 0)
        pieces.append(flip(part, "grid", d) if d else part)
    solved = solve(pieces, partner, fixed)
    back = [flip(p, "grid", d) if d else p for d, p in enumerate(solved)]
    stacked = jnp.take(jnp.stack(back), me ^ jnp.arange(groups), axis=0)
    vectors = stacked.reshape(bands, planes, square)
    product = gram_product(to_shares(orbitals), to_shares(vectors))
    rows = lax.psum_scatter(product * (1.0 / NPTS), "band", scatter_dimension=0, tiled=True)
    return (vectors, lax.psum(rows, "grid"))


def solution(mesh):
    return jax.shard_map(
        per_device,
        mesh=mesh,
        in_specs=(P("band", "grid", None), P()),
        out_specs=(P("band", "grid", None), P("band", None)),
        check_vma=False,
    )
```

time: 722 us -> 442 us (0.61)
  waiting for transfers between devices: 406 us -> 20.8 us
  Pallas kernels: 97.4 us -> 373 us
  starting transfers between devices: 132 us -> 14.6 us
  local copies, waits for them, and re-layouts: 64.1 us -> 22.3 us
  other arithmetic: 17.3 us -> 8.44 us
    pallas_call x10 -> x2, Pallas kernels: 97.4 us -> 373 us  [the longest x1 370 us: whole(): pl.pallas_call(lambda *refs: whole_body(chunks, groups, *refs), in_specs=...]
    ppermute x49 -> x9, waiting for transfers between devices: 216 us -> 20.8 us  [flip(): lax.ppermute(value, axis, [(i, i ^ bits) for i in range(lax.axis_size(axi...]
    ppermute x40 -> x0, waiting for transfers between devices: 190 us -> none  [shift(): return [lax.ppermute(v, 'band', pairs) for v in values]]
    ppermute x40 -> x0, starting transfers between devices: 68.5 us -> none  [shift(): return [lax.ppermute(v, 'band', pairs) for v in values]]
    ppermute x49 -> x9, starting transfers between devices: 63 us -> 14.6 us  [flip(): lax.ppermute(value, axis, [(i, i ^ bits) for i in range(lax.axis_size(axi...]
    unnamed x180 -> x8, local copies, waits for them, and re-layouts: 49.5 us -> 15.3 us
    concatenate x2 -> x0, other arithmetic: 7.71 us -> none  [the longest x1 6.65 us: per_device(): jnp.concatenate(vectors, axis=0)]
  transfers between devices with their start and end apart: 89 -> 9, of which waited for: 40 -> 9; matrix products, arithmetic and copies ran while one was open for 3% -> 0% of each run, Pallas kernels for 11% -> 0%
where the time goes in v2:
time: 442 us; the launch traced here: 441 us
  Pallas kernels  373 us (84%)
  local copies, waits for them, and re-layouts  22.3 us (5%)
  waiting for transfers between devices  20.8 us (5%)
  starting transfers between devices  14.6 us (3%)
  other arithmetic  8.44 us (2%)
    pallas_call x1, Pallas kernels, whole(): pl.pallas_call(lambda *refs: whole_body(chunks, groups, *refs), in_specs=...  370 us
    ppermute x9, waiting for transfers between devices, flip(): lax.ppermute(value, axis, [(i, i ^ bits) for i in range(lax.axis_size(axi...  20.8 us
    unnamed x8, local copies, waits for them, and re-layouts  15.3 us
    ppermute x9, starting transfers between devices, flip(): lax.ppermute(value, axis, [(i, i ^ bits) for i in range(lax.axis_size(axi...  14.6 us
  transfers between devices with their start and end apart: 9, of which 9 were waited for; matrix products, arithmetic and copies ran while one was open for 0% of the time, Pallas kernels for 0%

profile of v2, /device:TPU:0, one launch (start us, length us, event | category | flops | bytes accessed | tf_op | source)
XLA Modules:
  0.0 441.0 jit_solution(7199190958964440321)
XLA Ops:
  1.3 0.1 sine_add_fusion.2
  1.5 0.1 iota_add_fusion
  1.5 0.1 add.243
  1.6 0.1 add.239
  1.7 0.1 copy.17
  1.8 0.6 gather_fusion
  2.4 0.1 reduce-precision_convert_fusion.4
  2.5 0.1 reduce-precision_convert_fusion.3
  2.7 0.7 copy.18.refs_5_
  3.4 0.1 mul.238
  3.5 0.3 reduce-precision_convert_fusion.1
  3.8 0.1 broadcast_multiply_fusion
  3.9 0.1 mul.249
  4.1 0.1 broadcast_add_fusion
  4.2 1.2 add.230
  5.4 1.1 add.231
  6.6 0.1 add.233
  6.7 3.4 copy-done
  10.0 3.0 shard_map.41
  13.1 2.0 copy-done.1
  15.1 2.0 copy-done.2
  17.0 1.6 select_bitcast_fusion.refs_1_
  18.6 0.7 pad_maximum_fusion.1.refs_6_
  19.3 0.7 fusion.1.refs_9_
  20.0 1.2 divide_select_fusion.refs_4_
  21.2 0.7 pad_maximum_fusion.2
  21.9 370.2 %shard_map.42 = (bf16[64,16,4096]{2,1,0:T(8,128)(2,1)}, bf16[16,64,2048]{2,1,0:T(8,128)(2,1)}, bf16[2,2,8,64,2048]{4,3,2,1,0:T(8,128)(2,1)}, f32[5,128,128]{2,1,0:T(8,128)}) custom-call(bf16[64,16,4096]{2,1,0:T(8,128)(2,1)} %refs_0_.1, bf16[16,4096]{1,0:T(8,128)(2,1)} %select_bitcast_fusion.refs_1_, bf16[16,64,2048]{2,1,0:T(8,128)(2,1)} %copy-done.1, ...), custom_call_target="tpu_custom_call" | custom-call | flops 12884901888 | bytes 67108864 | tf_op jit(solution)/shard_map/pallas_call | solution.py:519
  392.1 1.1 copy.19
  393.2 0.9 select_select_fusion.5
  394.2 0.1 fusion.53
  394.3 0.1 fusion.55
  394.5 0.1 slice_bitcast_fusion.1
  394.6 0.1 slice_bitcast_fusion.3
  394.7 0.1 fusion.9
  394.8 0.1 fusion.10
  394.9 1.0 fusion.4
  395.9 1.6 collective-permute-start
  397.5 4.0 collective-permute-done
  401.5 0.7 collective-permute-start.1
  402.3 1.0 collective-permute-done.1
  403.3 0.6 collective-permute-start.2
  403.9 5.2 %collective-permute-done.2 = f32[4,64,128]{2,1,0:T(8,128)S(1)} collective-permute-done((f32[4,64,128]{2,1,0:T(8,128)S(1)}, f32[4,64,128]{2,1,0:T(8,128)S(1)}, u32[]{:S(2)}, u32[]{:S(2)}) %collective-permute-start.2) | collective-permute-done | bytes 131104 | tf_op jit(solution)/shard_map/ppermute | solution.py:556
  409.2 3.0 collective-permute-start.4
  412.2 0.9 collective-permute-done.3
  413.1 1.3 collective-permute-done.4
  414.4 0.1 copy.24
  414.5 0.1 copy.22
  414.6 0.1 copy.23
  414.8 0.1 dynamic-slice_bitcast_fusion.1
  414.9 3.5 collective-permute-start.6
  418.5 1.3 collective-permute-done.5
  419.7 1.0 collective-permute-done.6
  420.7 0.1 copy.28
  420.8 0.1 copy.26
  420.9 0.1 copy.27
  421.0 0.1 dynamic-slice_bitcast_fusion
  421.1 0.1 copy.29
  421.2 4.2 collective-permute-start.7
  425.4 0.9 collective-permute-start.8
  426.2 1.9 collective-permute-done.7
  428.2 4.2 collective-permute-done.8
  432.4 0.1 fusion.28
  432.5 0.7 copy_bitcast_fusion
  433.1 7.9 %copy.39 = bf16[64,16,4096]{2,1,0:T(8,128)(2,1)} copy(bf16[64,16,4096]{2,1,0:T(8,128)(2,1)} %get-tuple-element.56) | data formatting | bytes 16777216
  (36 shorter events, 0.5 us)
Async XLA Ops:
  6.7 3.4 copy-start
  13.1 2.0 copy-start.1
  15.1 2.0 copy-start.2
  395.9 5.6 %collective-permute-start = (f32[4,64,128]{2,1,0:T(8,128)S(1)}, f32[4,64,128]{2,1,0:T(8,128)S(1)}, u32[]{:S(2)}, u32[]{:S(2)}) collective-permute-start(f32[4,64,128]{2,1,0:T(8,128)S(1)} %constant_dynamic-slice_fusion), channel_id=1, source_target_pairs={{0,4},{4,0},{8,12},{12,8},{16,20},{20,16},{24,28},{28,24},{1,5},{5... | collective-permute-start | bytes 393224 | tf_op jit(solution)/shard_map/ppermute | solution.py:556
  401.5 1.7 collective-permute-start.1
  403.3 5.8 %collective-permute-start.2 = (f32[4,64,128]{2,1,0:T(8,128)S(1)}, f32[4,64,128]{2,1,0:T(8,128)S(1)}, u32[]{:S(2)}, u32[]{:S(2)}) collective-permute-start(f32[4,64,128]{2,1,0:T(8,128)S(1)} %add.256), channel_id=1, source_target_pairs={{0,2},{1,3},{2,0},{3,1},{4,6},{5,7},{6,4},{7,5},{8,10},{9,11},{10,... | collective-permute-start | bytes 393224 | tf_op jit(solution)/shard_map/ppermute | solution.py:556
  409.1 4.0 collective-permute-start.3
  409.2 5.2 %collective-permute-start.4 = (f32[64,128]{1,0:T(8,128)S(1)}, f32[64,128]{1,0:T(8,128)S(1)}, u32[]{:S(2)}, u32[]{:S(2)}) collective-permute-start(f32[64,128]{1,0:T(8,128)S(1)} %dynamic-slice_bitcast_fusion.2), channel_id=1, source_target_pairs={{0,12},{4,8},{8,4},{12,0},{16,28},{20,24},{24,20},{28,16},{1,13},{... | collective-permute-start | bytes 98312 | tf_op jit(solution)/shard_map/ppermute | solution.py:556
  414.9 4.9 %collective-permute-start.5 = (f32[64,128]{1,0:T(8,128)S(1)}, f32[64,128]{1,0:T(8,128)S(1)}, u32[]{:S(2)}, u32[]{:S(2)}) collective-permute-start(f32[64,128]{1,0:T(8,128)S(1)} %get-tuple-element.20), channel_id=1, source_target_pairs={{0,16},{4,20},{8,24},{12,28},{16,0},{20,4},{24,8},{28,12},{1,17},{... | collective-permute-start | bytes 98312 | tf_op jit(solution)/shard_map/ppermute | solution.py:556
  414.9 5.8 %collective-permute-start.6 = (f32[64,128]{1,0:T(8,128)S(1)}, f32[64,128]{1,0:T(8,128)S(1)}, u32[]{:S(2)}, u32[]{:S(2)}) collective-permute-start(f32[64,128]{1,0:T(8,128)S(1)} %get-tuple-element.20), channel_id=1, source_target_pairs={{0,20},{4,16},{8,28},{12,24},{16,4},{20,0},{24,12},{28,8},{1,21},{... | collective-permute-start | bytes 98312 | tf_op jit(solution)/shard_map/ppermute | solution.py:556
  421.2 6.9 %collective-permute-start.7 = (f32[64,128]{0,1:T(8,128)S(1)}, f32[64,128]{0,1:T(8,128)S(1)}, u32[]{:S(2)}, u32[]{:S(2)}) collective-permute-start(f32[64,128]{0,1:T(8,128)S(1)} %copy.29), channel_id=1, source_target_pairs={{0,24},{4,28},{8,16},{12,20},{16,8},{20,12},{24,0},{28,4},{1,25},{... | collective-permute-start | bytes 98312 | tf_op jit(solution)/shard_map/ppermute | solution.py:556
  425.4 7.0 %collective-permute-start.8 = (f32[64,128]{0,1:T(8,128)S(1)}, f32[64,128]{0,1:T(8,128)S(1)}, u32[]{:S(2)}, u32[]{:S(2)}) collective-permute-start(f32[64,128]{0,1:T(8,128)S(1)} %copy.29), channel_id=1, source_target_pairs={{0,28},{4,24},{8,20},{12,16},{16,12},{20,8},{24,4},{28,0},{1,29},{... | collective-permute-start | bytes 98312 | tf_op jit(solution)/shard_map/ppermute | solution.py:556

commit v3 on v2

v3 whole, which is shorter than its diff:
```python
import math
import jax, jax.numpy as jnp
from jax import lax
from jax.experimental import pallas as pl
from jax.experimental.pallas import tpu as pltpu
from jax.sharding import PartitionSpec as P

NG = 64
NPTS = NG ** 3
KERNEL_SCALE = 128.0
LANES = 128
BF = jnp.bfloat16
F32 = jnp.float32
HALF = NG // 2
XW = 512
PLANES = 32
TILE = 16
SWAP = 256
LOW = 9
HELD = ({2: (3,), 3: (4,)}, {0: (1, 2), 2: (3,), 3: (4,)}, {1: (1,), 0: (2,), 3: (3, 4)}, {1: (1,), 0: (2,)})


def cas_matrix(length):
    products = (
        jnp.arange(length, dtype=jnp.int32)[:, None]
        * jnp.arange(length, dtype=jnp.int32)[None, :]
        % length
    )
    angles = products.astype(F32) * (2.0 * math.pi / length)
    return jnp.cos(angles) + jnp.sin(angles)


def halves(value):
    high = value.astype(BF)
    return high, (value - high.astype(F32)).astype(BF)


def matrix_halves(value):
    high = lax.reduce_precision(value, 8, 7)
    return high.astype(BF), (value - high).astype(BF)


def kernel_table():
    frequency = jnp.arange(NG, dtype=jnp.int32)
    folded = jnp.minimum(frequency, NG - frequency).astype(F32)
    square = folded * folded
    summed = square[:, None, None] + square[None, :, None] + square[None, None, :]
    table = jnp.where(summed > 0, KERNEL_SCALE / NPTS / jnp.maximum(summed, 1.0), 0.0)
    return table.reshape(NG // 4, 4, NG, NG).transpose(0, 2, 1, 3).reshape(NG // 4, NG, 4 * NG)


def row_factor(matrix):
    high, low = matrix_halves(matrix)
    return jnp.concatenate([high, high, low], axis=1)


def lane_factor(matrix):
    high, low = matrix_halves(jnp.kron(jnp.eye(2, dtype=F32), matrix))
    upper = jnp.concatenate([high, low], axis=1)
    lower = jnp.concatenate([high, jnp.zeros_like(low)], axis=1)
    return jnp.concatenate([upper, lower], axis=0)


def dot(a, b):
    return jnp.dot(a, b, preferred_element_type=F32)


def solve_one(ins, partner, table, x_there, x_back, y_there, y_back, z_both, outs, work):
    rows = NG // len(ins)

    def along_rows(factor, value):
        high, low = halves(value)
        return dot(factor[...], jnp.concatenate([high, low, high], axis=0))

    def along_lanes(value):
        high, low = halves(value)
        both = dot(jnp.concatenate([high, low], axis=1), z_both[...])
        return both[:, :LANES] + both[:, LANES:]

    @pl.loop(0, NG * NG // XW, unroll=4)
    def _(i):
        at = pl.ds(pl.multiple_of(i * XW, XW), XW)
        field = jnp.concatenate([ref[:, at].astype(F32) for ref in ins], axis=0)
        field = along_rows(x_there, field * partner[:, at].astype(F32))
        for tile in range(XW // LANES):
            work[pl.ds(i * (XW // LANES) + tile, NG, stride=HALF), :] = field[:, tile * LANES:(tile + 1) * LANES]

    @pl.loop(0, NG // PLANES, unroll=2)
    def _(i):
        left = lax.broadcasted_iota(jnp.int32, (HALF, LANES), 1) < NG
        base = i * PLANES * HALF
        parts = []
        for pair in range(PLANES // 2):
            a = work[pl.ds(base + pair * NG, HALF), :]
            b = work[pl.ds(base + pair * NG + HALF, HALF), :]
            parts.append(jnp.where(left, a, pltpu.roll(b, NG, 1)))
            parts.append(jnp.where(left, pltpu.roll(a, NG, 1), b))
        field = along_lanes(jnp.concatenate(parts, axis=0))
        done = []
        for quad in range(PLANES // 4):
            wide = jnp.concatenate(
                [field[quad * 128:quad * 128 + 64], field[quad * 128 + 64:quad * 128 + 128]], axis=1
            )
            wide = along_rows(y_there, wide) * table[i * (PLANES // 4) + quad]
            wide = along_rows(y_back, wide)
            done.append(wide[:, :LANES])
            done.append(wide[:, LANES:])
        field = along_lanes(jnp.concatenate(done, axis=0))
        for pair in range(PLANES // 2):
            u = field[pair * NG:pair * NG + HALF]
            v = field[pair * NG + HALF:pair * NG + NG]
            work[pl.ds(base + pair * NG, HALF), :] = jnp.where(left, u, pltpu.roll(v, NG, 1))
            work[pl.ds(base + pair * NG + HALF, HALF), :] = jnp.where(left, pltpu.roll(u, NG, 1), v)

    @pl.loop(0, NG * NG // XW, unroll=4)
    def _(i):
        at = pl.ds(pl.multiple_of(i * XW, XW), XW)
        field = jnp.concatenate(
            [work[pl.ds(i * (XW // LANES) + tile, NG, stride=HALF), :] for tile in range(XW // LANES)], axis=1
        )
        field = (-along_rows(x_back, field) * partner[:, at].astype(F32)).astype(BF)
        for index, ref in enumerate(outs):
            ref[:, at] = field[index * rows:(index + 1) * rows]


def solve_body(groups, *refs):
    ins, outs = refs[:groups], refs[groups + 7:2 * groups + 7]
    solve_one([ref.at[0] for ref in ins], *refs[groups:groups + 7], [ref.at[0] for ref in outs], refs[-1])


def factors(planes_at):
    matrix = cas_matrix(NG)
    by_plane = jnp.take(matrix, planes_at, axis=1)
    by_line = matrix.reshape(NG, HALF, 2).transpose(0, 2, 1).reshape(NG, NG)
    return (
        kernel_table(), row_factor(by_plane), row_factor(by_plane.T),
        row_factor(by_line), row_factor(by_line.T), lane_factor(matrix),
    )


def solve(pieces, partner, fixed):
    groups = len(pieces)
    count, rows, square = pieces[0].shape
    block = pl.BlockSpec((1, rows, square), lambda i: (i, 0, 0))
    whole = lambda array: pl.BlockSpec(array.shape, lambda i: (0,) * array.ndim)
    fixed = (partner,) + fixed
    return pl.pallas_call(
        lambda *refs: solve_body(groups, *refs),
        grid=(count,),
        in_specs=[block] * groups + [whole(a) for a in fixed],
        out_specs=[block] * groups,
        out_shape=[jax.ShapeDtypeStruct(p.shape, BF) for p in pieces],
        scratch_shapes=[pltpu.VMEM((NG * HALF, LANES), F32)],
        compiler_params=pltpu.CompilerParams(vmem_limit_bytes=32 * 1024 * 1024),
        cost_estimate=pl.CostEstimate(
            flops=count * 12 * NG * NG * NG * 256, bytes_accessed=4 * count * NPTS, transcendentals=0
        ),
    )(*pieces, *fixed)
def swap_into(held, keep, send):
    width = held.shape[2] // 2
    mine = lax.axis_index("band") % 2

    @pl.loop(0, width // SWAP)
    def _(i):
        put = pl.ds(pl.multiple_of(i * SWAP, SWAP), SWAP)
        for at, out in ((mine, keep), (1 - mine, send)):
            lanes = pl.ds(pl.multiple_of(at * width + i * SWAP, SWAP), SWAP)
            out[:, :, put] = jnp.swapaxes(held[:, :, lanes], 0, 1)


def order_orbitals(orbitals):
    bands, rows, square = orbitals.shape
    part = jax.ShapeDtypeStruct((rows, bands, square // 2), BF)
    spec = pl.BlockSpec((rows, TILE, square // 2), lambda i: (0, i, 0))
    return pl.pallas_call(
        swap_into,
        grid=(bands // TILE,),
        in_specs=[pl.BlockSpec((TILE, rows, square), lambda i: (i, 0, 0))],
        out_specs=[spec] * 2,
        out_shape=[part] * 2,
        compiler_params=pltpu.CompilerParams(vmem_limit_bytes=24 * 1024 * 1024),
        cost_estimate=pl.CostEstimate(flops=0, bytes_accessed=4 * orbitals.size, transcendentals=0),
    )(orbitals)


def whole_body(chunks, groups, *refs):
    (orb, slab, okeep, osend, table, x_there, x_back, y_there, y_back, z_both,
     vectors, opeer, slots, gram,
     cubes, solved, fresh, partner, hyper, ekeep, epeer, esend, lslots, work, obuf, abuf,
     parts, turned, sums, come, last,
     hyper_sem, pick_sem, fwd_sem, own_sem, back_sem, stay_sem, out_sem,
     oy_sem, r_sem, ey_sem, l_sem, load_sem, sum_sem, last_sem) = refs
    rows = cubes.shape[2]
    bands = cubes.shape[0]
    count = TILE // groups
    ring = solved.shape[0]
    low = lslots.shape[3]
    high = rows - low
    band, me = lax.axis_index("band"), lax.axis_index("grid")
    layer, line = band // 2, band % 2
    peer = band ^ 1
    up, down = lax.rem(band + 2, 8), lax.rem(band + 6, 8)

    def remote(source, target, sems, axis, index):
        return pltpu.make_async_remote_copy(
            src_ref=source, dst_ref=target, send_sem=sems[0], recv_sem=sems[1],
            device_id={axis: index}, device_id_type=pl.DeviceIdType.MESH,
        )

    def sems(array, *at):
        return array.at[(0,) + at], array.at[(1,) + at]

    def start(moves):
        for move in moves:
            move.start()

    def arrive(moves):
        for move in moves:
            move.wait_recv()

    def leave(moves):
        for move in moves:
            move.wait_send()

    def on(*layers):
        hit = layer == layers[0]
        for other in layers[1:]:
            hit = hit | (layer == other)
        return pl.when(hit)

    barrier = pltpu.get_barrier_semaphore()
    for bits in range(1, 8):
        pl.semaphore_signal(barrier, inc=1, device_id={"band": band ^ bits}, device_id_type=pl.DeviceIdType.MESH)
    for d in range(1, groups):
        pl.semaphore_signal(barrier, inc=1, device_id={"grid": me ^ d}, device_id_type=pl.DeviceIdType.MESH)
    pl.semaphore_wait(barrier, 6 + groups)

    def forward(t):
        def at(d):
            return orb.at[(t // count) * TILE + (me ^ d) * count + lax.rem(t, count)]
        moves = [remote(at(d), cubes.at[t, d], sems(fwd_sem, t, d - 1), "grid", me ^ d) for d in range(1, groups)]
        return moves, pltpu.make_async_copy(at(0), cubes.at[t, 0], own_sem.at[t])

    def start_forward(t):
        moves, stay = forward(t)
        start(moves)
        stay.start()

    def back(t, mine):
        def at(d):
            return fresh.at[t // count, (me if mine else me ^ d) * count + lax.rem(t, count)]
        source = lax.rem(t, ring)
        moves = [remote(solved.at[source, d], at(d), sems(back_sem, t, d - 1), "grid", me ^ d) for d in range(1, groups)]
        own = fresh.at[t // count, me * count + lax.rem(t, count)]
        return moves, pltpu.make_async_copy(solved.at[source, 0], own, stay_sem.at[t])

    low_cut = ((0, (low + 1) // 2), ((low + 1) // 2, low // 2))
    high_cut = ((0, (high + 1) // 2), ((high + 1) // 2, high // 2))

    def r_move(slot, side, q, source, first=0, cut=low_cut):
        at, size = cut[q]
        return remote(
            source.at[pl.ds(first + at, size)], slots.at[slot, side, pl.ds(at, size)],
            sems(r_sem, slot, side, q), "band", up,
        )

    def r_pass(slot, side, q, onto):
        return r_move(onto, side, q, slots.at[slot, side])

    def r_here(slot, side, q, cut=low_cut):
        return r_move(slot, side, q, slots.at[slot, side], 0, cut)

    def l_move(slot, side, c, source, first, size):
        return remote(
            source.at[pl.ds(first, size)], lslots.at[slot, side, c, pl.ds(0, size)],
            sems(l_sem, slot, side, c), "band", down,
        )

    def l_here(slot, side, c, size=high):
        return l_move(slot, side, c, lslots.at[slot, side, c], 0, size)

    def oy(half):
        at = pl.ds(low, high) if half else pl.ds(0, low)
        return remote(osend.at[at], opeer.at[at], sems(oy_sem, half), "band", peer)

    def ey(c, half):
        at = pl.ds(low, high) if half else pl.ds(0, low)
        return remote(esend.at[c, at], epeer.at[c, at], sems(ey_sem, c, half), "band", peer)

    steps = [remote(slab, hyper.at[0], sems(hyper_sem, 0), "band", band ^ 1)]
    steps.append(remote(hyper.at[3], hyper.at[1], sems(hyper_sem, 1), "band", band ^ 2))
    steps.append(remote(hyper.at[4], hyper.at[2], sems(hyper_sem, 2), "band", band ^ 4))
    mine = pl.ds(0, rows)
    picks = [
        remote(partner.at[mine], partner.at[pl.ds(d * rows, rows)], sems(pick_sem, d - 1), "grid", me ^ d)
        for d in range(1, groups)
    ]
    steps[0].start()
    start_forward(0)
    start_forward(1)
    steps[0].wait_recv()
    hyper[3] = slab[...] + hyper[0]
    steps[1].start()
    oy(0).start()
    steps[1].wait_recv()
    hyper[4] = hyper[3] + hyper[1]
    steps[2].start()

    @on(0, 1)
    def _():
        start([r_move(0, 0, q, okeep) for q in range(2)])

    steps[2].wait_recv()
    partner[mine] = hyper[4] + hyper[2]
    start(picks)
    start_forward(2)
    start_forward(3)
    oy(1).start()

    def own_orbitals(q):
        @on(1)
        def _():
            r_here(0, 0, q).wait_recv()
            r_pass(0, 0, q, 1).start()

        @on(2)
        def _():
            r_here(0, 0, q).wait_recv()
            r_pass(0, 0, q, 0).start()

        @on(0)
        def _():
            r_move(1, 0, q, okeep, low, high_cut).start()

    def own_orbitals_on(q):
        @on(2)
        def _():
            r_here(1, 0, q).wait_recv()
            r_pass(1, 0, q, 1).start()

        if q == 0:
            oy(0).wait_recv()

            @on(0, 1)
            def _():
                start([r_move(0, 1, part, opeer) for part in range(2)])

    def peer_orbitals(q):
        if q == 0:
            oy(1).wait_recv()

        @on(1)
        def _():
            r_here(0, 1, q).wait_recv()
            r_pass(0, 1, q, 1).start()

        @on(2)
        def _():
            r_here(0, 1, q).wait_recv()
            r_pass(0, 1, q, 0).start()

        @on(0)
        def _():
            r_move(1, 1, q, opeer, low, high_cut).start()

    def peer_orbitals_on(q):
        @on(2)
        def _():
            r_here(1, 1, q).wait_recv()
            r_pass(1, 1, q, 1).start()

    def out_move(c):
        return pltpu.make_async_copy(fresh.at[c], vectors.at[pl.ds(c * TILE, TILE)], out_sem.at[c])

    def collect(c):
        for j in range(count):
            moves, stay = back(c * count + j, False)
            arrive(moves)
            stay.wait()
        out_move(c).start()
        swap_into(fresh.at[c], ekeep.at[c], esend.at[c])
        ey(c, 1).start()
        send_vectors(c, 0)
        ey(c, 0).start()

    def send_vectors(c, side):
        source = (epeer if side else ekeep).at[c]
        if side:
            ey(c, 1).wait_recv()

        @on(2, 3)
        def _():
            l_move(0, side, c, source, low, high).start()

        if side:
            ey(c, 0).wait_recv()

        @on(3)
        def _():
            l_move(1, side, c, source, 0, low).start()

    def pass_first(c, side):
        @on(2)
        def _():
            l_here(0, side, c).wait_recv()
            l_move(1, side, c, lslots.at[0, side, c], 0, high).start()

        @on(1)
        def _():
            l_here(0, side, c).wait_recv()
            l_move(0, side, c, lslots.at[0, side, c], 0, high).start()

    def pass_second(c, side):
        @on(1)
        def _():
            l_here(1, side, c).wait_recv()
            l_move(1, side, c, lslots.at[1, side, c], 0, high).start()

    arrive(picks)
    after = {
        0: [(own_orbitals, 0)],
        3: [(own_orbitals, 1)],
        4: [(own_orbitals_on, 0), (collect, 0)],
        5: [(pass_first, 0, 0)],
        6: [(own_orbitals_on, 1), (send_vectors, 0, 1), (pass_second, 0, 0)],
        7: [(pass_first, 0, 1)],
        8: [(peer_orbitals, 0), (pass_second, 0, 1), (collect, 1)],
        9: [(pass_first, 1, 0)],
        10: [(peer_orbitals, 1), (send_vectors, 1, 1), (pass_second, 1, 0)],
        11: [(pass_first, 1, 1)],
        12: [(peer_orbitals_on, 0), (pass_second, 1, 1), (collect, 2)],
        13: [(pass_first, 2, 0)],
        14: [(peer_orbitals_on, 1), (send_vectors, 2, 1), (pass_second, 2, 0)],
        15: [(pass_first, 2, 1)],
    }

    @pl.loop(0, bands)
    def _(t):
        moves, stay = forward(t)
        arrive(moves)
        stay.wait()

        @pl.when(t >= ring)
        def _():
            leave(back(t - ring, True)[0])

        at = lax.rem(t, ring)
        solve_one(
            [cubes.at[t, d] for d in range(groups)], partner, table, x_there, x_back,
            y_there, y_back, z_both, [solved.at[at, d] for d in range(groups)], work,
        )
        moves, stay = back(t, True)
        start(moves)
        stay.start()

        @pl.when(t + count < bands)
        def _():
            start_forward(t + count)

        for slot, events in after.items():
            @pl.when(t == slot)
            def _():
                for event in events:
                    event[0](*event[1:])

    for event in (
        (pass_second, 2, 1), (collect, 3), (pass_first, 3, 0), (send_vectors, 3, 1),
        (pass_second, 3, 0), (pass_first, 3, 1), (pass_second, 3, 1),
    ):
        event[0](*event[1:])

    sides = [(side, c) for side in range(2) for c in range(chunks)]

    @on(0)
    def _():
        for side, c in sides:
            arrive([l_here(slot, side, c) for slot in range(2)])

    @on(2)
    def _():
        for side, c in sides:
            l_here(1, side, c, low).wait_recv()

    @on(1)
    def _():
        for side in range(2):
            arrive([r_here(1, side, q, high_cut) for q in range(2)])

    @on(3)
    def _():
        for side in range(2):
            for slot in range(2):
                arrive([r_here(slot, side, q) for q in range(2)])

    def loads(p, at):
        return [
            pltpu.make_async_copy(source.at[p], obuf.at[at, side], load_sem.at[at, side])
            for side, source in enumerate((okeep, opeer))
        ]

    def slot_loads(slot, p, at):
        return [
            pltpu.make_async_copy(slots.at[slot, side, p], abuf.at[at, slot, side], load_sem.at[at, 2 + slot * 2 + side])
            for side in range(2)
        ]

    def with_slots(p, at, act):
        @pl.when((layer > 0) & (p < low))
        def _():
            act(0, slot_loads(0, p, at))

        @pl.when((layer > 1) & (p < low))
        def _():
            act(1, slot_loads(1, p, at))

        @pl.when((layer == 1) & (p >= low))
        def _():
            act(1, slot_loads(1, p - low, at))

    def start_loads(p, at):
        start(loads(p, at))
        with_slots(p, at, lambda slot, moves: start(moves))

    def across(a, b):
        return lax.dot_general(a, b, (((1,), (1,)), ((), ())), preferred_element_type=F32)

    parts[...] = jnp.zeros_like(parts)
    start_loads(0, 0)

    @pl.loop(0, rows)
    def _(p):
        at = lax.rem(p, 2)

        @pl.when(p + 1 < rows)
        def _():
            start_loads(p + 1, 1 - at)

        for move in loads(p, at):
            move.wait()
        here = jnp.concatenate([obuf[at, side] for side in range(2)], axis=0)
        there = jnp.concatenate([ref[c, p] for ref in (ekeep, epeer) for c in range(chunks)], axis=0)
        parts[0] += across(here, there)

        def add(slot, moves):
            for move in moves:
                move.wait()
            parts[1 + slot] += across(jnp.concatenate([abuf[at, slot, side] for side in range(2)], axis=0), there)

        with_slots(p, at, add)

        def moved(slot, plane):
            parts[3 + slot] += across(here, jnp.concatenate([lslots[slot, side, c, plane] for side, c in sides], axis=0))

        @pl.when((layer < 3) & (p >= low))
        def _():
            moved(0, p - low)

        @pl.when((layer < 2) & (p >= low))
        def _():
            moved(1, p - low)

        @pl.when((layer == 2) & (p < low))
        def _():
            moved(1, p)

    size = parts.shape[1]
    half = size // 2
    for at in range(chunks):
        @on(at)
        def _():
            for other in range(chunks):
                if other == at:
                    turned[other] = parts[0]
                else:
                    found = [parts[i] if i > 2 else parts[i].T for i in HELD[at].get(other, ())]
                    turned[other] = sum(found[1:], found[0]) if found else jnp.zeros((size, size), F32)
    for other in range(chunks):
        block = turned[other] * (1.0 / NPTS)
        block = jnp.where(line == 1, pltpu.roll(block, half, 1), block)
        sums[0, other] = block[half:]
        sums[1, other] = block[:half]
    totals = [
        remote(sums.at[0], come.at[0], sems(sum_sem, 0), "band", peer),
        remote(sums.at[2], come.at[1], sems(sum_sem, 1), "grid", me ^ 1),
        remote(sums.at[3], come.at[2], sems(sum_sem, 2), "grid", me ^ 2),
    ]
    for i, move in enumerate(totals):
        move.start()
        move.wait_recv()
        sums[2 + i] = sums[1 + i] + come[i]
    swaps = []
    for bits in range(1, chunks):
        block = sums.at[4, layer ^ bits]
        for turn in range(2):
            swaps.append((remote(
                block, last.at[bits - 1, line], sems(last_sem, bits - 1, turn), "band", band ^ (2 * bits + turn)
            ), remote(
                block, last.at[bits - 1, line ^ turn], sems(last_sem, bits - 1, turn), "band", band ^ (2 * bits + turn)
            )))
    for move, _ in swaps:
        move.start()
    gram[:, pl.ds(pl.multiple_of(layer * size, size), size)] = sums[4, layer]
    for _, move in swaps:
        move.wait_recv()
    for bits in range(1, chunks):
        whole_block = jnp.concatenate([last[bits - 1, 0], last[bits - 1, 1]], axis=0).T
        mine_block = jnp.where(line == 0, whole_block[:half], whole_block[half:])
        there = layer ^ bits
        gram[:, pl.ds(pl.multiple_of(there * size, size), size)] = sums[4, there] + mine_block

    leave(steps + picks + totals + [move for move, _ in swaps] + [oy(half) for half in range(2)])

    @pl.loop(0, bands)
    def _(t):
        leave(forward(t)[0])

        @pl.when(t >= bands - ring)
        def _():
            leave(back(t, True)[0])

    for c in range(chunks):
        out_move(c).wait()
        leave([ey(c, half) for half in range(2)])

    @on(0)
    def _():
        for side in range(2):
            leave([r_here(0, side, q) for q in range(2)] + [r_here(1, side, q, high_cut) for q in range(2)])

    @on(1, 2)
    def _():
        for side in range(2):
            leave([r_here(slot, side, q) for slot in range(2) for q in range(2)])

    @on(1, 2, 3)
    def _():
        for side, c in sides:
            l_here(0, side, c).wait_send()

    @on(1, 2)
    def _():
        for side, c in sides:
            l_here(1, side, c).wait_send()

    @on(3)
    def _():
        for side, c in sides:
            l_here(1, side, c, low).wait_send()


def whole(orbitals, slab, okeep, osend, fixed):
    bands, rows, square = orbitals.shape
    groups = lax.axis_size("grid")
    chunks, count = bands // TILE, TILE // groups
    low, width = LOW * rows // 16, square // 2
    ring = min(8, bands // groups)
    anywhere = pl.BlockSpec(memory_space=pl.ANY)
    inside = pl.BlockSpec(memory_space=pltpu.VMEM)
    dma = pltpu.SemaphoreType.DMA
    size = 2 * bands
    solves = bands // groups
    return pl.pallas_call(
        lambda *refs: whole_body(chunks, groups, *refs),
        in_specs=[anywhere, inside, anywhere, anywhere] + [inside] * len(fixed),
        out_specs=[anywhere, anywhere, anywhere, inside],
        out_shape=[
            jax.ShapeDtypeStruct(orbitals.shape, BF),
            jax.ShapeDtypeStruct((rows, bands, width), BF),
            jax.ShapeDtypeStruct((2, 2, low, bands, width), BF),
            jax.ShapeDtypeStruct((bands, 4 * size), F32),
        ],
        scratch_shapes=[
            pltpu.VMEM((solves, groups, rows, square), BF),
            pltpu.VMEM((ring, groups, rows, square), BF),
            pltpu.VMEM((chunks, TILE, rows, square), BF),
            pltpu.VMEM((NG, square), BF),
            pltpu.VMEM((5, rows, square), BF),
            pltpu.VMEM((chunks, rows, TILE, width), BF),
            pltpu.VMEM((chunks, rows, TILE, width), BF),
            pltpu.VMEM((chunks, rows, TILE, width), BF),
            pltpu.VMEM((2, 2, chunks, low, TILE, width), BF),
            pltpu.VMEM((NG * HALF, LANES), F32),
            pltpu.VMEM((2, 2, bands, width), BF),
            pltpu.VMEM((2, 2, 2, bands, width), BF),
            pltpu.VMEM((5, size, size), F32),
            pltpu.VMEM((4, size, size), F32),
            pltpu.VMEM((5, 4, bands, size), F32),
            pltpu.VMEM((3, 4, bands, size), F32),
            pltpu.VMEM((3, 2, bands, size), F32),
            dma((2, 3)), dma((2, groups - 1)), dma((2, solves, groups - 1)), dma((solves,)),
            dma((2, solves, groups - 1)), dma((solves,)), dma((chunks,)),
            dma((2, 2)), dma((2, 2, 2, 2)), dma((2, chunks, 2)), dma((2, 2, 2, chunks)), dma((2, 6)),
            dma((2, 3)), dma((2, 3, 2)),
        ],
        compiler_params=pltpu.CompilerParams(
            collective_id=0, has_side_effects=True, vmem_limit_bytes=60 * 1024 * 1024
        ),
        cost_estimate=pl.CostEstimate(
            flops=solves * 12 * NG * NG * NG * 256, bytes_accessed=16 * orbitals.size, transcendentals=0
        ),
    )(orbitals, slab, okeep, osend, *fixed)


def flip(value, axis, bits):
    return lax.ppermute(value, axis, [(i, i ^ bits) for i in range(lax.axis_size(axis))])


def gram_body(left, right, out):
    @pl.when(pl.program_id(0) == 0)
    def _():
        out[...] = jnp.zeros_like(out)

    size = out.shape[0]
    a = left[:, 0].reshape(size, left.shape[3])
    b = right[:, 0].reshape(size, right.shape[3])
    out[...] += lax.dot_general(a, b, (((1,), (1,)), ((), ())), preferred_element_type=F32)


def gram_product(left, right):
    shares, planes, bands, points = left.shape
    size = shares * bands
    if bands % 16 or points % 128:
        return jnp.einsum("gxbk,hxck->gbhc", left, right, preferred_element_type=F32).reshape(size, size)
    block = pl.BlockSpec((shares, 1, bands, points), lambda i: (0, i, 0, 0))
    return pl.pallas_call(
        gram_body,
        grid=(planes,),
        in_specs=[block, block],
        out_specs=pl.BlockSpec((size, size), lambda i: (0, 0)),
        out_shape=jax.ShapeDtypeStruct((size, size), F32),
        compiler_params=pltpu.CompilerParams(vmem_limit_bytes=32 * 1024 * 1024),
        cost_estimate=pl.CostEstimate(
            flops=2 * size * size * planes * points, bytes_accessed=4 * left.size, transcendentals=0
        ),
    )(left, right)


def to_shares(array):
    shares = lax.axis_size("band")
    bands, planes, square = array.shape
    cut = array.reshape(bands, planes, shares, square // shares).transpose(2, 1, 0, 3)
    return lax.all_to_all(cut, "band", split_axis=0, concat_axis=0)


def spread(slab):
    bit = 1
    while bit < lax.axis_size("band"):
        slab = slab + flip(slab, "band", bit)
        bit *= 2
    groups = lax.axis_size("grid")
    return jnp.concatenate([slab] + [flip(slab, "grid", d) for d in range(1, groups)], axis=0)


def per_device(orbitals, picks):
    bands, planes, square = orbitals.shape
    groups, shares = lax.axis_size("grid"), lax.axis_size("band")
    me = lax.axis_index("grid")
    order = (me ^ jnp.arange(groups, dtype=jnp.int32))[:, None] * planes
    fixed = factors((order + jnp.arange(planes, dtype=jnp.int32)[None]).reshape(-1))
    target = picks[0]
    mine = lax.dynamic_index_in_dim(orbitals, target % bands, 0, keepdims=False)
    slab = jnp.where(lax.axis_index("band") == target // bands, mine, 0).astype(BF)

    if shares == 8 and groups == 4 and bands == 4 * TILE and planes == 16:
        vectors, _, _, gram = whole(orbitals, slab, *order_orbitals(orbitals), fixed)
        return (vectors, gram)

    partner = spread(slab)
    count = bands // groups
    pieces = []
    for d in range(groups):
        part = lax.dynamic_slice_in_dim(orbitals, (me ^ d) * count, count, 0)
        pieces.append(flip(part, "grid", d) if d else part)
    solved = solve(pieces, partner, fixed)
    back = [flip(p, "grid", d) if d else p for d, p in enumerate(solved)]
    stacked = jnp.take(jnp.stack(back), me ^ jnp.arange(groups), axis=0)
    vectors = stacked.reshape(bands, planes, square)
    product = gram_product(to_shares(orbitals), to_shares(vectors))
    rows = lax.psum_scatter(product * (1.0 / NPTS), "band", scatter_dimension=0, tiled=True)
    return (vectors, lax.psum(rows, "grid"))


def solution(mesh):
    return jax.shard_map(
        per_device,
        mesh=mesh,
        in_specs=(P("band", "grid", None), P()),
        out_specs=(P("band", "grid", None), P("band", None)),
        check_vma=False,
    )
```

time: 442 us -> 359 us (0.81)
  Pallas kernels: 373 us -> 331 us
  waiting for transfers between devices: 20.8 us -> 0 us
  starting transfers between devices: 14.6 us -> 0 us
    pallas_call x1, Pallas kernels: 370 us -> 328 us  [whole(): pl.pallas_call(lambda *refs: whole_body(chunks, groups, *refs), in_specs=...]
    ppermute x9 -> x0, waiting for transfers between devices: 20.8 us -> none  [flip(): lax.ppermute(value, axis, [(i, i ^ bits) for i in range(lax.axis_size(axi...]
    ppermute x9 -> x0, starting transfers between devices: 14.6 us -> none  [flip(): lax.ppermute(value, axis, [(i, i ^ bits) for i in range(lax.axis_size(axi...]
    unnamed x8 -> x10, local copies, waits for them, and re-layouts: 15.3 us -> 16 us
  transfers between devices with their start and end apart: 9 -> 0, of which waited for: 9 -> 0; matrix products, arithmetic and copies ran while one was open for 0% -> 0% of each run, Pallas kernels for 0% -> 0%
where the time goes in v3:
time: 359 us; the launch traced here: 358 us
  Pallas kernels  331 us (92%)
  local copies, waits for them, and re-layouts  20.2 us (6%)
  other arithmetic  5.82 us (2%)
    pallas_call x1, Pallas kernels, whole(): pl.pallas_call(lambda *refs: whole_body(chunks, groups, *refs), in_specs=...  328 us
    unnamed x10, local copies, waits for them, and re-layouts  16 us

profile of v3, /device:TPU:0, one launch (start us, length us, event | category | flops | bytes accessed | tf_op | source)
XLA Modules:
  0.0 358.3 jit_solution(16901192852283146030)
XLA Ops:
  1.3 0.1 mul.223
  1.4 0.1 iota_add_fusion
  1.5 0.1 add.186
  1.6 0.1 add.182
  1.7 0.1 add.176
  1.8 0.1 sine_add_fusion.2
  2.0 0.1 copy.4
  2.0 0.6 gather_fusion
  2.6 0.1 reduce-precision_convert_fusion.3
  2.7 0.1 reduce-precision_convert_fusion.4
  2.8 0.7 pad_maximum_fusion.1.refs_6_
  3.5 0.7 copy.5.refs_5_
  4.2 0.3 reduce-precision_convert_fusion.1
  4.5 0.7 pad_maximum_fusion.2
  5.3 0.1 broadcast_multiply_fusion
  5.4 0.1 mul.234
  5.5 0.7 fusion.1.refs_9_
  6.2 1.6 select_bitcast_fusion.refs_1_
  7.8 0.1 broadcast_add_fusion
  7.9 1.2 add.173
  9.1 1.1 add.174
  10.3 1.2 divide_select_fusion.refs_4_
  11.4 0.0 copy-start
  11.4 3.4 copy-done
  14.8 3.0 shard_map.41
  17.8 0.0 copy-start.1
  17.9 2.0 copy-done.1
  19.9 0.0 copy-start.2
  19.9 2.0 copy-done.2
  21.8 327.8 %shard_map.42 = (bf16[64,16,4096]{2,1,0:T(8,128)(2,1)}, bf16[16,64,2048]{2,1,0:T(8,128)(2,1)}, bf16[2,2,9,64,2048]{4,3,2,1,0:T(8,128)(2,1)}, f32[64,512]{1,0:T(8,128)}) custom-call(bf16[64,16,4096]{2,1,0:T(8,128)(2,1)} %refs_0_.1, bf16[16,4096]{1,0:T(8,128)(2,1)} %select_bitcast_fusion.refs_1_, bf16[16,64,2048]{2,1,0:T(8,128)(2,1)} %copy-done.1, ...), custom_call_target="tpu_custom_call" | custom-call | flops 12884901888 | bytes 67108864 | tf_op jit(solution)/shard_map/pallas_call | solution.py:662
  349.7 0.0 copy-start.3
  349.7 7.9 %copy.9 = bf16[64,16,4096]{2,1,0:T(8,128)(2,1)} copy(bf16[64,16,4096]{2,1,0:T(8,128)(2,1)} %get-tuple-element.24) | data formatting | bytes 16777216
  357.6 0.0 copy-done.3
  357.6 0.7 copy.10
  (11 shorter events, 0.1 us)
Async XLA Ops:
  11.4 3.4 copy-start
  17.8 2.0 copy-start.1
  19.9 2.0 copy-start.2
  349.7 7.9 %copy-start.3 = (f32[64,512]{1,0:T(8,128)S(1)}, f32[64,512]{1,0:T(8,128)}, u32[]{:S(2)}) copy-start(f32[64,512]{1,0:T(8,128)} %get-tuple-element.25) | copy-start | bytes 393220

commit v4 on v3

--- a/solution.py
+++ b/solution.py
@@ -1,5 +1,8 @@
 import math
-import jax, jax.numpy as jnp
+import jax
+import jax.numpy as jnp
+import ml_dtypes
+import numpy as np
 from jax import lax
 from jax.experimental import pallas as pl
 from jax.experimental.pallas import tpu as pltpu
@@ -9,7 +12,7 @@
 NPTS = NG ** 3
 KERNEL_SCALE = 128.0
 LANES = 128
-BF = jnp.bfloat16
+BF = ml_dtypes.bfloat16
 F32 = jnp.float32
 HALF = NG // 2
 XW = 512
@@ -17,17 +20,14 @@
 TILE = 16
 SWAP = 256
 LOW = 9
-HELD = ({2: (3,), 3: (4,)}, {0: (1, 2), 2: (3,), 3: (4,)}, {1: (1,), 0: (2,), 3: (3, 4)}, {1: (1,), 0: (2,)})
+MORE = 3
+HELD = ({2: (3,), 3: (4,)}, {0: (1, 2), 2: (3,), 3: (4,)}, {1: (1,), 0: (2,), 3: (3, 4)}, {1: (1,), 0: (2,), 2: (5,)})
 
 
 def cas_matrix(length):
-    products = (
-        jnp.arange(length, dtype=jnp.int32)[:, None]
-        * jnp.arange(length, dtype=jnp.int32)[None, :]
-        % length
-    )
-    angles = products.astype(F32) * (2.0 * math.pi / length)
-    return jnp.cos(angles) + jnp.sin(angles)
+    products = np.arange(length)[:, None] * np.arange(length)[None, :] % length
+    angles = products * (2.0 * math.pi / length)
+    return (np.cos(angles) + np.sin(angles)).astype(np.float32)
 
 
 def halves(value):
@@ -35,30 +35,25 @@
     return high, (value - high.astype(F32)).astype(BF)
 
 
-def matrix_halves(value):
-    high = lax.reduce_precision(value, 8, 7)
-    return high.astype(BF), (value - high).astype(BF)
-
-
 def kernel_table():
-    frequency = jnp.arange(NG, dtype=jnp.int32)
-    folded = jnp.minimum(frequency, NG - frequency).astype(F32)
+    frequency = np.arange(NG)
+    folded = np.minimum(frequency, NG - frequency)
     square = folded * folded
     summed = square[:, None, None] + square[None, :, None] + square[None, None, :]
-    table = jnp.where(summed > 0, KERNEL_SCALE / NPTS / jnp.maximum(summed, 1.0), 0.0)
+    table = np.where(summed > 0, KERNEL_SCALE / NPTS / np.maximum(summed, 1), 0.0).astype(np.float32)
     return table.reshape(NG // 4, 4, NG, NG).transpose(0, 2, 1, 3).reshape(NG // 4, NG, 4 * NG)
 
 
 def row_factor(matrix):
-    high, low = matrix_halves(matrix)
-    return jnp.concatenate([high, high, low], axis=1)
+    high, low = halves(matrix)
+    return np.concatenate([high, high, low], axis=1)
 
 
 def lane_factor(matrix):
-    high, low = matrix_halves(jnp.kron(jnp.eye(2, dtype=F32), matrix))
-    upper = jnp.concatenate([high, low], axis=1)
-    lower = jnp.concatenate([high, jnp.zeros_like(low)], axis=1)
-    return jnp.concatenate([upper, lower], axis=0)
+    high, low = halves(np.kron(np.eye(2, dtype=np.float32), matrix))
+    upper = np.concatenate([high, low], axis=1)
+    lower = np.concatenate([high, np.zeros_like(low)], axis=1)
+    return np.concatenate([upper, lower], axis=0)
 
 
 def dot(a, b):
@@ -67,6 +62,8 @@
 
 def solve_one(ins, partner, table, x_there, x_back, y_there, y_back, z_both, outs, work):
     rows = NG // len(ins)
+    me = lax.axis_index("grid")
+    x_there, x_back = x_there.at[me], x_back.at[me]
 
     def along_rows(factor, value):
         high, low = halves(value)
@@ -128,14 +125,18 @@
     solve_one([ref.at[0] for ref in ins], *refs[groups:groups + 7], [ref.at[0] for ref in outs], refs[-1])
 
 
-def factors(planes_at):
+def factors(groups):
     matrix = cas_matrix(NG)
-    by_plane = jnp.take(matrix, planes_at, axis=1)
+    there, back = [], []
+    for me in range(groups):
+        order = [slab * (NG // groups) + plane for slab in (me ^ d for d in range(groups)) for plane in range(NG // groups)]
+        there.append(row_factor(matrix[:, order]))
+        back.append(row_factor(matrix[:, order].T))
     by_line = matrix.reshape(NG, HALF, 2).transpose(0, 2, 1).reshape(NG, NG)
-    return (
-        kernel_table(), row_factor(by_plane), row_factor(by_plane.T),
+    return [jnp.asarray(value) for value in (
+        kernel_table(), np.stack(there), np.stack(back),
         row_factor(by_line), row_factor(by_line.T), lane_factor(matrix),
-    )
+    )]
 
 
 def solve(pieces, partner, fixed):
@@ -143,7 +144,7 @@
     count, rows, square = pieces[0].shape
     block = pl.BlockSpec((1, rows, square), lambda i: (i, 0, 0))
     whole = lambda array: pl.BlockSpec(array.shape, lambda i: (0,) * array.ndim)
-    fixed = (partner,) + fixed
+    fixed = (partner,) + tuple(fixed)
     return pl.pallas_call(
         lambda *refs: solve_body(groups, *refs),
         grid=(count,),
@@ -185,17 +186,15 @@
 
 def whole_body(chunks, groups, *refs):
     (orb, slab, okeep, osend, table, x_there, x_back, y_there, y_back, z_both,
-     vectors, opeer, slots, gram,
+     vectors, opeer, slots, extra, gram,
      cubes, solved, fresh, partner, hyper, ekeep, epeer, esend, lslots, work, obuf, abuf,
      parts, turned, sums, come, last,
      hyper_sem, pick_sem, fwd_sem, own_sem, back_sem, stay_sem, out_sem,
-     oy_sem, r_sem, ey_sem, l_sem, load_sem, sum_sem, last_sem) = refs
-    rows = cubes.shape[2]
-    bands = cubes.shape[0]
-    count = TILE // groups
-    ring = solved.shape[0]
+     oy_sem, r_sem, c_sem, ey_sem, l_sem, load_sem, sum_sem, last_sem) = refs
+    count, rows = cubes.shape[2:4]
     low = lslots.shape[3]
     high = rows - low
+    more = extra.shape[1]
     band, me = lax.axis_index("band"), lax.axis_index("grid")
     layer, line = band // 2, band % 2
     peer = band ^ 1
@@ -235,24 +234,36 @@
         pl.semaphore_signal(barrier, inc=1, device_id={"grid": me ^ d}, device_id_type=pl.DeviceIdType.MESH)
     pl.semaphore_wait(barrier, 6 + groups)
 
-    def forward(t):
+    def forward(c):
         def at(d):
-            return orb.at[(t // count) * TILE + (me ^ d) * count + lax.rem(t, count)]
-        moves = [remote(at(d), cubes.at[t, d], sems(fwd_sem, t, d - 1), "grid", me ^ d) for d in range(1, groups)]
-        return moves, pltpu.make_async_copy(at(0), cubes.at[t, 0], own_sem.at[t])
-
-    def start_forward(t):
-        moves, stay = forward(t)
+            return orb.at[pl.ds(c * TILE + (me ^ d) * count, count)]
+        moves = [remote(at(d), cubes.at[c, d], sems(fwd_sem, c, d - 1), "grid", me ^ d) for d in range(1, groups)]
+        return moves, pltpu.make_async_copy(at(0), cubes.at[c, 0], own_sem.at[c])
+
+    def start_forward(c):
+        moves, stay = forward(c)
         start(moves)
         stay.start()
 
-    def back(t, mine):
+    def wait_forward(c):
+        moves, stay = forward(c)
+        arrive(moves)
+        stay.wait()
+
+    def back(c, mine):
         def at(d):
-            return fresh.at[t // count, (me if mine else me ^ d) * count + lax.rem(t, count)]
-        source = lax.rem(t, ring)
-        moves = [remote(solved.at[source, d], at(d), sems(back_sem, t, d - 1), "grid", me ^ d) for d in range(1, groups)]
-        own = fresh.at[t // count, me * count + lax.rem(t, count)]
-        return moves, pltpu.make_async_copy(solved.at[source, 0], own, stay_sem.at[t])
+            return fresh.at[c, pl.ds((me if mine else me ^ d) * count, count)]
+        moves = [remote(solved.at[c % 2, d], at(d), sems(back_sem, c, d - 1), "grid", me ^ d) for d in range(1, groups)]
+        own = fresh.at[c, pl.ds(me * count, count)]
+        return moves, pltpu.make_async_copy(solved.at[c % 2, 0], own, stay_sem.at[c])
+
+    def start_back(c):
+        moves, stay = back(c, True)
+        start(moves)
+        stay.start()
+
+    def free_solved(c):
+        leave(back(c, True)[0])
 
     low_cut = ((0, (low + 1) // 2), ((low + 1) // 2, low // 2))
     high_cut = ((0, (high + 1) // 2), ((high + 1) // 2, high // 2))
@@ -269,6 +280,9 @@
 
     def r_here(slot, side, q, cut=low_cut):
         return r_move(slot, side, q, slots.at[slot, side], 0, cut)
+
+    def c_move(side, source):
+        return remote(source.at[pl.ds(0, more)], extra.at[side], sems(c_sem, side), "band", up)
 
     def l_move(slot, side, c, source, first, size):
         return remote(
@@ -297,7 +311,6 @@
     ]
     steps[0].start()
     start_forward(0)
-    start_forward(1)
     steps[0].wait_recv()
     hyper[3] = slab[...] + hyper[0]
     steps[1].start()
@@ -310,11 +323,14 @@
     def _():
         start([r_move(0, 0, q, okeep) for q in range(2)])
 
+    @on(2)
+    def _():
+        c_move(0, okeep).start()
+
     steps[2].wait_recv()
     partner[mine] = hyper[4] + hyper[2]
     start(picks)
-    start_forward(2)
-    start_forward(3)
+    start_forward(1)
     oy(1).start()
 
     def own_orbitals(q):
@@ -345,6 +361,10 @@
             def _():
                 start([r_move(0, 1, part, opeer) for part in range(2)])
 
+            @on(2)
+            def _():
+                c_move(1, opeer).start()
+
     def peer_orbitals(q):
         if q == 0:
             oy(1).wait_recv()
@@ -373,10 +393,9 @@
         return pltpu.make_async_copy(fresh.at[c], vectors.at[pl.ds(c * TILE, TILE)], out_sem.at[c])
 
     def collect(c):
-        for j in range(count):
-            moves, stay = back(c * count + j, False)
-            arrive(moves)
-            stay.wait()
+        moves, stay = back(c, False)
+        arrive(moves)
+        stay.wait()
         out_move(c).start()
         swap_into(fresh.at[c], ekeep.at[c], esend.at[c])
         ey(c, 1).start()
@@ -397,7 +416,7 @@
 
         @on(3)
         def _():
-            l_move(1, side, c, source, 0, low).start()
+            l_move(1, side, c, source, more, low - more).start()
 
     def pass_first(c, side):
         @on(2)
@@ -417,80 +436,53 @@
             l_move(1, side, c, lslots.at[1, side, c], 0, high).start()
 
     arrive(picks)
+    before = {
+        0: [(wait_forward, 0)],
+        4: [(wait_forward, 1)],
+        8: [(pass_first, 0, 0), (own_orbitals_on, 0), (wait_forward, 2), (free_solved, 0)],
+        12: [(pass_second, 0, 1), (pass_first, 1, 0), (wait_forward, 3), (free_solved, 1)],
+    }
     after = {
         0: [(own_orbitals, 0)],
-        3: [(own_orbitals, 1)],
-        4: [(own_orbitals_on, 0), (collect, 0)],
-        5: [(pass_first, 0, 0)],
-        6: [(own_orbitals_on, 1), (send_vectors, 0, 1), (pass_second, 0, 0)],
-        7: [(pass_first, 0, 1)],
-        8: [(peer_orbitals, 0), (pass_second, 0, 1), (collect, 1)],
-        9: [(pass_first, 1, 0)],
-        10: [(peer_orbitals, 1), (send_vectors, 1, 1), (pass_second, 1, 0)],
-        11: [(pass_first, 1, 1)],
-        12: [(peer_orbitals_on, 0), (pass_second, 1, 1), (collect, 2)],
-        13: [(pass_first, 2, 0)],
-        14: [(peer_orbitals_on, 1), (send_vectors, 2, 1), (pass_second, 2, 0)],
-        15: [(pass_first, 2, 1)],
+        3: [(start_back, 0)],
+        4: [(own_orbitals, 1)],
+        5: [(start_forward, 2)],
+        7: [(start_back, 1), (collect, 0)],
+        8: [(pass_second, 0, 0)],
+        9: [(start_forward, 3), (send_vectors, 0, 1)],
+        11: [(start_back, 2), (pass_first, 0, 1), (own_orbitals_on, 1), (collect, 1)],
+        12: [(send_vectors, 1, 1), (pass_second, 1, 0)],
+        13: [(peer_orbitals, 0)],
+        15: [(start_back, 3), (pass_first, 1, 1), (collect, 2)],
     }
 
-    @pl.loop(0, bands)
-    def _(t):
-        moves, stay = forward(t)
-        arrive(moves)
-        stay.wait()
-
-        @pl.when(t >= ring)
-        def _():
-            leave(back(t - ring, True)[0])
-
-        at = lax.rem(t, ring)
-        solve_one(
-            [cubes.at[t, d] for d in range(groups)], partner, table, x_there, x_back,
-            y_there, y_back, z_both, [solved.at[at, d] for d in range(groups)], work,
-        )
-        moves, stay = back(t, True)
-        start(moves)
-        stay.start()
-
-        @pl.when(t + count < bands)
-        def _():
-            start_forward(t + count)
-
-        for slot, events in after.items():
+    def run(events):
+        for event in events:
+            event[0](*event[1:])
+
+    def at_slot(t, table):
+        for slot, events in table.items():
             @pl.when(t == slot)
             def _():
-                for event in events:
-                    event[0](*event[1:])
-
-    for event in (
-        (pass_second, 2, 1), (collect, 3), (pass_first, 3, 0), (send_vectors, 3, 1),
-        (pass_second, 3, 0), (pass_first, 3, 1), (pass_second, 3, 1),
-    ):
-        event[0](*event[1:])
+                run(events)
+
+    @pl.loop(0, chunks * count)
+    def _(t):
+        at_slot(t, before)
+        c, j = t // count, lax.rem(t, count)
+        solve_one(
+            [cubes.at[c, d, j] for d in range(groups)], partner, table, x_there, x_back,
+            y_there, y_back, z_both, [solved.at[lax.rem(c, 2), d, j] for d in range(groups)], work,
+        )
+        at_slot(t, after)
+
+    run((
+        (pass_second, 1, 1), (peer_orbitals, 1), (pass_first, 2, 0), (send_vectors, 2, 1), (pass_second, 2, 0),
+        (peer_orbitals_on, 0), (pass_first, 2, 1), (collect, 3), (pass_second, 2, 1),
+        (peer_orbitals_on, 1), (pass_first, 3, 0), (send_vectors, 3, 1), (pass_second, 3, 0),
+    ))
 
     sides = [(side, c) for side in range(2) for c in range(chunks)]
-
-    @on(0)
-    def _():
-        for side, c in sides:
-            arrive([l_here(slot, side, c) for slot in range(2)])
-
-    @on(2)
-    def _():
-        for side, c in sides:
-            l_here(1, side, c, low).wait_recv()
-
-    @on(1)
-    def _():
-        for side in range(2):
-            arrive([r_here(1, side, q, high_cut) for q in range(2)])
-
-    @on(3)
-    def _():
-        for side in range(2):
-            for slot in range(2):
-                arrive([r_here(slot, side, q) for q in range(2)])
 
     def loads(p, at):
         return [
@@ -504,49 +496,86 @@
             for side in range(2)
         ]
 
-    def with_slots(p, at, act):
+    def extra_loads(p, at):
+        return [
+            pltpu.make_async_copy(extra.at[side, p], abuf.at[at, 1, side], load_sem.at[at, 4 + side])
+            for side in range(2)
+        ]
+
+    def early_slots(p, at, act):
         @pl.when((layer > 0) & (p < low))
         def _():
-            act(0, slot_loads(0, p, at))
-
-        @pl.when((layer > 1) & (p < low))
-        def _():
-            act(1, slot_loads(1, p, at))
+            act(1, slot_loads(0, p, at), 0)
+
+        @pl.when((layer == 2) & (p < low))
+        def _():
+            act(2, slot_loads(1, p, at), 1)
 
         @pl.when((layer == 1) & (p >= low))
         def _():
-            act(1, slot_loads(1, p - low, at))
-
-    def start_loads(p, at):
-        start(loads(p, at))
-        with_slots(p, at, lambda slot, moves: start(moves))
+            act(2, slot_loads(1, p - low, at), 1)
+
+        @pl.when((layer == 3) & (p < more))
+        def _():
+            act(5, extra_loads(p, at), 1)
+
+    def late_slots(p, at, act):
+        @pl.when((layer == 3) & (p < low))
+        def _():
+            act(2, slot_loads(1, p, at), 1)
 
     def across(a, b):
         return lax.dot_general(a, b, (((1,), (1,)), ((), ())), preferred_element_type=F32)
 
-    parts[...] = jnp.zeros_like(parts)
-    start_loads(0, 0)
-
-    @pl.loop(0, rows)
-    def _(p):
-        at = lax.rem(p, 2)
-
-        @pl.when(p + 1 < rows)
-        def _():
-            start_loads(p + 1, 1 - at)
-
+    def rows_of(buffer):
+        return jnp.concatenate([buffer[side] for side in range(2)], axis=0)
+
+    def own_rows(p):
+        return jnp.concatenate([ref[c, p] for ref in (ekeep, epeer) for c in range(chunks)], axis=0)
+
+    def in_turn(first, last, load, use):
+        load(first, first % 2, lambda index, moves, slot: start(moves))
+
+        @pl.loop(first, last)
+        def _(p):
+            at = lax.rem(p, 2)
+
+            @pl.when(p + 1 < last)
+            def _():
+                load(p + 1, 1 - at, lambda index, moves, slot: start(moves))
+
+            use(p, at)
+
+    def with_own(slots_of):
+        def load(p, at, act):
+            act(0, loads(p, at), None)
+            slots_of(p, at, act)
+        return load
+
+    def early(p, at):
+        there = own_rows(p)
         for move in loads(p, at):
             move.wait()
-        here = jnp.concatenate([obuf[at, side] for side in range(2)], axis=0)
-        there = jnp.concatenate([ref[c, p] for ref in (ekeep, epeer) for c in range(chunks)], axis=0)
-        parts[0] += across(here, there)
-
-        def add(slot, moves):
+        parts[0] += across(rows_of(obuf.at[at]), there)
+
+        def add(index, moves, slot):
             for move in moves:
                 move.wait()
-            parts[1 + slot] += across(jnp.concatenate([abuf[at, slot, side] for side in range(2)], axis=0), there)
-
-        with_slots(p, at, add)
+            parts[index] += across(rows_of(abuf.at[at, slot]), there)
+
+        early_slots(p, at, add)
+
+    def late(p, at):
+        for move in loads(p, at):
+            move.wait()
+        here = rows_of(obuf.at[at])
+
+        def add(index, moves, slot):
+            for move in moves:
+                move.wait()
+            parts[index] += across(rows_of(abuf.at[at, slot]), own_rows(p))
+
+        late_slots(p, at, add)
 
         def moved(slot, plane):
             parts[3 + slot] += across(here, jnp.concatenate([lslots[slot, side, c, plane] for side, c in sides], axis=0))
@@ -559,9 +588,40 @@
         def _():
             moved(1, p - low)
 
-        @pl.when((layer == 2) & (p < low))
-        def _():
-            moved(1, p)
+        @pl.when((layer == 2) & (p >= more) & (p < low))
+        def _():
+            moved(1, p - more)
+
+    parts[...] = jnp.zeros_like(parts)
+    @on(1)
+    def _():
+        for side in range(2):
+            arrive([r_here(1, side, q, high_cut) for q in range(2)])
+
+    @on(3)
+    def _():
+        for side in range(2):
+            arrive([r_here(0, side, q) for q in range(2)] + [c_move(side, extra.at[side])])
+
+    in_turn(0, rows, with_own(early_slots), early)
+    run(((pass_first, 3, 1), (pass_second, 3, 1)))
+
+    @on(0)
+    def _():
+        for side, c in sides:
+            arrive([l_here(slot, side, c) for slot in range(2)])
+
+    @on(2)
+    def _():
+        for side, c in sides:
+            l_here(1, side, c, low - more).wait_recv()
+
+    @on(3)
+    def _():
+        for side in range(2):
+            arrive([r_here(1, side, q) for q in range(2)])
+
+    in_turn(0, rows, with_own(late_slots), late)
 
     size = parts.shape[1]
     half = size // 2
@@ -572,7 +632,7 @@
                 if other == at:
                     turned[other] = parts[0]
                 else:
-                    found = [parts[i] if i > 2 else parts[i].T for i in HELD[at].get(other, ())]
+                    found = [parts[i] if i in (3, 4) else parts[i].T for i in HELD[at].get(other, ())]
                     turned[other] = sum(found[1:], found[0]) if found else jnp.zeros((size, size), F32)
     for other in range(chunks):
         block = turned[other] * (1.0 / NPTS)
@@ -610,23 +670,21 @@
 
     leave(steps + picks + totals + [move for move, _ in swaps] + [oy(half) for half in range(2)])
 
-    @pl.loop(0, bands)
-    def _(t):
-        leave(forward(t)[0])
-
-        @pl.when(t >= bands - ring)
-        def _():
-            leave(back(t, True)[0])
-
     for c in range(chunks):
         out_move(c).wait()
-        leave([ey(c, half) for half in range(2)])
+        leave([ey(c, half) for half in range(2)] + forward(c)[0])
+        if c >= chunks - 2:
+            leave(back(c, True)[0])
 
     @on(0)
     def _():
         for side in range(2):
             leave([r_here(0, side, q) for q in range(2)] + [r_here(1, side, q, high_cut) for q in range(2)])
 
+    @on(2)
+    def _():
+        leave([c_move(side, extra.at[side]) for side in range(2)])
+
     @on(1, 2)
     def _():
         for side in range(2):
@@ -645,7 +703,7 @@
     @on(3)
     def _():
         for side, c in sides:
-            l_here(1, side, c, low).wait_send()
+            l_here(1, side, c, low - more).wait_send()
 
 
 def whole(orbitals, slab, okeep, osend, fixed):
@@ -653,25 +711,24 @@
     groups = lax.axis_size("grid")
     chunks, count = bands // TILE, TILE // groups
     low, width = LOW * rows // 16, square // 2
-    ring = min(8, bands // groups)
     anywhere = pl.BlockSpec(memory_space=pl.ANY)
     inside = pl.BlockSpec(memory_space=pltpu.VMEM)
     dma = pltpu.SemaphoreType.DMA
     size = 2 * bands
-    solves = bands // groups
     return pl.pallas_call(
         lambda *refs: whole_body(chunks, groups, *refs),
         in_specs=[anywhere, inside, anywhere, anywhere] + [inside] * len(fixed),
-        out_specs=[anywhere, anywhere, anywhere, inside],
+        out_specs=[anywhere] * 4 + [inside],
         out_shape=[
             jax.ShapeDtypeStruct(orbitals.shape, BF),
             jax.ShapeDtypeStruct((rows, bands, width), BF),
             jax.ShapeDtypeStruct((2, 2, low, bands, width), BF),
+            jax.ShapeDtypeStruct((2, MORE, bands, width), BF),
             jax.ShapeDtypeStruct((bands, 4 * size), F32),
         ],
         scratch_shapes=[
-            pltpu.VMEM((solves, groups, rows, square), BF),
-            pltpu.VMEM((ring, groups, rows, square), BF),
+            pltpu.VMEM((chunks, groups, count, rows, square), BF),
+            pltpu.VMEM((2, groups, count, rows, square), BF),
             pltpu.VMEM((chunks, TILE, rows, square), BF),
             pltpu.VMEM((NG, square), BF),
             pltpu.VMEM((5, rows, square), BF),
@@ -682,21 +739,21 @@
             pltpu.VMEM((NG * HALF, LANES), F32),
             pltpu.VMEM((2, 2, bands, width), BF),
             pltpu.VMEM((2, 2, 2, bands, width), BF),
-            pltpu.VMEM((5, size, size), F32),
+            pltpu.VMEM((6, size, size), F32),
             pltpu.VMEM((4, size, size), F32),
             pltpu.VMEM((5, 4, bands, size), F32),
             pltpu.VMEM((3, 4, bands, size), F32),
             pltpu.VMEM((3, 2, bands, size), F32),
-            dma((2, 3)), dma((2, groups - 1)), dma((2, solves, groups - 1)), dma((solves,)),
-            dma((2, solves, groups - 1)), dma((solves,)), dma((chunks,)),
-            dma((2, 2)), dma((2, 2, 2, 2)), dma((2, chunks, 2)), dma((2, 2, 2, chunks)), dma((2, 6)),
+            dma((2, 3)), dma((2, groups - 1)), dma((2, chunks, groups - 1)), dma((chunks,)),
+            dma((2, chunks, groups - 1)), dma((chunks,)), dma((chunks,)),
+            dma((2, 2)), dma((2, 2, 2, 2)), dma((2, 2)), dma((2, chunks, 2)), dma((2, 2, 2, chunks)), dma((2, 6)),
             dma((2, 3)), dma((2, 3, 2)),
         ],
         compiler_params=pltpu.CompilerParams(
             collective_id=0, has_side_effects=True, vmem_limit_bytes=60 * 1024 * 1024
         ),
         cost_estimate=pl.CostEstimate(
-            flops=solves * 12 * NG * NG * NG * 256, bytes_accessed=16 * orbitals.size, transcendentals=0
+            flops=chunks * count * 12 * NG * NG * NG * 256, bytes_accessed=16 * orbitals.size, transcendentals=0
         ),
     )(orbitals, slab, okeep, osend, *fixed)
 
@@ -755,14 +812,13 @@
     bands, planes, square = orbitals.shape
     groups, shares = lax.axis_size("grid"), lax.axis_size("band")
     me = lax.axis_index("grid")
-    order = (me ^ jnp.arange(groups, dtype=jnp.int32))[:, None] * planes
-    fixed = factors((order + jnp.arange(planes, dtype=jnp.int32)[None]).reshape(-1))
+    fixed = factors(groups)
     target = picks[0]
     mine = lax.dynamic_index_in_dim(orbitals, target % bands, 0, keepdims=False)
     slab = jnp.where(lax.axis_index("band") == target // bands, mine, 0).astype(BF)
 
     if shares == 8 and groups == 4 and bands == 4 * TILE and planes == 16:
-        vectors, _, _, gram = whole(orbitals, slab, *order_orbitals(orbitals), fixed)
+        vectors, _, _, _, gram = whole(orbitals, slab, *order_orbitals(orbitals), fixed)
         return (vectors, gram)
 
     partner = spread(slab)

time: 359 us -> 328 us (0.914)
  Pallas kernels: 331 us -> 308 us
  other arithmetic: 5.82 us -> 1.57 us
  local copies, waits for them, and re-layouts: 20.2 us -> 16 us
    pallas_call x1, Pallas kernels: 328 us -> 305 us  [whole(): pl.pallas_call(lambda *refs: whole_body(chunks, groups, *refs), in_specs=...]
where the time goes in v4:
time: 328 us; the launch traced here: 327 us
  Pallas kernels  308 us (94%)
  local copies, waits for them, and re-layouts  16 us (5%)
    pallas_call x1, Pallas kernels, whole(): pl.pallas_call(lambda *refs: whole_body(chunks, groups, *refs), in_specs=...  305 us
    unnamed x10, local copies, waits for them, and re-layouts  16 us

profile of v4, /device:TPU:0, one launch (start us, length us, event | category | flops | bytes accessed | tf_op | source)
XLA Modules:
  0.0 327.0 jit_solution(13680313831373765276)
XLA Ops:
  1.3 1.6 select_bitcast_fusion.refs_1_
  2.9 0.0 copy-start
  2.9 3.4 %copy-done = bf16[64,16,4096]{2,1,0:T(8,128)(2,1)S(1)} copy-done((bf16[64,16,4096]{2,1,0:T(8,128)(2,1)S(1)}, bf16[64,16,4096]{2,1,0:T(8,128)(2,1)}, u32[]{:S(2)}) %copy-start) | copy-done | bytes 8388632
  6.3 3.0 shard_map.95
  9.3 0.0 copy-start.1
  9.3 2.0 copy-done.1
  11.3 0.0 copy-start.2
  11.3 2.0 copy-done.2
  13.3 305.1 %shard_map.96 = (bf16[64,16,4096]{2,1,0:T(8,128)(2,1)}, bf16[16,64,2048]{2,1,0:T(8,128)(2,1)}, bf16[2,2,9,64,2048]{4,3,2,1,0:T(8,128)(2,1)}, bf16[2,3,64,2048]{3,2,1,0:T(8,128)(2,1)}, f32[64,512]{1,0:T(8,128)}) custom-call(bf16[64,16,4096]{2,1,0:T(8,128)(2,1)} %refs_0_.1, bf16[16,4096]{1,0:T(8,128)(2,1)} %select_bitcast_fusion.refs_1_, ...), custom_call_target="tpu_custom_call" | custom-call | flops 12884901888 | bytes 67108864 | tf_op jit(solution)/shard_map/pallas_call | solution.py:718
  318.4 0.0 copy-start.3
  318.4 7.9 %copy.13 = bf16[64,16,4096]{2,1,0:T(8,128)(2,1)} copy(bf16[64,16,4096]{2,1,0:T(8,128)(2,1)} %get-tuple-element.12) | data formatting | bytes 16777216
  326.3 0.0 copy-done.3
  326.3 0.7 copy.14
Async XLA Ops:
  2.9 3.4 %copy-start = (bf16[64,16,4096]{2,1,0:T(8,128)(2,1)S(1)}, bf16[64,16,4096]{2,1,0:T(8,128)(2,1)}, u32[]{:S(2)}) copy-start(bf16[64,16,4096]{2,1,0:T(8,128)(2,1)} %refs_0_.1) | copy-start | bytes 25165828
  9.3 2.0 copy-start.1
  11.3 2.0 copy-start.2
  318.4 7.9 %copy-start.3 = (f32[64,512]{1,0:T(8,128)S(1)}, f32[64,512]{1,0:T(8,128)}, u32[]{:S(2)}) copy-start(f32[64,512]{1,0:T(8,128)} %get-tuple-element.13) | copy-start | bytes 393220

commit v5 on v4

--- a/solution.py
+++ b/solution.py
@@ -179,7 +179,7 @@
         in_specs=[pl.BlockSpec((TILE, rows, square), lambda i: (i, 0, 0))],
         out_specs=[spec] * 2,
         out_shape=[part] * 2,
-        compiler_params=pltpu.CompilerParams(vmem_limit_bytes=24 * 1024 * 1024),
+        compiler_params=pltpu.CompilerParams(vmem_limit_bytes=60 * 1024 * 1024),
         cost_estimate=pl.CostEstimate(flops=0, bytes_accessed=4 * orbitals.size, transcendentals=0),
     )(orbitals)
 

time: 328 us -> 325 us (level)
  local copies, waits for them, and re-layouts: 16 us -> 8.58 us
  Pallas kernels: 308 us -> 313 us
    unnamed x10 -> x4, local copies, waits for them, and re-layouts: 16 us -> 8.58 us
    pallas_call x1, Pallas kernels: 3.01 us -> 7.91 us  [order_orbitals(): pl.pallas_call(swap_into, grid=(bands // TILE,), in_specs=[pl.BlockSpec((...]
where the time goes in v5:
time: 325 us; the launch traced here: 324 us
  Pallas kernels  313 us (96%)
  local copies, waits for them, and re-layouts  8.58 us (3%)
    pallas_call x1, Pallas kernels, whole(): pl.pallas_call(lambda *refs: whole_body(chunks, groups, *refs), in_specs=...  305 us
    unnamed x4, local copies, waits for them, and re-layouts  8.58 us
    pallas_call x1, Pallas kernels, order_orbitals(): pl.pallas_call(swap_into, grid=(bands // TILE,), in_specs=[pl.BlockSpec((...  7.91 us

profile of v5, /device:TPU:0, one launch (start us, length us, event | category | flops | bytes accessed | tf_op | source)
XLA Modules:
  0.0 324.5 jit_solution(18030972690625228608)
XLA Ops:
  1.3 1.6 select_bitcast_fusion.refs_1_
  2.9 7.9 %shard_map.95 = (bf16[16,64,2048]{2,1,0:T(8,128)(2,1)}, bf16[16,64,2048]{2,1,0:T(8,128)(2,1)}) custom-call(bf16[64,16,4096]{2,1,0:T(8,128)(2,1)} %refs_0_.1), custom_call_target="tpu_custom_call" | custom-call | bytes 16777216 | tf_op jit(solution)/shard_map/pallas_call | solution.py:176
  10.8 305.1 %shard_map.96 = (bf16[64,16,4096]{2,1,0:T(8,128)(2,1)}, bf16[16,64,2048]{2,1,0:T(8,128)(2,1)}, bf16[2,2,9,64,2048]{4,3,2,1,0:T(8,128)(2,1)}, bf16[2,3,64,2048]{3,2,1,0:T(8,128)(2,1)}, f32[64,512]{1,0:T(8,128)}) custom-call(bf16[64,16,4096]{2,1,0:T(8,128)(2,1)} %refs_0_.1, bf16[16,4096]{1,0:T(8,128)(2,1)} %select_bitcast_fusion.refs_1_, ...), custom_call_target="tpu_custom_call" | custom-call | flops 12884901888 | bytes 67108864 | tf_op jit(solution)/shard_map/pallas_call | solution.py:718
  315.9 0.0 copy-start
  315.9 7.9 %copy.13 = bf16[64,16,4096]{2,1,0:T(8,128)(2,1)} copy(bf16[64,16,4096]{2,1,0:T(8,128)(2,1)} %get-tuple-element.12) | data formatting | bytes 16777216
  323.8 0.0 copy-done
  323.8 0.7 copy.14
Async XLA Ops:
  315.9 7.9 %copy-start = (f32[64,512]{1,0:T(8,128)S(1)}, f32[64,512]{1,0:T(8,128)}, u32[]{:S(2)}) copy-start(f32[64,512]{1,0:T(8,128)} %get-tuple-element.13) | copy-start | bytes 393220

commit v6 on v5

--- a/solution.py
+++ b/solution.py
@@ -330,7 +330,6 @@
     steps[2].wait_recv()
     partner[mine] = hyper[4] + hyper[2]
     start(picks)
-    start_forward(1)
     oy(1).start()
 
     def own_orbitals(q):
@@ -436,6 +435,7 @@
             l_move(1, side, c, lslots.at[1, side, c], 0, high).start()
 
     arrive(picks)
+    start_forward(1)
     before = {
         0: [(wait_forward, 0)],
         4: [(wait_forward, 1)],

time: 325 us -> 325 us (level)
  no operation moved by 1% of the time
where the time goes in v6:
time: 325 us; the launch traced here: 324 us
  Pallas kernels  313 us (96%)
  local copies, waits for them, and re-layouts  8.58 us (3%)
    pallas_call x1, Pallas kernels, whole(): pl.pallas_call(lambda *refs: whole_body(chunks, groups, *refs), in_specs=...  305 us
    unnamed x4, local copies, waits for them, and re-layouts  8.58 us
    pallas_call x1, Pallas kernels, order_orbitals(): pl.pallas_call(swap_into, grid=(bands // TILE,), in_specs=[pl.BlockSpec((...  7.91 us

profile of v6, /device:TPU:0, one launch (start us, length us, event | category | flops | bytes accessed | tf_op | source)
XLA Modules:
  0.0 324.5 jit_solution(603387842339444455)
XLA Ops:
  1.3 1.6 select_bitcast_fusion.refs_1_
  2.9 7.9 %shard_map.95 = (bf16[16,64,2048]{2,1,0:T(8,128)(2,1)}, bf16[16,64,2048]{2,1,0:T(8,128)(2,1)}) custom-call(bf16[64,16,4096]{2,1,0:T(8,128)(2,1)} %refs_0_.1), custom_call_target="tpu_custom_call" | custom-call | bytes 16777216 | tf_op jit(solution)/shard_map/pallas_call | solution.py:176
  10.8 305.1 %shard_map.96 = (bf16[64,16,4096]{2,1,0:T(8,128)(2,1)}, bf16[16,64,2048]{2,1,0:T(8,128)(2,1)}, bf16[2,2,9,64,2048]{4,3,2,1,0:T(8,128)(2,1)}, bf16[2,3,64,2048]{3,2,1,0:T(8,128)(2,1)}, f32[64,512]{1,0:T(8,128)}) custom-call(bf16[64,16,4096]{2,1,0:T(8,128)(2,1)} %refs_0_.1, bf16[16,4096]{1,0:T(8,128)(2,1)} %select_bitcast_fusion.refs_1_, ...), custom_call_target="tpu_custom_call" | custom-call | flops 12884901888 | bytes 67108864 | tf_op jit(solution)/shard_map/pallas_call | solution.py:718
  315.9 0.0 copy-start
  315.9 7.9 %copy.13 = bf16[64,16,4096]{2,1,0:T(8,128)(2,1)} copy(bf16[64,16,4096]{2,1,0:T(8,128)(2,1)} %get-tuple-element.12) | data formatting | bytes 16777216
  323.8 0.0 copy-done
  323.8 0.7 copy.14
Async XLA Ops:
  315.9 7.9 %copy-start = (f32[64,512]{1,0:T(8,128)S(1)}, f32[64,512]{1,0:T(8,128)}, u32[]{:S(2)}) copy-start(f32[64,512]{1,0:T(8,128)} %get-tuple-element.13) | copy-start | bytes 393220
